TPU v7x, 32 devices: a whole 2x2x4 slice. The times are simulated.
32 devices in a mesh: gx: 4 (over x, core), gy: 4 (over z), gz: 2 (over y).
Axes of the slice: x: 2, y: 2, z: 4, core: 2. Of those that a mesh axis runs over, the one named last changes fastest.
Arguments:
- flow_adjoint: float32 [19, 64, 64, 256], P(None, 'gx', 'gy', 'gz'), may hold values from -6 to 6
- solute_adjoint: float32 [7, 64, 64, 256], P(None, 'gx', 'gy', 'gz'), may hold values from -6 to 6
- flow_density: bfloat16 [4, 64, 64, 256], P(None, 'gx', 'gy', 'gz'), may hold values from 0.796875 to 1.25
- flow_velocity: bfloat16 [4, 3, 64, 64, 256], P(None, None, 'gx', 'gy', 'gz'), may hold values from -0.119628906 to 0.119628906
- solute_level: bfloat16 [4, 64, 64, 256], P(None, 'gx', 'gy', 'gz'), may hold values from 0.099609375 to 3
- solid: int32 [64, 64, 256], P('gx', 'gy', 'gz'), may hold values 0 or 1
- owner: int32 [8], replicated, may hold values from 0 to 1, as said below
Outputs:
- flow_result: float32 [19, 64, 64, 256], P(None, 'gx', 'gy', 'gz')
- solute_result: float32 [7, 64, 64, 256], P(None, 'gx', 'gy', 'gz')
Inputs may be any that keep to these rules, and one draw needn't show every extreme that they name: owner never falls along the list; every gz device holds 1 to 7 blocks.
All inputs are finite; a program needn't handle non-finite values. No bound on the sum of `solid` on one device may be relied on, other than what follows from the above.
Results may differ from a plain program's by a relative error of at most 0.0003.
Values sent between devices are 32-bit elements; how exact they have to be, the bound alone decides.
No kernel may reach another device: no remote copies, remote signals or barrier semaphores. Data moves between devices by JAX's collectives and lax.ppermute only.
A program may use at most 128 MiB of HBM per device.

v0:
```python
import jax
import jax.numpy as jnp
from jax import lax
from jax.sharding import PartitionSpec as P

BZC = 16


FLOW_DIRS = [
    (0, 0, 0),
    (1, 0, 0),
    (-1, 0, 0),
    (0, 1, 0),
    (0, -1, 0),
    (0, 0, 1),
    (0, 0, -1),
    (1, 1, 0),
    (-1, -1, 0),
    (1, -1, 0),
    (-1, 1, 0),
    (1, 0, 1),
    (-1, 0, -1),
    (1, 0, -1),
    (-1, 0, 1),
    (0, 1, 1),
    (0, -1, -1),
    (0, 1, -1),
    (0, -1, 1),
]
FLOW_WEIGHTS = [1.0 / 3.0] + [1.0 / 18.0] * 6 + [1.0 / 36.0] * 12
SOLUTE_DIRS = FLOW_DIRS[:7]
SOLUTE_WEIGHTS = [0.25] + [0.125] * 6
flow_omega = 1.25
solute_omega = 1.6
langmuir_rate = 0.05


def shifted(shard, axis, by):
    length = lax.axis_size(axis)
    pairs = [(i, i + by) for i in range(length) if 0 <= i + by < length]
    return lax.ppermute(shard, axis, pairs)


def padded_2(shard, sides, width):
    for axis, dim in sides:
        size, length = (lax.axis_size(axis), shard.shape[dim])
        up = [(i, (i + 1) % size) for i in range(size - 1)]
        down = [(j, i) for i, j in up]
        last = lax.slice_in_dim(shard, length - width, length, axis=dim)
        initial = lax.slice_in_dim(shard, 0, width, axis=dim)
        before = lax.ppermute(last, axis, up)
        after = lax.ppermute(initial, axis, down)
        shard = jnp.concatenate([before, shard, after], axis=dim)
    return shard


def opposite(table):
    return [table.index((-entry[0], -entry[1], -entry[2])) for entry in table]


def extend(field, length):
    top_layer = lax.dynamic_slice_in_dim(field, length - 1, 1, 3)
    from_below = shifted(top_layer, "gz", 1)
    from_above = shifted(field[:, :, :, 0:1], "gz", -1)
    grown = jnp.concatenate([from_below, field, jnp.zeros_like(from_below)], axis=3)
    grown = lax.dynamic_update_slice_in_dim(grown, from_above, length + 1, 3)
    return padded_2(grown, (("gx", 1), ("gy", 2)), 1)


def reverse_stream(padded, solid_pad, table, reverse):
    width_x = padded.shape[1] - 2
    width_y = padded.shape[2] - 2
    width_z = padded.shape[3] - 2
    centre = padded[:, 1:-1, 1:-1, 1:-1]
    result_rows = []
    for number, (step_x, step_y, step_z) in enumerate(table):
        near = padded[
            number,
            1 + step_x : 1 + step_x + width_x,
            1 + step_y : 1 + step_y + width_y,
            1 + step_z : 1 + step_z + width_z,
        ]
        blocked = solid_pad[
            1 + step_x : 1 + step_x + width_x,
            1 + step_y : 1 + step_y + width_y,
            1 + step_z : 1 + step_z + width_z,
        ]
        result_rows.append(jnp.where(blocked == 0, near, centre[reverse[number]]))
    return jnp.stack(result_rows)


def solute_update(read, level, velocity):
    vel_x = velocity[0].astype(jnp.float32)
    vel_y = velocity[1].astype(jnp.float32)
    vel_z = velocity[2].astype(jnp.float32)
    level = level.astype(jnp.float32)
    moment_zero = 0.0
    moment_x = 0.0
    moment_y = 0.0
    moment_z = 0.0
    for number, (step_x, step_y, step_z) in enumerate(SOLUTE_DIRS):
        weighted = SOLUTE_WEIGHTS[number] * read[number]
        moment_zero = moment_zero + weighted
        moment_x = moment_x + step_x * weighted
        moment_y = moment_y + step_y * weighted
        moment_z = moment_z + step_z * weighted
    uptake = langmuir_rate / ((1.0 + level) * (1.0 + level))
    common = (
        solute_omega
        * (moment_zero + 4.0 * (moment_x * vel_x + moment_y * vel_y + moment_z * vel_z))
        - uptake * moment_zero
    )
    updated = jnp.stack(
        [(1.0 - solute_omega) * read[number] + common for number in range(len(SOLUTE_DIRS))]
    )
    factor = 4.0 * solute_omega * level
    pull = jnp.stack([factor * moment_x, factor * moment_y, factor * moment_z])
    return (updated, pull)


def flow_update(read, density, velocity, pull):
    vel_x = velocity[0].astype(jnp.float32)
    vel_y = velocity[1].astype(jnp.float32)
    vel_z = velocity[2].astype(jnp.float32)
    speed_sq = vel_x * vel_x + vel_y * vel_y + vel_z * vel_z
    moment_zero = 0.0
    moment_x = 0.0
    moment_y = 0.0
    moment_z = 0.0
    for number, (step_x, step_y, step_z) in enumerate(FLOW_DIRS):
        weighted = FLOW_WEIGHTS[number] * read[number]
        along = step_x * vel_x + step_y * vel_y + step_z * vel_z
        moment_zero = moment_zero + weighted * (1.0 - 4.5 * along * along + 1.5 * speed_sq)
        shared = 9.0 * weighted * along
        moment_x = moment_x + weighted * (3.0 * step_x - 3.0 * vel_x) + shared * step_x
        moment_y = moment_y + weighted * (3.0 * step_y - 3.0 * vel_y) + shared * step_y
        moment_z = moment_z + weighted * (3.0 * step_z - 3.0 * vel_z) + shared * step_z
    inverse_density = 1.0 / density.astype(jnp.float32)
    result_rows = []
    for number, (step_x, step_y, step_z) in enumerate(FLOW_DIRS):
        relax = moment_zero + step_x * moment_x + step_y * moment_y + step_z * moment_z
        source = (
            pull[0] * (step_x - vel_x) + pull[1] * (step_y - vel_y) + pull[2] * (step_z - vel_z)
        ) * inverse_density
        result_rows.append((1.0 - flow_omega) * read[number] + flow_omega * relax + source)
    return jnp.stack(result_rows)


def per_device(
    flow_adjoint, solute_adjoint, flow_density, flow_velocity, solute_level, solid, owner
):
    depth = solid.shape[2]
    column = lax.axis_index("gz")
    count = jnp.sum((owner == column).astype(jnp.int32))
    length = count * BZC
    live = jnp.arange(depth, dtype=jnp.int32) < length
    valid = jnp.where(live[None, None, :] & (solid == 0), 1.0, 0.0).astype(jnp.float32)
    live_mask = jnp.where(live, 1.0, 0.0).astype(jnp.float32)
    top_solid = lax.dynamic_slice_in_dim(solid, length - 1, 1, 2)
    solid_below = shifted(top_solid, "gz", 1)
    solid_above = shifted(solid[:, :, 0:1], "gz", -1)
    solid_grown = jnp.concatenate([solid_below, solid, jnp.zeros_like(solid_below)], axis=2)
    solid_grown = lax.dynamic_update_slice_in_dim(solid_grown, solid_above, length + 1, 2)
    solid_pad = padded_2(solid_grown, (("gx", 0), ("gy", 1)), 1)
    flow_reverse = opposite(FLOW_DIRS)
    solute_reverse = opposite(SOLUTE_DIRS)
    flow = flow_adjoint * live_mask
    solute = solute_adjoint * live_mask
    steps = flow_density.shape[0]
    pulls = [None] * steps
    for step in reversed(range(steps)):
        read = reverse_stream(extend(solute, length), solid_pad, SOLUTE_DIRS, solute_reverse)
        solute, pulls[step] = solute_update(read, solute_level[step], flow_velocity[step])
        solute = solute * valid
    for step in reversed(range(steps)):
        read = reverse_stream(extend(flow, length), solid_pad, FLOW_DIRS, flow_reverse)
        flow = flow_update(read, flow_density[step], flow_velocity[step], pulls[step]) * valid
    return (flow, solute)


def solution(mesh):
    in_specs = (
        P(None, "gx", "gy", "gz"),
        P(None, "gx", "gy", "gz"),
        P(None, "gx", "gy", "gz"),
        P(None, None, "gx", "gy", "gz"),
        P(None, "gx", "gy", "gz"),
        P("gx", "gy", "gz"),
        P(),
    )
    out_specs = (P(None, "gx", "gy", "gz"), P(None, "gx", "gy", "gz"))
    return jax.shard_map(
        per_device, mesh=mesh, in_specs=in_specs, out_specs=out_specs, check_vma=False
    )
```

profile of v0, /device:TPU:1, one launch (start us, length us, event | category | flops | bytes accessed | tf_op | source)
XLA Modules:
  0.0 576.2 jit_solution(16388484700615093987)
XLA Ops:
  13.2 5.2 collective-permute-start.12
  30.3 5.2 collective-permute-start
  61.6 11.2 %dynamic_update_slice.29 = f32[7,16,16,130]{3,2,1,0:T(8,128)} dynamic-update-slice(f32[7,16,16,130]{3,2,1,0:T(8,128)} %maximum_maximum_fusion.4, f32[7,16,16,1]{3,2,1,0:T(8,128)S(1)} %copy.99, s32[]{:T(128)} %constant.154.clone.1, s32[]{:T(128)} %constant.154.clone.1, s32[]{:T(128)} %constant.154.clone.1, s32[]{:T(128)S(6)} %select_n.333) | dynamic-update-slice | bytes 14340 | tf_op jit(solution)/shard_map/dynamic_update_slice | solution.py:66
  72.8 4.7 copy.93
  77.5 5.4 maximum_maximum_fusion
  82.9 4.7 copy.95
  87.6 26.2 %dynamic_update_slice.27 = f32[19,16,16,130]{3,2,1,0:T(8,128)} dynamic-update-slice(f32[19,16,16,130]{3,2,1,0:T(8,128)} %maximum_maximum_fusion, f32[19,16,16,1]{3,2,1,0:T(8,128)} %copy.95, s32[]{:T(128)} %constant.154.clone.1, s32[]{:T(128)} %constant.154.clone.1, s32[]{:T(128)} %constant.154.clone.1, s32[]{:T(128)S(6)} %select_n.333) | dynamic-update-slice | bytes 38916 | tf_op jit(solution)/shard_map/dynamic_update_slice | solution.py:66
  141.2 4.8 collective-permute-start.17
  146.9 6.2 %collective-permute-done.16 = f32[7,18,1,130]{3,2,1,0:T(1,128)S(1)} collective-permute-done((f32[7,18,1,130]{3,2,1,0:T(1,128)S(1)}, f32[7,18,1,130]{3,2,1,0:T(1,128)S(1)}, u32[]{:S(2)}, u32[]{:S(2)}) %collective-permute-start.16) | collective-permute-done | bytes 65552 | tf_op jit(solution)/shard_map/ppermute | solution.py:52
  153.2 5.8 %constant_dynamic-update-slice_fusion.18 = (f32[19,16,16,128]{3,2,1,0:T(8,128)S(1)}, f32[16,16,128]{2,1,0:T(8,128)S(1)}, f32[16,16,128]{2,1,0:T(8,128)S(1)}, f32...) fusion(f32[19,16,16,130]{3,2,1,0:T(8,128)S(1)} %bitcast.2496, ...), kind=kLoop, calls=%fused_computation.251 | loop fusion | flops 18710528 | bytes 19931136
  164.7 5.5 collective-permute-start.24
  182.0 5.3 collective-permute-start.18
  201.0 10.7 %dynamic_update_slice.31 = f32[7,16,16,130]{3,2,1,0:T(8,128)} dynamic-update-slice(f32[7,16,16,130]{3,2,1,0:T(8,128)} %maximum_maximum_fusion.5, f32[7,16,16,1]{3,2,1,0:T(8,128)} %copy.107, s32[]{:T(128)} %constant.154.clone.1, s32[]{:T(128)} %constant.154.clone.1, s32[]{:T(128)} %constant.154.clone.1, s32[]{:T(128)S(6)} %select_n.333) | dynamic-update-slice | bytes 14340 | tf_op jit(solution)/shard_map/dynamic_update_slice | solution.py:66
  211.7 4.7 copy.101
  216.4 5.4 maximum_maximum_fusion.1
  221.7 4.7 copy.103
  226.4 26.2 %dynamic_update_slice.30 = f32[19,16,16,130]{3,2,1,0:T(8,128)} dynamic-update-slice(f32[19,16,16,130]{3,2,1,0:T(8,128)} %maximum_maximum_fusion.1, f32[19,16,16,1]{3,2,1,0:T(8,128)} %copy.103, s32[]{:T(128)} %constant.154.clone.1, s32[]{:T(128)} %constant.154.clone.1, s32[]{:T(128)} %constant.154.clone.1, s32[]{:T(128)S(6)} %select_n.333) | dynamic-update-slice | bytes 38916 | tf_op jit(solution)/shard_map/dynamic_update_slice | solution.py:66
  284.4 5.3 constant_dynamic-update-slice_fusion.44
  297.1 5.6 collective-permute-start.36
  321.2 5.2 collective-permute-start.30
  340.1 10.7 %dynamic_update_slice.33 = f32[7,16,16,130]{3,2,1,0:T(8,128)} dynamic-update-slice(f32[7,16,16,130]{3,2,1,0:T(8,128)} %maximum_maximum_fusion.6, f32[7,16,16,1]{3,2,1,0:T(8,128)} %copy.115, s32[]{:T(128)} %constant.154.clone.1, s32[]{:T(128)} %constant.154.clone.1, s32[]{:T(128)} %constant.154.clone.1, s32[]{:T(128)S(6)} %select_n.333) | dynamic-update-slice | bytes 14340 | tf_op jit(solution)/shard_map/dynamic_update_slice | solution.py:66
  350.8 4.7 copy.109
  355.5 5.4 maximum_maximum_fusion.2
  360.9 4.7 copy.111
  365.5 26.1 %dynamic_update_slice.32 = f32[19,16,16,130]{3,2,1,0:T(8,128)} dynamic-update-slice(f32[19,16,16,130]{3,2,1,0:T(8,128)} %maximum_maximum_fusion.2, f32[19,16,16,1]{3,2,1,0:T(8,128)} %copy.111, s32[]{:T(128)} %constant.154.clone.1, s32[]{:T(128)} %constant.154.clone.1, s32[]{:T(128)} %constant.154.clone.1, s32[]{:T(128)S(6)} %select_n.333) | dynamic-update-slice | bytes 38916 | tf_op jit(solution)/shard_map/dynamic_update_slice | solution.py:66
  423.7 5.3 constant_dynamic-update-slice_fusion.70
  436.5 5.5 collective-permute-start.48
  460.5 5.2 collective-permute-start.42
  479.2 10.7 %dynamic_update_slice.35 = f32[7,16,16,130]{3,2,1,0:T(8,128)} dynamic-update-slice(f32[7,16,16,130]{3,2,1,0:T(8,128)} %maximum_maximum_fusion.7, f32[7,16,16,1]{3,2,1,0:T(8,128)} %copy.123, s32[]{:T(128)} %constant.154.clone.1, s32[]{:T(128)} %constant.154.clone.1, s32[]{:T(128)} %constant.154.clone.1, s32[]{:T(128)S(6)} %select_n.333) | dynamic-update-slice | bytes 14340 | tf_op jit(solution)/shard_map/dynamic_update_slice | solution.py:66
  497.4 4.7 copy.117
  502.0 5.4 maximum_maximum_fusion.3
  512.1 26.2 %dynamic_update_slice.34 = f32[19,16,16,130]{3,2,1,0:T(8,128)} dynamic-update-slice(f32[19,16,16,130]{3,2,1,0:T(8,128)} %maximum_maximum_fusion.3, f32[19,16,16,1]{3,2,1,0:T(8,128)} %copy.119, s32[]{:T(128)} %constant.154.clone.1, s32[]{:T(128)} %constant.154.clone.1, s32[]{:T(128)} %constant.154.clone.1, s32[]{:T(128)S(6)} %select_n.333) | dynamic-update-slice | bytes 38916 | tf_op jit(solution)/shard_map/dynamic_update_slice | solution.py:66
  (471 shorter events, 299.8 us)
Async XLA Ops:
  4.3 36.6 %collective-permute-start.2 = (s32[16,16,1]{2,1,0:T(8,128)}, s32[16,16,1]{2,1,0:T(8,128)}, u32[]{:S(2)}, u32[]{:S(2)}) collective-permute-start(s32[16,16,1]{2,1,0:T(8,128)} %get-tuple-element.268), channel_id=1, source_target_pairs={{0,1},{2,3},{4,5},{6,7},{8,9},{10,11},{12,13},{14,15},{16,17},{18,... | collective-permute-start | bytes 3080 | tf_op jit(solution)/shard_map/ppermute | solution.py:41
  9.0 35.0 %collective-permute-start.3 = (s32[16,16,1]{2,1,0:T(8,128)}, s32[16,16,1]{2,1,0:T(8,128)}, u32[]{:S(2)}, u32[]{:S(2)}) collective-permute-start(s32[16,16,1]{2,1,0:T(8,128)} %get-tuple-element.267), channel_id=1, source_target_pairs={{1,0},{3,2},{5,4},{7,6},{9,8},{11,10},{13,12},{15,14},{17,16},{19,... | collective-permute-start | bytes 3080 | tf_op jit(solution)/shard_map/ppermute | solution.py:41
  13.2 38.2 %collective-permute-start.12 = (f32[7,16,16,1]{2,1,3,0:T(8,128)}, f32[7,16,16,1]{2,1,3,0:T(8,128)}, u32[]{:S(2)}, u32[]{:S(2)}) collective-permute-start(f32[7,16,16,1]{2,1,3,0:T(8,128)} %copy.96), channel_id=1, source_target_pairs={{0,1},{2,3},{4,5},{6,7},{8,9},{10,11},{12,13},{14,15},{16,17},{18,... | collective-permute-start | bytes 21512 | tf_op jit(solution)/shard_map/ppermute | solution.py:41
  19.8 40.3 %collective-permute-start.13 = (f32[7,16,16,1]{2,1,3,0:T(8,128)}, f32[7,16,16,1]{2,1,3,0:T(8,128)}, u32[]{:S(2)}, u32[]{:S(2)}) collective-permute-start(f32[7,16,16,1]{2,1,3,0:T(8,128)} %copy.98), channel_id=1, source_target_pairs={{1,0},{3,2},{5,4},{7,6},{9,8},{11,10},{13,12},{15,14},{17,16},{19,... | collective-permute-start | bytes 21512 | tf_op jit(solution)/shard_map/ppermute | solution.py:41
  30.3 42.6 %collective-permute-start = (f32[19,16,16,1]{0,2,3,1:T(8,128)}, f32[19,16,16,1]{0,2,3,1:T(8,128)}, u32[]{:S(2)}, u32[]{:S(2)}) collective-permute-start(f32[19,16,16,1]{0,2,3,1:T(8,128)} %copy.92), channel_id=1, source_target_pairs={{0,1},{2,3},{4,5},{6,7},{8,9},{10,11},{12,13},{14,15},{16,17},{18,... | collective-permute-start | bytes 58376 | tf_op jit(solution)/shard_map/ppermute | solution.py:41
  40.9 42.0 %collective-permute-start.1 = (f32[19,16,16,1]{0,2,3,1:T(8,128)}, f32[19,16,16,1]{0,2,3,1:T(8,128)}, u32[]{:S(2)}, u32[]{:S(2)}) collective-permute-start(f32[19,16,16,1]{0,2,3,1:T(8,128)} %copy.94), channel_id=1, source_target_pairs={{1,0},{3,2},{5,4},{7,6},{9,8},{11,10},{13,12},{15,14},{17,16},{19,... | collective-permute-start | bytes 58376 | tf_op jit(solution)/shard_map/ppermute | solution.py:41
  47.5 74.9 %collective-permute-start.4 = (s32[1,16,130]{2,1,0:T(8,128)S(1)}, s32[1,16,130]{2,1,0:T(8,128)S(1)}, u32[]{:S(2)}, u32[]{:S(2)}) collective-permute-start(s32[1,16,130]{2,1,0:T(8,128)S(1)} %get-tuple-element.266), channel_id=1, source_target_pairs={{8,0},{16,8},{24,16},{9,1},{17,9},{25,17},{10,2},{18,10},{26,18},{... | collective-permute-start | bytes 24968 | tf_op jit(solution)/shard_map/ppermute | solution.py:52
  51.4 74.6 %collective-permute-start.6 = (s32[1,16,130]{2,1,0:T(8,128)S(1)}, s32[1,16,130]{2,1,0:T(8,128)S(1)}, u32[]{:S(2)}, u32[]{:S(2)}) collective-permute-start(s32[1,16,130]{2,1,0:T(8,128)S(1)} %get-tuple-element.265), channel_id=1, source_target_pairs={{0,8},{8,16},{16,24},{1,9},{9,17},{17,25},{2,10},{10,18},{18,26},{... | collective-permute-start | bytes 24968 | tf_op jit(solution)/shard_map/ppermute | solution.py:51
  114.9 14.8 %collective-permute-start.5 = (f32[19,1,16,130]{3,2,1,0:T(8,128)S(1)}, f32[19,1,16,130]{3,2,1,0:T(8,128)S(1)}, u32[]{:S(2)}, u32[]{:S(2)}) collective-permute-start(f32[19,1,16,130]{3,2,1,0:T(8,128)S(1)} %get-tuple-element.225), channel_id=1, source_target_pairs={{8,0},{16,8},{24,16},{9,1},{17,9},{25,17},{10,2},{18,10},{26,18},{... | collective-permute-start | bytes 474248 | tf_op jit(solution)/shard_map/ppermute | solution.py:52
  120.5 17.9 %collective-permute-start.14 = (f32[7,1,16,130]{3,2,1,0:T(8,128)S(1)}, f32[7,1,16,130]{3,2,1,0:T(8,128)S(1)}, u32[]{:S(2)}, u32[]{:S(2)}) collective-permute-start(f32[7,1,16,130]{3,2,1,0:T(8,128)S(1)} %get-tuple-element.249), channel_id=1, source_target_pairs={{8,0},{16,8},{24,16},{9,1},{17,9},{25,17},{10,2},{18,10},{26,18},{... | collective-permute-start | bytes 174728 | tf_op jit(solution)/shard_map/ppermute | solution.py:52
  122.4 17.3 %collective-permute-start.15 = (f32[7,1,16,130]{3,2,1,0:T(8,128)S(1)}, f32[7,1,16,130]{3,2,1,0:T(8,128)S(1)}, u32[]{:S(2)}, u32[]{:S(2)}) collective-permute-start(f32[7,1,16,130]{3,2,1,0:T(8,128)S(1)} %get-tuple-element.248), channel_id=1, source_target_pairs={{0,8},{8,16},{16,24},{1,9},{9,17},{17,25},{2,10},{10,18},{18,26},{... | collective-permute-start | bytes 174728 | tf_op jit(solution)/shard_map/ppermute | solution.py:51
  126.1 15.0 %collective-permute-start.10 = (s32[18,1,130]{2,1,0:T(1,128)S(1)}, s32[18,1,130]{2,1,0:T(1,128)S(1)}, u32[]{:S(2)}, u32[]{:S(2)}) collective-permute-start(s32[18,1,130]{2,1,0:T(1,128)S(1)} %get-tuple-element.263), channel_id=1, source_target_pairs={{0,2},{2,4},{4,6},{1,3},{3,5},{5,7},{8,10},{10,12},{12,14},{9,11},... | collective-permute-start | bytes 28088 | tf_op jit(solution)/shard_map/ppermute | solution.py:51
  129.6 16.4 %collective-permute-start.8 = (s32[18,1,130]{2,1,0:T(1,128)S(1)}, s32[18,1,130]{2,1,0:T(1,128)S(1)}, u32[]{:S(2)}, u32[]{:S(2)}) collective-permute-start(s32[18,1,130]{2,1,0:T(1,128)S(1)} %get-tuple-element.264), channel_id=1, source_target_pairs={{2,0},{4,2},{6,4},{3,1},{5,3},{7,5},{10,8},{12,10},{14,12},{11,9},... | collective-permute-start | bytes 28088 | tf_op jit(solution)/shard_map/ppermute | solution.py:52
  134.2 19.0 %collective-permute-start.11 = (f32[19,18,1,130]{3,2,1,0:T(1,128)S(1)}, f32[19,18,1,130]{3,2,1,0:T(1,128)S(1)}, u32[]{:S(2)}, u32[]{:S(2)}) collective-permute-start(f32[19,18,1,130]{3,2,1,0:T(1,128)S(1)} %get-tuple-element.216), channel_id=1, source_target_pairs={{0,2},{2,4},{4,6},{1,3},{3,5},{5,7},{8,10},{10,12},{12,14},{9,11},... | collective-permute-start | bytes 533528 | tf_op jit(solution)/shard_map/ppermute | solution.py:51
  138.4 14.8 %collective-permute-start.9 = (f32[19,18,1,130]{3,2,1,0:T(1,128)S(1)}, f32[19,18,1,130]{3,2,1,0:T(1,128)S(1)}, u32[]{:S(2)}, u32[]{:S(2)}) collective-permute-start(f32[19,18,1,130]{3,2,1,0:T(1,128)S(1)} %get-tuple-element.217), channel_id=1, source_target_pairs={{2,0},{4,2},{6,4},{3,1},{5,3},{7,5},{10,8},{12,10},{14,12},{11,9},... | collective-permute-start | bytes 533528 | tf_op jit(solution)/shard_map/ppermute | solution.py:52
  164.7 28.1 %collective-permute-start.24 = (f32[7,16,16,1]{2,1,3,0:T(8,128)}, f32[7,16,16,1]{2,1,3,0:T(8,128)}, u32[]{:S(2)}, u32[]{:S(2)}) collective-permute-start(f32[7,16,16,1]{2,1,3,0:T(8,128)} %copy.104), channel_id=1, source_target_pairs={{0,1},{2,3},{4,5},{6,7},{8,9},{10,11},{12,13},{14,15},{16,17},{18,... | collective-permute-start | bytes 21512 | tf_op jit(solution)/shard_map/ppermute | solution.py:41
  171.6 26.9 %collective-permute-start.25 = (f32[7,16,16,1]{2,1,3,0:T(8,128)}, f32[7,16,16,1]{2,1,3,0:T(8,128)}, u32[]{:S(2)}, u32[]{:S(2)}) collective-permute-start(f32[7,16,16,1]{2,1,3,0:T(8,128)} %copy.106), channel_id=1, source_target_pairs={{1,0},{3,2},{5,4},{7,6},{9,8},{11,10},{13,12},{15,14},{17,16},{19,... | collective-permute-start | bytes 21512 | tf_op jit(solution)/shard_map/ppermute | solution.py:41
  182.0 29.7 %collective-permute-start.18 = (f32[19,16,16,1]{0,2,3,1:T(8,128)}, f32[19,16,16,1]{0,2,3,1:T(8,128)}, u32[]{:S(2)}, u32[]{:S(2)}) collective-permute-start(f32[19,16,16,1]{0,2,3,1:T(8,128)} %copy.100), channel_id=1, source_target_pairs={{0,1},{2,3},{4,5},{6,7},{8,9},{10,11},{12,13},{14,15},{16,17},{18,... | collective-permute-start | bytes 58376 | tf_op jit(solution)/shard_map/ppermute | solution.py:41
  191.3 30.4 %collective-permute-start.19 = (f32[19,16,16,1]{0,2,3,1:T(8,128)}, f32[19,16,16,1]{0,2,3,1:T(8,128)}, u32[]{:S(2)}, u32[]{:S(2)}) collective-permute-start(f32[19,16,16,1]{0,2,3,1:T(8,128)} %copy.102), channel_id=1, source_target_pairs={{1,0},{3,2},{5,4},{7,6},{9,8},{11,10},{13,12},{15,14},{17,16},{19,... | collective-permute-start | bytes 58376 | tf_op jit(solution)/shard_map/ppermute | solution.py:41
  268.5 15.7 %collective-permute-start.22 = (f32[19,18,1,130]{3,2,1,0:T(1,128)S(1)}, f32[19,18,1,130]{3,2,1,0:T(1,128)S(1)}, u32[]{:S(2)}, u32[]{:S(2)}) collective-permute-start(f32[19,18,1,130]{3,2,1,0:T(1,128)S(1)} %get-tuple-element.215), channel_id=1, source_target_pairs={{2,0},{4,2},{6,4},{3,1},{5,3},{7,5},{10,8},{12,10},{14,12},{11,9},... | collective-permute-start | bytes 533528 | tf_op jit(solution)/shard_map/ppermute | solution.py:52
  297.1 34.8 %collective-permute-start.36 = (f32[7,16,16,1]{2,1,3,0:T(8,128)}, f32[7,16,16,1]{2,1,3,0:T(8,128)}, u32[]{:S(2)}, u32[]{:S(2)}) collective-permute-start(f32[7,16,16,1]{2,1,3,0:T(8,128)} %copy.112), channel_id=1, source_target_pairs={{0,1},{2,3},{4,5},{6,7},{8,9},{10,11},{12,13},{14,15},{16,17},{18,... | collective-permute-start | bytes 21512 | tf_op jit(solution)/shard_map/ppermute | solution.py:41
  304.1 33.6 %collective-permute-start.37 = (f32[7,16,16,1]{2,1,3,0:T(8,128)}, f32[7,16,16,1]{2,1,3,0:T(8,128)}, u32[]{:S(2)}, u32[]{:S(2)}) collective-permute-start(f32[7,16,16,1]{2,1,3,0:T(8,128)} %copy.114), channel_id=1, source_target_pairs={{1,0},{3,2},{5,4},{7,6},{9,8},{11,10},{13,12},{15,14},{17,16},{19,... | collective-permute-start | bytes 21512 | tf_op jit(solution)/shard_map/ppermute | solution.py:41
  321.2 29.6 %collective-permute-start.30 = (f32[19,16,16,1]{0,2,3,1:T(8,128)}, f32[19,16,16,1]{0,2,3,1:T(8,128)}, u32[]{:S(2)}, u32[]{:S(2)}) collective-permute-start(f32[19,16,16,1]{0,2,3,1:T(8,128)} %copy.108), channel_id=1, source_target_pairs={{0,1},{2,3},{4,5},{6,7},{8,9},{10,11},{12,13},{14,15},{16,17},{18,... | collective-permute-start | bytes 58376 | tf_op jit(solution)/shard_map/ppermute | solution.py:41
  330.5 30.4 %collective-permute-start.31 = (f32[19,16,16,1]{0,2,3,1:T(8,128)}, f32[19,16,16,1]{0,2,3,1:T(8,128)}, u32[]{:S(2)}, u32[]{:S(2)}) collective-permute-start(f32[19,16,16,1]{0,2,3,1:T(8,128)} %copy.110), channel_id=1, source_target_pairs={{1,0},{3,2},{5,4},{7,6},{9,8},{11,10},{13,12},{15,14},{17,16},{19,... | collective-permute-start | bytes 58376 | tf_op jit(solution)/shard_map/ppermute | solution.py:41
  398.4 15.1 %collective-permute-start.38 = (f32[7,1,16,130]{3,2,1,0:T(8,128)S(1)}, f32[7,1,16,130]{3,2,1,0:T(8,128)S(1)}, u32[]{:S(2)}, u32[]{:S(2)}) collective-permute-start(f32[7,1,16,130]{3,2,1,0:T(8,128)S(1)} %get-tuple-element.245), channel_id=1, source_target_pairs={{8,0},{16,8},{24,16},{9,1},{17,9},{25,17},{10,2},{18,10},{26,18},{... | collective-permute-start | bytes 174728 | tf_op jit(solution)/shard_map/ppermute | solution.py:52
  407.7 15.8 %collective-permute-start.34 = (f32[19,18,1,130]{3,2,1,0:T(1,128)S(1)}, f32[19,18,1,130]{3,2,1,0:T(1,128)S(1)}, u32[]{:S(2)}, u32[]{:S(2)}) collective-permute-start(f32[19,18,1,130]{3,2,1,0:T(1,128)S(1)} %get-tuple-element.213), channel_id=1, source_target_pairs={{2,0},{4,2},{6,4},{3,1},{5,3},{7,5},{10,8},{12,10},{14,12},{11,9},... | collective-permute-start | bytes 533528 | tf_op jit(solution)/shard_map/ppermute | solution.py:52
  436.5 34.5 %collective-permute-start.48 = (f32[7,16,16,1]{2,1,3,0:T(8,128)}, f32[7,16,16,1]{2,1,3,0:T(8,128)}, u32[]{:S(2)}, u32[]{:S(2)}) collective-permute-start(f32[7,16,16,1]{2,1,3,0:T(8,128)} %copy.120), channel_id=1, source_target_pairs={{0,1},{2,3},{4,5},{6,7},{8,9},{10,11},{12,13},{14,15},{16,17},{18,... | collective-permute-start | bytes 21512 | tf_op jit(solution)/shard_map/ppermute | solution.py:41
  443.3 33.4 %collective-permute-start.49 = (f32[7,16,16,1]{2,1,3,0:T(8,128)}, f32[7,16,16,1]{2,1,3,0:T(8,128)}, u32[]{:S(2)}, u32[]{:S(2)}) collective-permute-start(f32[7,16,16,1]{2,1,3,0:T(8,128)} %copy.122), channel_id=1, source_target_pairs={{1,0},{3,2},{5,4},{7,6},{9,8},{11,10},{13,12},{15,14},{17,16},{19,... | collective-permute-start | bytes 21512 | tf_op jit(solution)/shard_map/ppermute | solution.py:41
  460.5 36.9 %collective-permute-start.42 = (f32[19,16,16,1]{0,2,3,1:T(8,128)}, f32[19,16,16,1]{0,2,3,1:T(8,128)}, u32[]{:S(2)}, u32[]{:S(2)}) collective-permute-start(f32[19,16,16,1]{0,2,3,1:T(8,128)} %copy.116), channel_id=1, source_target_pairs={{0,1},{2,3},{4,5},{6,7},{8,9},{10,11},{12,13},{14,15},{16,17},{18,... | collective-permute-start | bytes 58376 | tf_op jit(solution)/shard_map/ppermute | solution.py:41
  469.7 37.7 %collective-permute-start.43 = (f32[19,16,16,1]{0,2,3,1:T(8,128)}, f32[19,16,16,1]{0,2,3,1:T(8,128)}, u32[]{:S(2)}, u32[]{:S(2)}) collective-permute-start(f32[19,16,16,1]{0,2,3,1:T(8,128)} %copy.118), channel_id=1, source_target_pairs={{1,0},{3,2},{5,4},{7,6},{9,8},{11,10},{13,12},{15,14},{17,16},{19,... | collective-permute-start | bytes 58376 | tf_op jit(solution)/shard_map/ppermute | solution.py:41
  491.5 46.7 %collective-permute-start.50 = (f32[7,1,16,130]{3,2,1,0:T(8,128)}, f32[7,1,16,130]{3,2,1,0:T(8,128)}, u32[]{:S(2)}, u32[]{:S(2)}) collective-permute-start(f32[7,1,16,130]{3,2,1,0:T(8,128)} %get-tuple-element.243), channel_id=1, source_target_pairs={{8,0},{16,8},{24,16},{9,1},{17,9},{25,17},{10,2},{18,10},{26,18},{... | collective-permute-start | bytes 174728 | tf_op jit(solution)/shard_map/ppermute | solution.py:52
  494.3 44.0 %collective-permute-start.51 = (f32[7,1,16,130]{3,2,1,0:T(8,128)}, f32[7,1,16,130]{3,2,1,0:T(8,128)}, u32[]{:S(2)}, u32[]{:S(2)}) collective-permute-start(f32[7,1,16,130]{3,2,1,0:T(8,128)} %get-tuple-element.242), channel_id=1, source_target_pairs={{0,8},{8,16},{16,24},{1,9},{9,17},{17,25},{2,10},{10,18},{18,26},{... | collective-permute-start | bytes 174728 | tf_op jit(solution)/shard_map/ppermute | solution.py:51
  (121 other events, 1934.8 us)
where the time goes:
time: 586 us; the launch traced here: 576 us
  local copies, waits for them, and re-layouts  280 us (48%)
  starting transfers between devices  163 us (28%)
  other arithmetic  107 us (18%)
  waiting for transfers between devices  22.1 us (4%)
    dynamic_update_slice x8, local copies, waits for them, and re-layouts, extend(): grown = lax.dynamic_update_slice_in_dim(grown, from_above, length + 1, 3)  148 us
    ppermute x18, starting transfers between devices, padded_2(): before = lax.ppermute(last, axis, up)  67.6 us
    ppermute x18, starting transfers between devices, shifted(): return lax.ppermute(shard, axis, pairs)  59.7 us
    ppermute x16, local copies, waits for them, and re-layouts, shifted(): return lax.ppermute(shard, axis, pairs)  56.1 us
    unnamed x96, other arithmetic  42.8 us
    slice x16, local copies, waits for them, and re-layouts, extend(): from_above = shifted(field[:, :, :, 0:1], 'gz', -1)  37.6 us
    ppermute x18, starting transfers between devices, padded_2(): after = lax.ppermute(initial, axis, down)  35.6 us
    concatenate x8, other arithmetic, extend(): jnp.concatenate([from_below, field, jnp.zeros_like(from_below)], axis=3)  34.2 us
  transfers between devices with their start and end apart: 54, of which 9 were waited for; matrix products, arithmetic and copies ran while one was open for 48% of the time, Pallas kernels for 0%

commit v1 on v0

v1 whole, which is shorter than its diff:
```python
import functools

import jax
import jax.numpy as jnp
from jax import lax
from jax.experimental import pallas as pl
from jax.experimental.pallas import tpu as pltpu
from jax.sharding import PartitionSpec as P

BZC = 16

FLOW_DIRS = [
    (0, 0, 0),
    (1, 0, 0),
    (-1, 0, 0),
    (0, 1, 0),
    (0, -1, 0),
    (0, 0, 1),
    (0, 0, -1),
    (1, 1, 0),
    (-1, -1, 0),
    (1, -1, 0),
    (-1, 1, 0),
    (1, 0, 1),
    (-1, 0, -1),
    (1, 0, -1),
    (-1, 0, 1),
    (0, 1, 1),
    (0, -1, -1),
    (0, 1, -1),
    (0, -1, 1),
]
NF = 19
NS = 7
OPPOSITE = [FLOW_DIRS.index((-a, -b, -c)) for a, b, c in FLOW_DIRS]
SOLID = NF + NS
AUX = SOLID + 1
NA = 5
flow_omega = 1.25
solute_omega = 1.6
langmuir_rate = 0.05
VMEM_LIMIT = 50 * 1024 * 1024
F32 = jnp.float32


class Plan:
    def __init__(self, steps, nx, ny, depth):
        self.steps, self.nx, self.ny, self.depth = steps, nx, ny, depth
        self.halo = w = steps
        self.chan = AUX + NA * steps
        self.sent = AUX + NA * (steps - 1)
        self.pitch = -(-(ny + 2 * w) // 8) * 8
        self.wide = nx + 2 * w
        self.count = {k: AUX + NA * (steps - k) for k in range(1, w)}
        self.base, at = {}, 0
        for k in range(1, w):
            self.base[k] = at
            at += self.count[k]
        self.base[w] = at
        self.slab = at + 7

    def last(self, axis, sign):
        flow = [i for i, c in enumerate(FLOW_DIRS) if c[axis] == sign]
        solute = [NF + i for i, c in enumerate(FLOW_DIRS[:NS]) if c[axis] == sign]
        return flow + solute + [SOLID]


def lanes(depth):
    return lax.broadcasted_iota(jnp.int32, (8, depth), 1)


def occupied(owner_ref):
    me = lax.axis_index("gz")
    count = jnp.int32(0)
    for j in range(owner_ref.shape[0]):
        count = count + jnp.where(owner_ref[j] == me, 1, 0).astype(jnp.int32)
    return count * BZC


def z_places(plan, length, ring):
    w, depth = plan.halo, plan.depth
    if ring == 2:
        first = lax.axis_index("gz") == 0
        return [(jnp.where(first, length - w, 0), jnp.where(first, length, depth - w))]
    return [(length - w, jnp.int32(depth - w)), (jnp.int32(0), length)]


def for_channels(plan, sources, body, steps):
    flow, solute, density, velocity, level, solid = sources
    body(0, NF, lambda i, x: flow[i, x])
    body(NF, NS, lambda i, x: solute[i, x])
    body(SOLID, 1, lambda i, x: solid[x].astype(F32))
    for s in steps:
        t = plan.steps - 1 - s
        at = AUX + NA * s
        body(at, 1, lambda i, x, t=t: density[t, x].astype(F32))
        body(at + 1, 1, lambda i, x, t=t: level[t, x].astype(F32))
        body(at + 2, 3, lambda i, x, t=t: velocity[t, i, x].astype(F32))


def each(number, body):
    if number == 1:
        body(0)
    else:
        lax.fori_loop(0, number, lambda i, c: (body(i), c)[1], 0)


def pack_kernel(plan, ring, owner, flow, solute, density, velocity, level, solid, *outs):
    w, depth = plan.halo, plan.depth
    length = occupied(owner)
    lane = lanes(depth)
    places = z_places(plan, length, ring)
    tall = plan.ny // 8
    for (start, _), out in zip(places, outs):
        place = (lane - start) & (depth - 1)

        def body(at, number, read):
            def one(i):
                def merge(lo, count):
                    if count == 1:
                        x, h = divmod(lo, tall)
                        return read(i, x)[8 * h : 8 * h + 8]
                    half = count // 2
                    first, second = merge(lo, half), merge(lo + half, half)
                    return jnp.where(place < w * half, first, pltpu.roll(second, w * half, 1))

                packed = merge(0, plan.nx * tall)
                out[at + i] = pltpu.roll(packed, (depth - start) & (depth - 1), 1)

            each(number, one)

        for_channels(plan, (flow, solute, density, velocity, level, solid), body, range(plan.steps - 1))


def unpack(plan, ring, owner, sources, received, write, steps):
    w, depth = plan.halo, plan.depth
    length = occupied(owner)
    lane = lanes(depth)
    live = lane < length
    places = z_places(plan, length, ring)
    halos = [((lane - to) & (depth - 1)) < w for _, to in places]
    tall = plan.ny // 8

    def body(at, number, read):
        def one(i):
            slabs = []
            if not isinstance(at, int) or at < plan.sent:
                slabs = [pltpu.roll(r[at + i], to, 1) for r, (_, to) in zip(received, places)]
            for x in range(plan.nx):
                row = read(i, x)
                for h in range(tall):
                    tile = jnp.where(live, row[8 * h : 8 * h + 8], 0.0)
                    back = (depth - w * (x * tall + h)) % depth
                    for slab, halo in zip(slabs, halos):
                        tile = jnp.where(halo, pltpu.roll(slab, back, 1) if back else slab, tile)
                    write(at + i, x, h, tile)

        each(number, one)

    for_channels(plan, sources, body, steps)


def faces_kernel(plan, ring, parts, owner, flow, solute, density, velocity, level, solid, *rest):
    received, (y_low, y_high, x_low, x_high, cells) = rest[:parts], rest[parts:]
    w, nx, ny = plan.halo, plan.nx, plan.ny

    def write(c, x, h, tile):
        cells[c, x * ny + 8 * h : x * ny + 8 * h + 8, :] = tile

    unpack(plan, ring, owner, (flow, solute, density, velocity, level, solid), received, write, range(plan.steps - 1))

    def y_row(c, y):
        return cells[c, pl.ds(y, nx, stride=ny), :]

    def x_row(c, x):
        return cells[c, x * ny : (x + 1) * ny, :]

    for k in range(1, w):
        base = plan.base[k]

        def one(c, base=base, k=k):
            y_low[base + c] = y_row(c, k - 1)
            y_high[base + c] = y_row(c, ny - k)
            x_low[base + c] = x_row(c, k - 1)
            x_high[base + c] = x_row(c, nx - k)

        each(plan.count[k], one)
    for j in range(7):
        at = plan.base[w] + j
        y_low[at] = y_row(plan.last(1, 1)[j], w - 1)
        y_high[at] = y_row(plan.last(1, -1)[j], ny - w)
        x_low[at] = x_row(plan.last(0, 1)[j], w - 1)
        x_high[at] = x_row(plan.last(0, -1)[j], nx - w)


def inner_kernel(plan, ring, parts, owner, flow, solute, density, velocity, level, solid, *rest):
    received, out = rest[:parts], rest[parts]
    w, pitch = plan.halo, plan.pitch

    def write(c, x, h, tile):
        row = x * pitch + w + 8 * h
        out[c, row : row + 8, :] = tile

    unpack(plan, ring, owner, (flow, solute, density, velocity, level, solid), received, write, range(plan.steps))


def corners_kernel(plan, from_low, from_high, low, high):
    w, nx, ny = plan.halo, plan.nx, plan.ny
    low[...] = jnp.zeros(low.shape, F32)
    high[...] = jnp.zeros(high.shape, F32)
    tall = 2 * w
    for out, sign in ((low, 1), (high, -1)):
        x_last = plan.last(0, sign)
        for k in range(1, w + 1):
            x = k - 1 if sign == 1 else nx - k
            for m in range(1, w + 1):
                for source, row, y_sign in ((from_low, w - m, -1), (from_high, w - 1 + m, 1)):
                    y_last = plan.last(1, y_sign)
                    if k < w and m < w:
                        number = min(plan.count[k], plan.count[m])
                        out[pl.ds(plan.base[k] * tall + row, number, stride=tall), :] = source[
                            pl.ds(plan.base[m] * nx + x, number, stride=nx), :
                        ]
                        continue
                    for c in range(AUX):
                        if (k == w and c not in x_last) or (m == w and c not in y_last):
                            continue
                        to = plan.base[k] + (x_last.index(c) if k == w else c)
                        at = plan.base[m] + (y_last.index(c) if m == w else c)
                        out[to * tall + row : to * tall + row + 1, :] = source[at * nx + x : at * nx + x + 1, :]


PAD = 8


def steps_kernel(plan, owner, inner, y_low, y_high, x_low, x_high, c_low, c_high, flow_out, solute_out, cells, other, masks, sem):
    w, nx, ny, depth, pitch = plan.halo, plan.nx, plan.ny, plan.depth, plan.pitch
    copy = pltpu.make_async_copy(inner, cells.at[:, pl.ds(PAD + w * pitch, nx * pitch), :], sem)
    copy.start()
    for k in range(1, w + 1):
        for x_part, c_part, x, sign in ((x_low, c_low, w - k, -1), (x_high, c_high, w + nx - 1 + k, 1)):
            row = PAD + x * pitch

            def one(c, j, row=row, x_part=x_part, c_part=c_part):
                cells[c, row : row + w, :] = c_part[j, 0:w, :]
                cells[c, row + w : row + w + ny, :] = x_part[j]
                cells[c, row + w + ny : row + w + ny + w, :] = c_part[j, w : 2 * w, :]

            if k < w:
                each(plan.count[k], lambda c, one=one, k=k: one(c, plan.base[k] + c))
            else:
                for j, c in enumerate(plan.last(0, sign)):
                    one(c, plan.base[w] + j)
    copy.wait()
    for m in range(1, w + 1):
        for part, y, sign in ((y_low, w - m, -1), (y_high, w + ny - 1 + m, 1)):
            row = PAD + w * pitch + y

            def one(c, j, row=row, part=part):
                cells[c, pl.ds(row, nx, stride=pitch), :] = part[j]

            if m < w:
                each(plan.count[m], lambda c, one=one, m=m: one(c, plan.base[m] + c))
            else:
                for j, c in enumerate(plan.last(1, sign)):
                    one(c, plan.base[w] + j)

    length = occupied(owner)
    lane = lanes(depth)
    gx, gy, gz = (lax.axis_index(a) for a in ("gx", "gy", "gz"))
    last_x, last_y, last_z = (lax.axis_size(a) - 1 for a in ("gx", "gy", "gz"))
    above = jnp.where(gz < last_z, w, 0)
    below = jnp.where(gz > 0, w, 0)
    in_z = (lane < length + above) | (lane >= depth - below)
    y_first = jnp.where(gy > 0, 0, w)
    y_end = jnp.where(gy < last_y, ny + 2 * w, w + ny)
    x_first = jnp.where(gx > 0, 0, w)
    x_end = jnp.where(gx < last_x, nx + 2 * w, w + nx)
    sub = lax.broadcasted_iota(jnp.int32, (8, depth), 0)

    def prepare(x, carry):
        in_x = ((x >= x_first) & (x < x_end)).astype(F32)
        for h in range(pitch // 8):
            row = pl.multiple_of(PAD + x * pitch + 8 * h, 8)
            flags = cells[SOLID, pl.ds(row, 8), :]
            y = sub + 8 * h
            masks[0, pl.ds(row, 8), :] = pltpu.roll(flags, depth - 1, 1)
            masks[1, pl.ds(row, 8), :] = pltpu.roll(flags, 1, 1)
            inside = in_z & (y >= y_first) & (y < y_end) & (flags == 0.0)
            masks[2, pl.ds(row, 8), :] = jnp.where(inside, in_x, 0.0)
        return carry

    lax.fori_loop(0, plan.wide, prepare, 0)

    live = lane < length

    def tile(source, s, row, write):
        def field(ref, c, move=0):
            return ref[c, pl.ds(row + move, 8), :]

        blocked = {}

        def reads(first, number):
            result = []
            for i in range(number):
                sx, sy, sz = FLOW_DIRS[i]
                if i == 0:
                    result.append(field(source, first))
                    continue
                move = sx * pitch + sy
                near = field(source, first + i, move)
                if sz:
                    near = pltpu.roll(near, (depth - sz) % depth, 1)
                if i not in blocked:
                    flags = field(cells, SOLID, move) if sz == 0 else field(masks, 0 if sz == 1 else 1, move)
                    blocked[i] = flags != 0.0
                result.append(jnp.where(blocked[i], field(source, first + OPPOSITE[i]), near))
            return result

        valid = field(masks, 2)
        if s == plan.steps - 1:
            valid = jnp.where(live, valid, 0.0)
        aux = AUX + NA * s
        density, level, ux, uy, uz = (field(cells, aux + n) for n in range(NA))

        h = reads(NF, NS)
        px, py, pz = h[1] - h[2], h[3] - h[4], h[5] - h[6]
        p0 = 0.25 * h[0] + 0.125 * ((h[1] + h[2]) + (h[3] + h[4]) + (h[5] + h[6]))
        grown = 1.0 + level
        uptake = langmuir_rate / (grown * grown)
        common = valid * (
            (solute_omega - uptake) * p0 + (solute_omega * 0.5) * (px * ux + py * uy + pz * uz)
        )
        keep = (1.0 - solute_omega) * valid
        for i in range(NS):
            write(NF + i, keep * h[i] + common)
        factor = (0.5 * solute_omega) * level / jnp.maximum(density, 0.5)
        fx, fy, fz = factor * px, factor * py, factor * pz

        g = reads(0, NF)
        a = {i: g[i] + g[i + 1] for i in range(1, NF, 2)}
        d = {i: g[i] - g[i + 1] for i in range(1, NF, 2)}
        m1x = (d[1] + d[1]) + (d[7] + d[9]) + (d[11] + d[13])
        m1y = (d[3] + d[3]) + (d[7] - d[9]) + (d[15] + d[17])
        m1z = (d[5] + d[5]) + (d[11] - d[13]) + (d[15] - d[17])
        exy, exz, eyz = a[7] + a[9], a[11] + a[13], a[15] + a[17]
        tx, ty, tz = a[1] + a[1], a[3] + a[3], a[5] + a[5]
        mxx, myy, mzz = tx + exy + exz, ty + exy + eyz, tz + exz + eyz
        mxy, mxz, myz = a[7] - a[9], a[11] - a[13], a[15] - a[17]
        m0 = 12.0 * g[0] + (tx + ty + tz) + (exy + exz + eyz)
        qx = mxx * ux + mxy * uy + mxz * uz
        qy = mxy * ux + myy * uy + myz * uz
        qz = mxz * ux + myz * uy + mzz * uz
        square = ux * ux + uy * uy + uz * uz
        scaled = flow_omega / 36.0
        zero = m0 * (scaled + (1.5 * scaled) * square) - (4.5 * scaled) * (qx * ux + qy * uy + qz * uz)
        zero = valid * (zero - (fx * ux + fy * uy + fz * uz))
        bx = valid * ((3.0 * scaled) * (m1x + 3.0 * qx - m0 * ux) + fx)
        by = valid * ((3.0 * scaled) * (m1y + 3.0 * qy - m0 * uy) + fy)
        bz = valid * ((3.0 * scaled) * (m1z + 3.0 * qz - m0 * uz) + fz)
        keep = (1.0 - flow_omega) * valid
        write(0, keep * g[0] + zero)
        moves = {1: bx, 3: by, 5: bz, 7: bx + by, 9: bx - by, 11: bx + bz, 13: bx - bz, 15: by + bz, 17: by - bz}
        for i, move in moves.items():
            write(i, keep * g[i] + (zero + move))
            write(i + 1, keep * g[i + 1] + (zero - move))

    buffers = [cells, other]
    for s in range(plan.steps - 1):
        source, target = buffers[s % 2], buffers[(s + 1) % 2]
        first = PAD + (1 + s) * pitch
        tiles = (plan.wide - 2 - 2 * s) * (pitch // 8)

        def body(n, carry, source=source, target=target, first=first, s=s):
            row = pl.multiple_of(first + 8 * n, 8)

            def write(c, value):
                target[c, pl.ds(row, 8), :] = value

            tile(source, s, row, write)
            return carry

        lax.fori_loop(0, tiles, body, 0)

    s = plan.steps - 1
    source = buffers[s % 2]

    def last(x, carry):
        for h in range(ny // 8):
            row = PAD + (x + w) * pitch + w + 8 * h

            def write(c, value, h=h):
                if c < NF:
                    flow_out[c, x, 8 * h : 8 * h + 8, :] = value
                else:
                    solute_out[c - NF, x, 8 * h : 8 * h + 8, :] = value

            tile(source, s, row, write)
        return carry

    lax.fori_loop(0, nx, last, 0)


VMEM = pl.BlockSpec(memory_space=pltpu.VMEM)
SMEM = pl.BlockSpec(memory_space=pltpu.SMEM)
ANY = pl.BlockSpec(memory_space=pl.ANY)


def call(kernel, ins, outs, name, cost, scratch=()):
    return pl.pallas_call(
        kernel,
        in_specs=ins,
        out_shape=outs,
        out_specs=[VMEM] * len(outs),
        scratch_shapes=list(scratch),
        name=name,
        cost_estimate=pl.CostEstimate(flops=cost, bytes_accessed=1 << 23, transcendentals=0),
        compiler_params=pltpu.CompilerParams(vmem_limit_bytes=VMEM_LIMIT),
    )


def per_device(flow_adjoint, solute_adjoint, flow_density, flow_velocity, solute_level, solid, owner):
    steps = flow_density.shape[0]
    nx, ny, depth = solid.shape
    plan = Plan(steps, nx, ny, depth)
    ring = lax.axis_size("gz")
    w = plan.halo
    fields = (flow_adjoint, solute_adjoint, flow_density, flow_velocity, solute_level, solid)

    def move(value, axis, by):
        size = lax.axis_size(axis)
        return lax.ppermute(value, axis, [(i, i + by) for i in range(size) if 0 <= i + by < size])

    parts = 1 if ring == 2 else 2
    packed_shape = jax.ShapeDtypeStruct((plan.sent, 8, depth), F32)
    packed = call(
        functools.partial(pack_kernel, plan, ring), [SMEM] + [VMEM] * 6, [packed_shape] * parts, "pack_column", 1 << 22
    )(owner, *fields)
    if ring == 2:
        received = [lax.ppermute(packed[0], "gz", [(0, 1), (1, 0)])]
    else:
        received = [move(packed[0], "gz", 1), move(packed[1], "gz", -1)]

    def slab(rows):
        return jax.ShapeDtypeStruct((plan.slab, rows, depth), F32)

    y_low, y_high, x_low, x_high = call(
        functools.partial(faces_kernel, plan, ring, parts),
        [SMEM] + [VMEM] * (6 + parts),
        [slab(nx), slab(nx), slab(ny), slab(ny)],
        "faces",
        1 << 22,
        [pltpu.VMEM((plan.sent, nx * ny, depth), F32)],
    )(owner, *fields, *received)
    from_y_low = move(y_high, "gy", 1)
    from_y_high = move(y_low, "gy", -1)
    from_x_low = move(x_high, "gx", 1)
    from_x_high = move(x_low, "gx", -1)
    inner = call(
        functools.partial(inner_kernel, plan, ring, parts),
        [SMEM] + [VMEM] * (6 + parts),
        [jax.ShapeDtypeStruct((plan.chan, nx * plan.pitch, depth), F32)],
        "inner",
        1 << 22,
    )(owner, *fields, *received)[0]

    def rows(value):
        return value.reshape(-1, depth)

    corner = jax.ShapeDtypeStruct((plan.slab * 2 * w, depth), F32)
    c_low, c_high = call(
        functools.partial(corners_kernel, plan), [VMEM] * 2, [corner, corner], "corners", 1 << 20
    )(rows(from_y_low), rows(from_y_high))
    shape = (plan.slab, 2 * w, depth)
    from_c_low = move(c_high, "gx", 1).reshape(shape)
    from_c_high = move(c_low, "gx", -1).reshape(shape)
    height = plan.wide * plan.pitch + 2 * PAD
    flow, solute = call(
        functools.partial(steps_kernel, plan),
        [SMEM, ANY] + [VMEM] * 6,
        [jax.ShapeDtypeStruct(flow_adjoint.shape, F32), jax.ShapeDtypeStruct(solute_adjoint.shape, F32)],
        "steps",
        1 << 28,
        [
            pltpu.VMEM((plan.chan, height, depth), F32),
            pltpu.VMEM((NF + NS, height, depth), F32),
            pltpu.VMEM((3, height, depth), F32),
            pltpu.SemaphoreType.DMA,
        ],
    )(owner, inner, from_y_low, from_y_high, from_x_low, from_x_high, from_c_low, from_c_high)
    return (flow, solute)


def solution(mesh):
    in_specs = (
        P(None, "gx", "gy", "gz"),
        P(None, "gx", "gy", "gz"),
        P(None, "gx", "gy", "gz"),
        P(None, None, "gx", "gy", "gz"),
        P(None, "gx", "gy", "gz"),
        P("gx", "gy", "gz"),
        P(),
    )
    out_specs = (P(None, "gx", "gy", "gz"), P(None, "gx", "gy", "gz"))
    return jax.shard_map(
        per_device, mesh=mesh, in_specs=in_specs, out_specs=out_specs, check_vma=False
    )
```

time: 586 us -> 118 us (0.20); the launches traced: 576 us -> 118 us
  local copies, waits for them, and re-layouts: 280 us -> 6.71 us
  starting transfers between devices: 163 us -> 21 us
  other arithmetic: 107 us -> 0 us
  Pallas kernels: 0 us -> 70.3 us
    dynamic_update_slice x9 -> x0, local copies, waits for them, and re-layouts: 151 us -> none  [the longest x8 148 us: extend(): grown = lax.dynamic_update_slice_in_dim(grown, from_above, length + 1, 3)]
    ppermute x54 -> x7, starting transfers between devices: 163 us -> 21 us  [the longest x6 18.9 us: move(): lax.ppermute(value, axis, [(i, i + by) for i in range(size) if 0 <= i + b...]
    pallas_call x0 -> x5, Pallas kernels: none -> 70.3 us  [the longest x1 30.1 us: per_device(): call(functools.partial(steps_kernel, plan), [SMEM, ANY] + [VMEM] * 6, [ja...]
    ppermute x16 -> x0, local copies, waits for them, and re-layouts: 56.1 us -> none  [shifted(): return lax.ppermute(shard, axis, pairs)]
    concatenate x19 -> x0, other arithmetic: 48.3 us -> none  [the longest x8 34.2 us: extend(): jnp.concatenate([from_below, field, jnp.zeros_like(from_below)], axis=3)]
    slice x26 -> x0, local copies, waits for them, and re-layouts: 46.2 us -> none  [the longest x16 37.6 us: extend(): from_above = shifted(field[:, :, :, 0:1], 'gz', -1)]
    unnamed x96 -> x0, other arithmetic: 42.8 us -> none
    dynamic_slice x8 -> x0, local copies, waits for them, and re-layouts: 23.8 us -> none  [extend(): top_layer = lax.dynamic_slice_in_dim(field, length - 1, 1, 3)]
  transfers between devices with their start and end apart: 54 -> 7, of which waited for: 9 -> 3; matrix products, arithmetic and copies ran while one was open for 48% -> 0% of each run, Pallas kernels for 0% -> 10%
where the time goes in v1:
time: 118 us
  Pallas kernels  70.3 us (60%)
  starting transfers between devices  21 us (18%)
  waiting for transfers between devices  19 us (16%)
  local copies, waits for them, and re-layouts  6.71 us (6%)
    pallas_call x1, Pallas kernels, per_device(): call(functools.partial(steps_kernel, plan), [SMEM, ANY] + [VMEM] * 6, [ja...  30.1 us
    ppermute x6, starting transfers between devices, move(): lax.ppermute(value, axis, [(i, i + by) for i in range(size) if 0 <= i + b...  18.9 us
    pallas_call x1, Pallas kernels, per_device(): call(functools.partial(pack_kernel, plan, ring), [SMEM] + [VMEM] * 6, [pa...  16.9 us
    ppermute x6, waiting for transfers between devices, move(): lax.ppermute(value, axis, [(i, i + by) for i in range(size) if 0 <= i + b...  14.9 us
    pallas_call x1, Pallas kernels, per_device(): call(functools.partial(inner_kernel, plan, ring, parts), [SMEM] + [VMEM]...  11.8 us
    pallas_call x1, Pallas kernels, per_device(): call(functools.partial(faces_kernel, plan, ring, parts), [SMEM] + [VMEM]...  11 us
    unnamed x22, local copies, waits for them, and re-layouts  6.71 us
    ppermute x1, waiting for transfers between devices, per_device(): received = [lax.ppermute(packed[0], 'gz', [(0, 1), (1, 0)])]  4.1 us
  transfers between devices with their start and end apart: 7, of which 3 were waited for; matrix products, arithmetic and copies ran while one was open for 0% of the time, Pallas kernels for 10%

profile of v1, /device:TPU:1, one launch (start us, length us, event | category | flops | bytes accessed | tf_op | source)
XLA Modules:
  0.0 117.8 jit_solution(17864892732182706828)
XLA Ops:
  0.6 0.0 copy-start
  0.6 1.2 copy-done
  1.8 1.1 copy-done.2
  2.9 0.9 copy-done.4
  3.9 0.9 copy-done.5
  4.8 0.9 copy-done.7
  5.8 0.7 copy-done.9
  6.4 16.9 %pack_column.1 = f32[42,8,128]{2,1,0:T(8,128)S(1)} custom-call(s32[8]{0:T(128)S(1)} %copy-done.9, f32[19,16,16,128]{3,2,1,0:T(8,128)} %flow.5, f32[7,16,16,128]{3,2,1,0:T(8,128)S(1)} %copy-done, bf16[4,16,16,128]{3,2,1,0:T(8,128)(2,1)S(1)} %copy-done.4, bf16[4,3,16,16,128]{4,3,2,1,0:T(8,128)(2,1)S(1)} %copy-done.2, bf16[4,16,16,128]{3,2,1,0:T(8,128)(2,1)S(1)} %copy-done.5, ...), custom_call_target="tpu_custom_call" | custom-call | flops 4194304 | bytes 8388608 | tf_op jit(solution)/shard_map/pack_column/pallas_call | solution.py:436
  23.3 0.0 copy-start.8
  23.3 2.1 %collective-permute-start = (f32[42,8,128]{2,1,0:T(8,128)S(1)}, f32[42,8,128]{2,1,0:T(8,128)S(1)}, u32[]{:S(2)}, u32[]{:S(2)}) collective-permute-start(f32[42,8,128]{2,1,0:T(8,128)S(1)} %pack_column.1), channel_id=1, source_target_pairs={{0,1},{1,0},{2,3},{3,2},{4,5},{5,4},{6,7},{7,6},{8,9},{9,8},{10,11... | collective-permute-start | bytes 516104 | tf_op jit(solution)/shard_map/ppermute | solution.py:440
  25.5 4.1 %collective-permute-done.rest_0_ = f32[42,8,128]{2,1,0:T(8,128)S(1)} collective-permute-done((f32[42,8,128]{2,1,0:T(8,128)S(1)}, f32[42,8,128]{2,1,0:T(8,128)S(1)}, u32[]{:S(2)}, u32[]{:S(2)}) %collective-permute-start) | collective-permute-done | bytes 172064 | tf_op jit(solution)/shard_map/ppermute | solution.py:440
  29.6 11.0 %faces.1 = (f32[118,16,128]{2,1,0:T(8,128)S(1)}, f32[118,16,128]{2,1,0:T(8,128)}, f32[118,16,128]{2,1,0:T(8,128)}, f32[118,16,128]{2,1,0:T(8,128)}) custom-call(s32[8]{0:T(128)S(1)} %copy-done.9, f32[19,16,16,128]{3,2,1,0:T(8,128)} %flow.5, f32[7,16,16,128]{3,2,1,0:T(8,128)S(1)} %copy-done, bf16[4,16,16,128]{3,2,1,0:T(8,128)(2,1)S(1)} %copy-done.4, ...), custom_call_target="tpu_custom_call" | custom-call | flops 4194304 | bytes 8388608 | tf_op jit(solution)/shard_map/faces/pallas_call | solution.py:447
  40.6 3.2 %collective-permute-start.1 = (f32[118,16,128]{2,1,0:T(8,128)}, f32[118,16,128]{2,1,0:T(8,128)S(1)}, u32[]{:S(2)}, u32[]{:S(2)}) collective-permute-start(f32[118,16,128]{2,1,0:T(8,128)} %get-tuple-element.8), channel_id=1, source_target_pairs={{0,2},{2,4},{4,6},{1,3},{3,5},{5,7},{8,10},{10,12},{12,14},{9,11},... | collective-permute-start | bytes 2899976 | tf_op jit(solution)/shard_map/ppermute | solution.py:432
  43.7 1.3 %collective-permute-start.2 = (f32[118,16,128]{2,1,0:T(8,128)S(1)}, f32[118,16,128]{2,1,0:T(8,128)S(1)}, u32[]{:S(2)}, u32[]{:S(2)}) collective-permute-start(f32[118,16,128]{2,1,0:T(8,128)S(1)} %get-tuple-element.9), channel_id=1, source_target_pairs={{2,0},{4,2},{6,4},{3,1},{5,3},{7,5},{10,8},{12,10},{14,12},{11,9},... | collective-permute-start | bytes 2899976 | tf_op jit(solution)/shard_map/ppermute | solution.py:432
  45.0 4.8 %collective-permute-start.3 = (f32[118,16,128]{2,1,0:T(8,128)}, f32[118,16,128]{2,1,0:T(8,128)S(1)}, u32[]{:S(2)}, u32[]{:S(2)}) collective-permute-start(f32[118,16,128]{2,1,0:T(8,128)} %get-tuple-element.10), channel_id=1, source_target_pairs={{0,8},{8,16},{16,24},{1,9},{9,17},{17,25},{2,10},{10,18},{18,26},{... | collective-permute-start | bytes 2899976 | tf_op jit(solution)/shard_map/ppermute | solution.py:432
  49.9 1.9 %collective-permute-start.4 = (f32[118,16,128]{2,1,0:T(8,128)}, f32[118,16,128]{2,1,0:T(8,128)S(1)}, u32[]{:S(2)}, u32[]{:S(2)}) collective-permute-start(f32[118,16,128]{2,1,0:T(8,128)} %get-tuple-element.11), channel_id=1, source_target_pairs={{8,0},{16,8},{24,16},{9,1},{17,9},{25,17},{10,2},{18,10},{26,18},{... | collective-permute-start | bytes 2899976 | tf_op jit(solution)/shard_map/ppermute | solution.py:432
  51.8 11.3 %collective-permute-done.1.y_low = f32[118,16,128]{2,1,0:T(8,128)S(1)} collective-permute-done((f32[118,16,128]{2,1,0:T(8,128)}, f32[118,16,128]{2,1,0:T(8,128)S(1)}, u32[]{:S(2)}, u32[]{:S(2)}) %collective-permute-start.1) | collective-permute-done | bytes 966688 | tf_op jit(solution)/shard_map/ppermute | solution.py:432
  63.1 3.6 %collective-permute-done.2.y_high = f32[118,16,128]{2,1,0:T(8,128)S(1)} collective-permute-done((f32[118,16,128]{2,1,0:T(8,128)S(1)}, f32[118,16,128]{2,1,0:T(8,128)S(1)}, u32[]{:S(2)}, u32[]{:S(2)}) %collective-permute-start.2) | collective-permute-done | bytes 966688 | tf_op jit(solution)/shard_map/ppermute | solution.py:432
  66.7 0.4 corners.1
  67.1 5.8 %collective-permute-start.5 = (f32[944,128]{1,0:T(8,128)S(1)}, f32[944,128]{1,0:T(8,128)S(1)}, u32[]{:S(2)}, u32[]{:S(2)}) collective-permute-start(f32[944,128]{1,0:T(8,128)S(1)} %get-tuple-element.12), channel_id=1, source_target_pairs={{0,8},{8,16},{16,24},{1,9},{9,17},{17,25},{2,10},{10,18},{18,26},{... | collective-permute-start | bytes 1449992 | tf_op jit(solution)/shard_map/ppermute | solution.py:432
  72.9 1.9 %collective-permute-start.6 = (f32[944,128]{1,0:T(8,128)S(1)}, f32[944,128]{1,0:T(8,128)S(1)}, u32[]{:S(2)}, u32[]{:S(2)}) collective-permute-start(f32[944,128]{1,0:T(8,128)S(1)} %get-tuple-element.13), channel_id=1, source_target_pairs={{8,0},{16,8},{24,16},{9,1},{17,9},{25,17},{10,2},{18,10},{26,18},{... | collective-permute-start | bytes 1449992 | tf_op jit(solution)/shard_map/ppermute | solution.py:432
  74.8 0.0 copy-done.1
  74.8 0.0 copy-done.3
  74.8 0.0 copy-done.6
  74.8 0.0 copy-done.8
  74.8 11.8 %inner.1 = f32[47,384,128]{2,1,0:T(8,128)} custom-call(s32[8]{0:T(128)S(1)} %copy-done.9, f32[19,16,16,128]{3,2,1,0:T(8,128)} %flow.5, f32[7,16,16,128]{3,2,1,0:T(8,128)S(1)} %copy-done.1, bf16[4,16,16,128]{3,2,1,0:T(8,128)(2,1)S(1)} %copy-done.4, bf16[4,3,16,16,128]{4,3,2,1,0:T(8,128)(2,1)S(1)} %copy-done.3, bf16[4,16,16,128]{3,2,1,0:T(8,128)(2,1)S(1)} %copy-done.6, ...), custom_call_target="tpu_custom_call" | custom-call | flops 4194304 | bytes 8388608 | tf_op jit(solution)/shard_map/inner/pallas_call | solution.py:459
  86.7 0.0 collective-permute-done.3.x_low
  86.7 0.0 collective-permute-done.4.x_high
  86.7 0.0 collective-permute-done.5
  86.7 0.0 collective-permute-done.6
  86.7 0.9 copy-done.10
  87.6 30.1 %steps.1 = (f32[19,16,16,128]{3,2,1,0:T(8,128)}, f32[7,16,16,128]{3,2,1,0:T(8,128)}) custom-call(s32[8]{0:T(128)S(1)} %copy-done.9, f32[47,384,128]{2,1,0:T(8,128)} %inner.1, f32[118,16,128]{2,1,0:T(8,128)S(1)} %collective-permute-done.1.y_low, f32[118,16,128]{2,1,0:T(8,128)S(1)} %collective-permute-done.2.y_high, ...), custom_call_target="tpu_custom_call" | custom-call | flops 268435456 | bytes 8388608 | tf_op jit(solution)/shard_map/steps/pallas_call | solution.py:478
  (9 shorter events, 0.0 us)
Async XLA Ops:
  0.6 1.2 %copy-start = (f32[7,16,16,128]{3,2,1,0:T(8,128)S(1)}, f32[7,16,16,128]{3,2,1,0:T(8,128)}, u32[]{:S(2)}) copy-start(f32[7,16,16,128]{3,2,1,0:T(8,128)} %solute.5) | copy-start | bytes 2752516
  1.8 1.1 copy-start.2
  2.9 0.9 copy-start.4
  3.9 0.9 copy-start.5
  4.8 0.9 copy-start.7
  5.8 0.7 copy-start.9
  23.3 51.5 %copy-start.1 = (f32[7,16,16,128]{3,2,1,0:T(8,128)S(1)}, f32[7,16,16,128]{3,2,1,0:T(8,128)}, u32[]{:S(2)}) copy-start(f32[7,16,16,128]{3,2,1,0:T(8,128)} %solute.5) | copy-start | bytes 2752516
  23.3 51.5 %copy-start.3 = (bf16[4,3,16,16,128]{4,3,2,1,0:T(8,128)(2,1)S(1)}, bf16[4,3,16,16,128]{4,3,2,1,0:T(8,128)(2,1)}, u32[]{:S(2)}) copy-start(bf16[4,3,16,16,128]{4,3,2,1,0:T(8,128)(2,1)} %velocity.5) | copy-start | bytes 2359300
  23.3 51.5 %copy-start.6 = (bf16[4,16,16,128]{3,2,1,0:T(8,128)(2,1)S(1)}, bf16[4,16,16,128]{3,2,1,0:T(8,128)(2,1)}, u32[]{:S(2)}) copy-start(bf16[4,16,16,128]{3,2,1,0:T(8,128)(2,1)} %level.5) | copy-start | bytes 786436
  23.3 51.5 %copy-start.8 = (s32[16,16,128]{2,1,0:T(8,128)S(1)}, s32[16,16,128]{2,1,0:T(8,128)}, u32[]{:S(2)}) copy-start(s32[16,16,128]{2,1,0:T(8,128)} %solid.5) | copy-start | bytes 393220
  23.3 6.2 %collective-permute-start = (f32[42,8,128]{2,1,0:T(8,128)S(1)}, f32[42,8,128]{2,1,0:T(8,128)S(1)}, u32[]{:S(2)}, u32[]{:S(2)}) collective-permute-start(f32[42,8,128]{2,1,0:T(8,128)S(1)} %pack_column.1), channel_id=1, source_target_pairs={{0,1},{1,0},{2,3},{3,2},{4,5},{5,4},{6,7},{7,6},{8,9},{9,8},{10,11... | collective-permute-start | bytes 516104 | tf_op jit(solution)/shard_map/ppermute | solution.py:440
  40.6 22.5 %collective-permute-start.1 = (f32[118,16,128]{2,1,0:T(8,128)}, f32[118,16,128]{2,1,0:T(8,128)S(1)}, u32[]{:S(2)}, u32[]{:S(2)}) collective-permute-start(f32[118,16,128]{2,1,0:T(8,128)} %get-tuple-element.8), channel_id=1, source_target_pairs={{0,2},{2,4},{4,6},{1,3},{3,5},{5,7},{8,10},{10,12},{12,14},{9,11},... | collective-permute-start | bytes 2899976 | tf_op jit(solution)/shard_map/ppermute | solution.py:432
  43.7 23.0 %collective-permute-start.2 = (f32[118,16,128]{2,1,0:T(8,128)S(1)}, f32[118,16,128]{2,1,0:T(8,128)S(1)}, u32[]{:S(2)}, u32[]{:S(2)}) collective-permute-start(f32[118,16,128]{2,1,0:T(8,128)S(1)} %get-tuple-element.9), channel_id=1, source_target_pairs={{2,0},{4,2},{6,4},{3,1},{5,3},{7,5},{10,8},{12,10},{14,12},{11,9},... | collective-permute-start | bytes 2899976 | tf_op jit(solution)/shard_map/ppermute | solution.py:432
  45.0 41.6 %collective-permute-start.3 = (f32[118,16,128]{2,1,0:T(8,128)}, f32[118,16,128]{2,1,0:T(8,128)S(1)}, u32[]{:S(2)}, u32[]{:S(2)}) collective-permute-start(f32[118,16,128]{2,1,0:T(8,128)} %get-tuple-element.10), channel_id=1, source_target_pairs={{0,8},{8,16},{16,24},{1,9},{9,17},{17,25},{2,10},{10,18},{18,26},{... | collective-permute-start | bytes 2899976 | tf_op jit(solution)/shard_map/ppermute | solution.py:432
  49.9 36.8 %collective-permute-start.4 = (f32[118,16,128]{2,1,0:T(8,128)}, f32[118,16,128]{2,1,0:T(8,128)S(1)}, u32[]{:S(2)}, u32[]{:S(2)}) collective-permute-start(f32[118,16,128]{2,1,0:T(8,128)} %get-tuple-element.11), channel_id=1, source_target_pairs={{8,0},{16,8},{24,16},{9,1},{17,9},{25,17},{10,2},{18,10},{26,18},{... | collective-permute-start | bytes 2899976 | tf_op jit(solution)/shard_map/ppermute | solution.py:432
  67.1 19.6 %collective-permute-start.5 = (f32[944,128]{1,0:T(8,128)S(1)}, f32[944,128]{1,0:T(8,128)S(1)}, u32[]{:S(2)}, u32[]{:S(2)}) collective-permute-start(f32[944,128]{1,0:T(8,128)S(1)} %get-tuple-element.12), channel_id=1, source_target_pairs={{0,8},{8,16},{16,24},{1,9},{9,17},{17,25},{2,10},{10,18},{18,26},{... | collective-permute-start | bytes 1449992 | tf_op jit(solution)/shard_map/ppermute | solution.py:432
  72.9 13.8 %collective-permute-start.6 = (f32[944,128]{1,0:T(8,128)S(1)}, f32[944,128]{1,0:T(8,128)S(1)}, u32[]{:S(2)}, u32[]{:S(2)}) collective-permute-start(f32[944,128]{1,0:T(8,128)S(1)} %get-tuple-element.13), channel_id=1, source_target_pairs={{8,0},{16,8},{24,16},{9,1},{17,9},{25,17},{10,2},{18,10},{26,18},{... | collective-permute-start | bytes 1449992 | tf_op jit(solution)/shard_map/ppermute | solution.py:432
  86.7 0.9 copy-start.10

commit v2 on v1

--- a/solution.py
+++ b/solution.py
@@ -85,9 +85,13 @@
     return [(length - w, jnp.int32(depth - w)), (jnp.int32(0), length)]
 
 
-def for_channels(plan, sources, body, steps):
-    flow, solute, density, velocity, level, solid = sources
+def for_channels(plan, arrays, held, sems, body, steps):
+    copies = fetch(arrays, held, sems)
+    flow, solute, density, velocity, level, solid = held
+    copies[0].wait()
     body(0, NF, lambda i, x: flow[i, x])
+    for copy in copies[1:]:
+        copy.wait()
     body(NF, NS, lambda i, x: solute[i, x])
     body(SOLID, 1, lambda i, x: solid[x].astype(F32))
     for s in steps:
@@ -98,41 +102,56 @@
         body(at + 2, 3, lambda i, x, t=t: velocity[t, i, x].astype(F32))
 
 
-def each(number, body):
-    if number == 1:
-        body(0)
+def each(number, body, unroll=4):
+    def several(i, carry):
+        for u in range(unroll):
+            body(i * unroll + u)
+        return carry
+
+    turns = number // unroll
+    if turns > 1:
+        lax.fori_loop(0, turns, several, 0)
     else:
-        lax.fori_loop(0, number, lambda i, c: (body(i), c)[1], 0)
-
-
-def pack_kernel(plan, ring, owner, flow, solute, density, velocity, level, solid, *outs):
+        turns = 0
+    for i in range(turns * unroll, number):
+        body(i)
+
+
+def fetch(arrays, held, sems):
+    copies = [pltpu.make_async_copy(a, b, sems.at[i]) for i, (a, b) in enumerate(zip(arrays, held))]
+    for copy in copies:
+        copy.start()
+    return copies
+
+
+def pack_kernel(plan, ring, parts, *refs):
+    owner, arrays, outs, held, sems = refs[0], refs[1:7], refs[7 : 7 + parts], refs[7 + parts : 13 + parts], refs[-1]
     w, depth = plan.halo, plan.depth
     length = occupied(owner)
-    lane = lanes(depth)
+    group = lanes(depth) // w
     places = z_places(plan, length, ring)
     tall = plan.ny // 8
-    for (start, _), out in zip(places, outs):
-        place = (lane - start) & (depth - 1)
-
-        def body(at, number, read):
-            def one(i):
-                def merge(lo, count):
-                    if count == 1:
-                        x, h = divmod(lo, tall)
-                        return read(i, x)[8 * h : 8 * h + 8]
-                    half = count // 2
-                    first, second = merge(lo, half), merge(lo + half, half)
-                    return jnp.where(place < w * half, first, pltpu.roll(second, w * half, 1))
-
-                packed = merge(0, plan.nx * tall)
-                out[at + i] = pltpu.roll(packed, (depth - start) & (depth - 1), 1)
-
-            each(number, one)
-
-        for_channels(plan, (flow, solute, density, velocity, level, solid), body, range(plan.steps - 1))
-
-
-def unpack(plan, ring, owner, sources, received, write, steps):
+    shifts = [[(w * n + depth - start) & (depth - 1) for n in range(plan.nx * tall)] for start, _ in places]
+
+    def body(at, number, read):
+        def one(i):
+            packed = [None] * parts
+            for x in range(plan.nx):
+                row = read(i, x)
+                for h in range(tall):
+                    n = x * tall + h
+                    for p in range(parts):
+                        moved = pltpu.roll(row[8 * h : 8 * h + 8], shifts[p][n], 1)
+                        packed[p] = moved if n == 0 else jnp.where(group == n, moved, packed[p])
+            for p in range(parts):
+                outs[p][at + i] = packed[p]
+
+        each(number, one, 3)
+
+    for_channels(plan, arrays, held, sems, body, range(plan.steps - 1))
+
+
+def unpack(plan, ring, owner, arrays, held, sems, received, write, steps):
     w, depth = plan.halo, plan.depth
     length = occupied(owner)
     lane = lanes(depth)
@@ -155,19 +174,20 @@
                         tile = jnp.where(halo, pltpu.roll(slab, back, 1) if back else slab, tile)
                     write(at + i, x, h, tile)
 
-        each(number, one)
-
-    for_channels(plan, sources, body, steps)
-
-
-def faces_kernel(plan, ring, parts, owner, flow, solute, density, velocity, level, solid, *rest):
-    received, (y_low, y_high, x_low, x_high, cells) = rest[:parts], rest[parts:]
+        each(number, one, 3)
+
+    for_channels(plan, arrays, held, sems, body, steps)
+
+
+def faces_kernel(plan, ring, parts, *refs):
+    owner, arrays, received, rest = refs[0], refs[1:7], refs[7 : 7 + parts], refs[7 + parts :]
+    (y_low, y_high, x_low, x_high, cells), held, sems = rest[:5], rest[5:11], rest[11]
     w, nx, ny = plan.halo, plan.nx, plan.ny
 
     def write(c, x, h, tile):
         cells[c, x * ny + 8 * h : x * ny + 8 * h + 8, :] = tile
 
-    unpack(plan, ring, owner, (flow, solute, density, velocity, level, solid), received, write, range(plan.steps - 1))
+    unpack(plan, ring, owner, arrays, held, sems, received, write, range(plan.steps - 1))
 
     def y_row(c, y):
         return cells[c, pl.ds(y, nx, stride=ny), :]
@@ -193,18 +213,19 @@
         x_high[at] = x_row(plan.last(0, -1)[j], nx - w)
 
 
-def inner_kernel(plan, ring, parts, owner, flow, solute, density, velocity, level, solid, *rest):
-    received, out = rest[:parts], rest[parts]
+def inner_kernel(plan, ring, parts, *refs):
+    owner, arrays, received, rest = refs[0], refs[1:7], refs[7 : 7 + parts], refs[7 + parts :]
+    out, held, sems = rest[0], rest[1:7], rest[7]
     w, pitch = plan.halo, plan.pitch
 
     def write(c, x, h, tile):
         row = x * pitch + w + 8 * h
         out[c, row : row + 8, :] = tile
 
-    unpack(plan, ring, owner, (flow, solute, density, velocity, level, solid), received, write, range(plan.steps))
-
-
-def corners_kernel(plan, from_low, from_high, low, high):
+    unpack(plan, ring, owner, arrays, held, sems, received, write, range(plan.steps))
+
+
+def corners_kernel(plan, from_low, from_high, inner, low, high):
     w, nx, ny = plan.halo, plan.nx, plan.ny
     low[...] = jnp.zeros(low.shape, F32)
     high[...] = jnp.zeros(high.shape, F32)
@@ -233,37 +254,51 @@
 PAD = 8
 
 
-def steps_kernel(plan, owner, inner, y_low, y_high, x_low, x_high, c_low, c_high, flow_out, solute_out, cells, other, masks, sem):
+def steps_kernel(plan, owner, inner, y_low, y_high, x_low, x_high, c_low, c_high, flow_out, solute_out, cells, other, fields, masks, sems):
     w, nx, ny, depth, pitch = plan.halo, plan.nx, plan.ny, plan.depth, plan.pitch
-    copy = pltpu.make_async_copy(inner, cells.at[:, pl.ds(PAD + w * pitch, nx * pitch), :], sem)
-    copy.start()
+    middle = pl.ds(PAD + w * pitch, nx * pitch)
+    copies = [
+        pltpu.make_async_copy(inner.at[pl.ds(0, SOLID)], cells.at[:, middle, :], sems.at[0]),
+        pltpu.make_async_copy(inner.at[pl.ds(SOLID, plan.chan - SOLID)], fields.at[:, middle, :], sems.at[1]),
+    ]
+    for copy in copies:
+        copy.start()
+
+    def channels(number, body):
+        each(SOLID, lambda c: body(cells, c, c))
+        each(number - SOLID, lambda c: body(fields, c, SOLID + c))
+
+    def channel(c):
+        return (cells, c) if c < SOLID else (fields, c - SOLID)
+
     for k in range(1, w + 1):
         for x_part, c_part, x, sign in ((x_low, c_low, w - k, -1), (x_high, c_high, w + nx - 1 + k, 1)):
             row = PAD + x * pitch
 
-            def one(c, j, row=row, x_part=x_part, c_part=c_part):
-                cells[c, row : row + w, :] = c_part[j, 0:w, :]
-                cells[c, row + w : row + w + ny, :] = x_part[j]
-                cells[c, row + w + ny : row + w + ny + w, :] = c_part[j, w : 2 * w, :]
+            def one(ref, c, j, row=row, x_part=x_part, c_part=c_part):
+                ref[c, row : row + w, :] = c_part[j, 0:w, :]
+                ref[c, row + w : row + w + ny, :] = x_part[j]
+                ref[c, row + w + ny : row + w + ny + w, :] = c_part[j, w : 2 * w, :]
 
             if k < w:
-                each(plan.count[k], lambda c, one=one, k=k: one(c, plan.base[k] + c))
+                channels(plan.count[k], lambda ref, c, j, one=one, k=k: one(ref, c, plan.base[k] + j))
             else:
                 for j, c in enumerate(plan.last(0, sign)):
-                    one(c, plan.base[w] + j)
-    copy.wait()
+                    one(*channel(c), plan.base[w] + j)
+    for copy in copies:
+        copy.wait()
     for m in range(1, w + 1):
         for part, y, sign in ((y_low, w - m, -1), (y_high, w + ny - 1 + m, 1)):
             row = PAD + w * pitch + y
 
-            def one(c, j, row=row, part=part):
-                cells[c, pl.ds(row, nx, stride=pitch), :] = part[j]
+            def one(ref, c, j, row=row, part=part):
+                ref[c, pl.ds(row, nx, stride=pitch), :] = part[j]
 
             if m < w:
-                each(plan.count[m], lambda c, one=one, m=m: one(c, plan.base[m] + c))
+                channels(plan.count[m], lambda ref, c, j, one=one, m=m: one(ref, c, plan.base[m] + j))
             else:
                 for j, c in enumerate(plan.last(1, sign)):
-                    one(c, plan.base[w] + j)
+                    one(*channel(c), plan.base[w] + j)
 
     length = occupied(owner)
     lane = lanes(depth)
@@ -282,7 +317,7 @@
         in_x = ((x >= x_first) & (x < x_end)).astype(F32)
         for h in range(pitch // 8):
             row = pl.multiple_of(PAD + x * pitch + 8 * h, 8)
-            flags = cells[SOLID, pl.ds(row, 8), :]
+            flags = fields[0, pl.ds(row, 8), :]
             y = sub + 8 * h
             masks[0, pl.ds(row, 8), :] = pltpu.roll(flags, depth - 1, 1)
             masks[1, pl.ds(row, 8), :] = pltpu.roll(flags, 1, 1)
@@ -312,7 +347,7 @@
                 if sz:
                     near = pltpu.roll(near, (depth - sz) % depth, 1)
                 if i not in blocked:
-                    flags = field(cells, SOLID, move) if sz == 0 else field(masks, 0 if sz == 1 else 1, move)
+                    flags = field(fields, 0, move) if sz == 0 else field(masks, 0 if sz == 1 else 1, move)
                     blocked[i] = flags != 0.0
                 result.append(jnp.where(blocked[i], field(source, first + OPPOSITE[i]), near))
             return result
@@ -320,8 +355,8 @@
         valid = field(masks, 2)
         if s == plan.steps - 1:
             valid = jnp.where(live, valid, 0.0)
-        aux = AUX + NA * s
-        density, level, ux, uy, uz = (field(cells, aux + n) for n in range(NA))
+        aux = AUX - SOLID + NA * s
+        density, level, ux, uy, uz = (field(fields, aux + n) for n in range(NA))
 
         h = reads(NF, NS)
         px, py, pz = h[1] - h[2], h[3] - h[4], h[5] - h[6]
@@ -369,18 +404,18 @@
     for s in range(plan.steps - 1):
         source, target = buffers[s % 2], buffers[(s + 1) % 2]
         first = PAD + (1 + s) * pitch
-        tiles = (plan.wide - 2 - 2 * s) * (pitch // 8)
 
         def body(n, carry, source=source, target=target, first=first, s=s):
-            row = pl.multiple_of(first + 8 * n, 8)
-
-            def write(c, value):
-                target[c, pl.ds(row, 8), :] = value
-
-            tile(source, s, row, write)
+            for h in range(pitch // 8):
+                row = pl.multiple_of(first + pitch * n + 8 * h, 8)
+
+                def write(c, value, row=row):
+                    target[c, pl.ds(row, 8), :] = value
+
+                tile(source, s, row, write)
             return carry
 
-        lax.fori_loop(0, tiles, body, 0)
+        lax.fori_loop(0, plan.wide - 2 - 2 * s, body, 0)
 
     s = plan.steps - 1
     source = buffers[s % 2]
@@ -406,7 +441,7 @@
 ANY = pl.BlockSpec(memory_space=pl.ANY)
 
 
-def call(kernel, ins, outs, name, cost, scratch=()):
+def call(kernel, ins, outs, name, cost, scratch=(), limit=VMEM_LIMIT):
     return pl.pallas_call(
         kernel,
         in_specs=ins,
@@ -415,7 +450,7 @@
         scratch_shapes=list(scratch),
         name=name,
         cost_estimate=pl.CostEstimate(flops=cost, bytes_accessed=1 << 23, transcendentals=0),
-        compiler_params=pltpu.CompilerParams(vmem_limit_bytes=VMEM_LIMIT),
+        compiler_params=pltpu.CompilerParams(vmem_limit_bytes=limit),
     )
 
 
@@ -433,8 +468,15 @@
 
     parts = 1 if ring == 2 else 2
     packed_shape = jax.ShapeDtypeStruct((plan.sent, 8, depth), F32)
+    held = [pltpu.VMEM(f.shape, f.dtype) for f in fields] + [pltpu.SemaphoreType.DMA((len(fields),))]
     packed = call(
-        functools.partial(pack_kernel, plan, ring), [SMEM] + [VMEM] * 6, [packed_shape] * parts, "pack_column", 1 << 22
+        functools.partial(pack_kernel, plan, ring, parts),
+        [SMEM] + [ANY] * 6,
+        [packed_shape] * parts,
+        "pack_column",
+        1 << 22,
+        held,
+        60 << 20,
     )(owner, *fields)
     if ring == 2:
         received = [lax.ppermute(packed[0], "gz", [(0, 1), (1, 0)])]
@@ -446,11 +488,11 @@
 
     y_low, y_high, x_low, x_high = call(
         functools.partial(faces_kernel, plan, ring, parts),
-        [SMEM] + [VMEM] * (6 + parts),
+        [SMEM] + [ANY] * 6 + [VMEM] * parts,
         [slab(nx), slab(nx), slab(ny), slab(ny)],
         "faces",
         1 << 22,
-        [pltpu.VMEM((plan.sent, nx * ny, depth), F32)],
+        [pltpu.VMEM((plan.sent, nx * ny, depth), F32)] + held,
     )(owner, *fields, *received)
     from_y_low = move(y_high, "gy", 1)
     from_y_high = move(y_low, "gy", -1)
@@ -458,10 +500,11 @@
     from_x_high = move(x_low, "gx", -1)
     inner = call(
         functools.partial(inner_kernel, plan, ring, parts),
-        [SMEM] + [VMEM] * (6 + parts),
+        [SMEM] + [ANY] * 6 + [VMEM] * parts,
         [jax.ShapeDtypeStruct((plan.chan, nx * plan.pitch, depth), F32)],
         "inner",
-        1 << 22,
+        1 << 24,
+        held,
     )(owner, *fields, *received)[0]
 
     def rows(value):
@@ -469,8 +512,8 @@
 
     corner = jax.ShapeDtypeStruct((plan.slab * 2 * w, depth), F32)
     c_low, c_high = call(
-        functools.partial(corners_kernel, plan), [VMEM] * 2, [corner, corner], "corners", 1 << 20
-    )(rows(from_y_low), rows(from_y_high))
+        functools.partial(corners_kernel, plan), [VMEM] * 2 + [ANY], [corner, corner], "corners", 1 << 20
+    )(rows(from_y_low), rows(from_y_high), inner)
     shape = (plan.slab, 2 * w, depth)
     from_c_low = move(c_high, "gx", 1).reshape(shape)
     from_c_high = move(c_low, "gx", -1).reshape(shape)
@@ -482,10 +525,11 @@
         "steps",
         1 << 28,
         [
-            pltpu.VMEM((plan.chan, height, depth), F32),
-            pltpu.VMEM((NF + NS, height, depth), F32),
+            pltpu.VMEM((SOLID, height, depth), F32),
+            pltpu.VMEM((SOLID, height, depth), F32),
+            pltpu.VMEM((plan.chan - SOLID, height, depth), F32),
             pltpu.VMEM((3, height, depth), F32),
-            pltpu.SemaphoreType.DMA,
+            pltpu.SemaphoreType.DMA((2,)),
         ],
     )(owner, inner, from_y_low, from_y_high, from_x_low, from_x_high, from_c_low, from_c_high)
     return (flow, solute)

time: 118 us -> 83.4 us (0.71)
  Pallas kernels: 70.3 us -> 43.3 us
  local copies, waits for them, and re-layouts: 6.71 us -> 0.03 us
    pallas_call x4, Pallas kernels: 40.1 us -> 23.1 us  [the longest x1 9.42 us: per_device(): call(functools.partial(inner_kernel, plan, ring, parts), [SMEM] + [ANY] *...]
    pallas_call x1, Pallas kernels: 30.1 us -> 20.3 us  [per_device(): call(functools.partial(steps_kernel, plan), [SMEM, ANY] + [VMEM] * 6, [ja...]
    unnamed x22 -> x14, local copies, waits for them, and re-layouts: 6.71 us -> 0.03 us
    ppermute x6, waiting for transfers between devices: 14.9 us -> 13.6 us  [move(): lax.ppermute(value, axis, [(i, i + by) for i in range(size) if 0 <= i + b...]
  transfers between devices with their start and end apart: 7 -> 7, of which waited for: 3 -> 5; matrix products, arithmetic and copies ran while one was open for 0% -> 0% of each run, Pallas kernels for 10% -> 12%
where the time goes in v2:
time: 83.4 us; the launch traced here: 83.1 us
  Pallas kernels  43.3 us (52%)
  starting transfers between devices  21 us (25%)
  waiting for transfers between devices  17.9 us (21%)
    pallas_call x1, Pallas kernels, per_device(): call(functools.partial(steps_kernel, plan), [SMEM, ANY] + [VMEM] * 6, [ja...  20.3 us
    ppermute x6, starting transfers between devices, move(): lax.ppermute(value, axis, [(i, i + by) for i in range(size) if 0 <= i + b...  18.9 us
    ppermute x6, waiting for transfers between devices, move(): lax.ppermute(value, axis, [(i, i + by) for i in range(size) if 0 <= i + b...  13.6 us
    pallas_call x1, Pallas kernels, per_device(): call(functools.partial(inner_kernel, plan, ring, parts), [SMEM] + [ANY] *...  9.42 us
    pallas_call x1, Pallas kernels, per_device(): call(functools.partial(faces_kernel, plan, ring, parts), [SMEM] + [ANY] *...  8.17 us
    pallas_call x1, Pallas kernels, per_device(): call(functools.partial(pack_kernel, plan, ring, parts), [SMEM] + [ANY] *...  5.08 us
    ppermute x1, waiting for transfers between devices, per_device(): received = [lax.ppermute(packed[0], 'gz', [(0, 1), (1, 0)])]  4.31 us
    ppermute x1, starting transfers between devices, per_device(): received = [lax.ppermute(packed[0], 'gz', [(0, 1), (1, 0)])]  2.13 us
  transfers between devices with their start and end apart: 7, of which 5 were waited for; matrix products, arithmetic and copies ran while one was open for 0% of the time, Pallas kernels for 12%

profile of v2, /device:TPU:1, one launch (start us, length us, event | category | flops | bytes accessed | tf_op | source)
XLA Modules:
  0.0 83.1 jit_solution(15435701558435620101)
XLA Ops:
  0.6 0.0 copy-start.5
  0.6 0.0 copy-start.4
  0.7 0.0 copy-start.3
  0.7 0.0 copy-start.1
  0.7 0.0 copy-start.2
  0.7 0.0 copy-start
  0.7 5.1 %pack_column.1 = f32[42,8,128]{2,1,0:T(8,128)} custom-call(s32[8]{0:T(128)} %owner.1, f32[19,16,16,128]{3,2,1,0:T(8,128)} %refs_1_.5, f32[7,16,16,128]{3,2,1,0:T(8,128)} %refs_2_.5, bf16[4,16,16,128]{3,2,1,0:T(8,128)(2,1)} %refs_3_.5, bf16[4,3,16,16,128]{4,3,2,1,0:T(8,128)(2,1)} %refs_4_.5, bf16[4,16,16,128]{3,2,1,0:T(8,128)(2,1)} %refs_5_.5, ...), custom_call_target="tpu_custom_call" | custom-call | flops 4194304 | bytes 8388608 | tf_op jit(solution)/shard_map/pack_column/pallas_call | solution.py:472
  5.8 2.1 %collective-permute-start = (f32[42,8,128]{2,1,0:T(8,128)}, f32[42,8,128]{2,1,0:T(8,128)S(1)}, u32[]{:S(2)}, u32[]{:S(2)}) collective-permute-start(f32[42,8,128]{2,1,0:T(8,128)} %pack_column.1), channel_id=1, source_target_pairs={{0,1},{1,0},{2,3},{3,2},{4,5},{5,4},{6,7},{7,6},{8,9},{9,8},{10,11... | collective-permute-start | bytes 516104 | tf_op jit(solution)/shard_map/ppermute | solution.py:482
  7.9 4.3 %collective-permute-done.refs_7_ = f32[42,8,128]{2,1,0:T(8,128)S(1)} collective-permute-done((f32[42,8,128]{2,1,0:T(8,128)}, f32[42,8,128]{2,1,0:T(8,128)S(1)}, u32[]{:S(2)}, u32[]{:S(2)}) %collective-permute-start) | collective-permute-done | bytes 172064 | tf_op jit(solution)/shard_map/ppermute | solution.py:482
  12.2 0.0 copy-done.5
  12.2 0.0 copy-done.4
  12.2 0.0 copy-done.3
  12.2 0.0 copy-done.1
  12.2 0.0 copy-done.2
  12.3 0.0 copy-done
  12.3 8.2 %faces.1 = (f32[118,16,128]{2,1,0:T(8,128)S(1)}, f32[118,16,128]{2,1,0:T(8,128)}, f32[118,16,128]{2,1,0:T(8,128)}, f32[118,16,128]{2,1,0:T(8,128)}) custom-call(s32[8]{0:T(128)S(1)} %copy-done.5, f32[19,16,16,128]{3,2,1,0:T(8,128)} %refs_1_.5, f32[7,16,16,128]{3,2,1,0:T(8,128)S(1)} %copy-done, bf16[4,16,16,128]{3,2,1,0:T(8,128)(2,1)S(1)} %copy-done.2, ...), custom_call_target="tpu_custom_call" | custom-call | flops 4194304 | bytes 8388608 | tf_op jit(solution)/shard_map/faces/pallas_call | solution.py:489
  20.4 3.2 %collective-permute-start.1 = (f32[118,16,128]{2,1,0:T(8,128)}, f32[118,16,128]{2,1,0:T(8,128)S(1)}, u32[]{:S(2)}, u32[]{:S(2)}) collective-permute-start(f32[118,16,128]{2,1,0:T(8,128)} %get-tuple-element.8), channel_id=1, source_target_pairs={{0,2},{2,4},{4,6},{1,3},{3,5},{5,7},{8,10},{10,12},{12,14},{9,11},... | collective-permute-start | bytes 2899976 | tf_op jit(solution)/shard_map/ppermute | solution.py:467
  23.6 1.3 %collective-permute-start.2 = (f32[118,16,128]{2,1,0:T(8,128)S(1)}, f32[118,16,128]{2,1,0:T(8,128)S(1)}, u32[]{:S(2)}, u32[]{:S(2)}) collective-permute-start(f32[118,16,128]{2,1,0:T(8,128)S(1)} %get-tuple-element.9), channel_id=1, source_target_pairs={{2,0},{4,2},{6,4},{3,1},{5,3},{7,5},{10,8},{12,10},{14,12},{11,9},... | collective-permute-start | bytes 2899976 | tf_op jit(solution)/shard_map/ppermute | solution.py:467
  24.9 4.8 %collective-permute-start.3 = (f32[118,16,128]{2,1,0:T(8,128)}, f32[118,16,128]{2,1,0:T(8,128)S(1)}, u32[]{:S(2)}, u32[]{:S(2)}) collective-permute-start(f32[118,16,128]{2,1,0:T(8,128)} %get-tuple-element.10), channel_id=1, source_target_pairs={{0,8},{8,16},{16,24},{1,9},{9,17},{17,25},{2,10},{10,18},{18,26},{... | collective-permute-start | bytes 2899976 | tf_op jit(solution)/shard_map/ppermute | solution.py:467
  29.8 1.9 %collective-permute-start.4 = (f32[118,16,128]{2,1,0:T(8,128)}, f32[118,16,128]{2,1,0:T(8,128)S(1)}, u32[]{:S(2)}, u32[]{:S(2)}) collective-permute-start(f32[118,16,128]{2,1,0:T(8,128)} %get-tuple-element.11), channel_id=1, source_target_pairs={{8,0},{16,8},{24,16},{9,1},{17,9},{25,17},{10,2},{18,10},{26,18},{... | collective-permute-start | bytes 2899976 | tf_op jit(solution)/shard_map/ppermute | solution.py:467
  31.7 9.4 %inner.1 = f32[47,384,128]{2,1,0:T(8,128)} custom-call(s32[8]{0:T(128)S(1)} %copy-done.5, f32[19,16,16,128]{3,2,1,0:T(8,128)} %refs_1_.5, f32[7,16,16,128]{3,2,1,0:T(8,128)S(1)} %copy-done, bf16[4,16,16,128]{3,2,1,0:T(8,128)(2,1)S(1)} %copy-done.2, bf16[4,3,16,16,128]{4,3,2,1,0:T(8,128)(2,1)S(1)} %copy-done.1, bf16[4,16,16,128]{3,2,1,0:T(8,128)(2,1)S(1)} %copy-done.3, ...), custom_call_target="tpu_custom_call" | custom-call | flops 16777216 | bytes 8388608 | tf_op jit(solution)/shard_map/inner/pallas_call | solution.py:501
  41.1 1.9 %collective-permute-done.1.y_low = f32[118,16,128]{2,1,0:T(8,128)S(1)} collective-permute-done((f32[118,16,128]{2,1,0:T(8,128)}, f32[118,16,128]{2,1,0:T(8,128)S(1)}, u32[]{:S(2)}, u32[]{:S(2)}) %collective-permute-start.1) | collective-permute-done | bytes 966688 | tf_op jit(solution)/shard_map/ppermute | solution.py:467
  43.0 3.6 %collective-permute-done.2.y_high = f32[118,16,128]{2,1,0:T(8,128)S(1)} collective-permute-done((f32[118,16,128]{2,1,0:T(8,128)S(1)}, f32[118,16,128]{2,1,0:T(8,128)S(1)}, u32[]{:S(2)}, u32[]{:S(2)}) %collective-permute-start.2) | collective-permute-done | bytes 966688 | tf_op jit(solution)/shard_map/ppermute | solution.py:467
  46.6 0.4 corners.1
  47.0 5.8 %collective-permute-start.5 = (f32[944,128]{1,0:T(8,128)S(1)}, f32[944,128]{1,0:T(8,128)S(1)}, u32[]{:S(2)}, u32[]{:S(2)}) collective-permute-start(f32[944,128]{1,0:T(8,128)S(1)} %get-tuple-element.12), channel_id=1, source_target_pairs={{0,8},{8,16},{16,24},{1,9},{9,17},{17,25},{2,10},{10,18},{18,26},{... | collective-permute-start | bytes 1449992 | tf_op jit(solution)/shard_map/ppermute | solution.py:467
  52.7 1.9 %collective-permute-start.6 = (f32[944,128]{1,0:T(8,128)S(1)}, f32[944,128]{1,0:T(8,128)S(1)}, u32[]{:S(2)}, u32[]{:S(2)}) collective-permute-start(f32[944,128]{1,0:T(8,128)S(1)} %get-tuple-element.13), channel_id=1, source_target_pairs={{8,0},{16,8},{24,16},{9,1},{17,9},{25,17},{10,2},{18,10},{26,18},{... | collective-permute-start | bytes 1449992 | tf_op jit(solution)/shard_map/ppermute | solution.py:467
  54.7 0.0 collective-permute-done.3.x_low
  54.7 0.0 collective-permute-done.4.x_high
  54.7 0.0 copy-start.6
  54.7 3.7 %collective-permute-done.5 = f32[944,128]{1,0:T(8,128)S(1)} collective-permute-done((f32[944,128]{1,0:T(8,128)S(1)}, f32[944,128]{1,0:T(8,128)S(1)}, u32[]{:S(2)}, u32[]{:S(2)}) %collective-permute-start.5) | collective-permute-done | bytes 483360 | tf_op jit(solution)/shard_map/ppermute | solution.py:467
  58.4 4.4 %collective-permute-done.6 = f32[944,128]{1,0:T(8,128)S(1)} collective-permute-done((f32[944,128]{1,0:T(8,128)S(1)}, f32[944,128]{1,0:T(8,128)S(1)}, u32[]{:S(2)}, u32[]{:S(2)}) %collective-permute-start.6) | collective-permute-done | bytes 483360 | tf_op jit(solution)/shard_map/ppermute | solution.py:467
  62.8 20.3 %steps.1 = (f32[19,16,16,128]{3,2,1,0:T(8,128)}, f32[7,16,16,128]{3,2,1,0:T(8,128)}) custom-call(s32[8]{0:T(128)S(1)} %copy-done.5, f32[47,384,128]{2,1,0:T(8,128)} %inner.1, f32[118,16,128]{2,1,0:T(8,128)S(1)} %collective-permute-done.1.y_low, f32[118,16,128]{2,1,0:T(8,128)S(1)} %collective-permute-done.2.y_high, ...), custom_call_target="tpu_custom_call" | custom-call | flops 268435456 | bytes 8388608 | tf_op jit(solution)/shard_map/steps/pallas_call | solution.py:521
  (1 shorter events, 0.0 us)
Async XLA Ops:
  0.6 11.6 %copy-start.5 = (s32[8]{0:T(128)S(1)}, s32[8]{0:T(128)}, u32[]{:S(2)}) copy-start(s32[8]{0:T(128)} %owner.1) | copy-start | bytes 100
  0.6 11.6 %copy-start.4 = (s32[16,16,128]{2,1,0:T(8,128)S(1)}, s32[16,16,128]{2,1,0:T(8,128)}, u32[]{:S(2)}) copy-start(s32[16,16,128]{2,1,0:T(8,128)} %refs_6_.5) | copy-start | bytes 393220
  0.7 11.6 %copy-start.3 = (bf16[4,16,16,128]{3,2,1,0:T(8,128)(2,1)S(1)}, bf16[4,16,16,128]{3,2,1,0:T(8,128)(2,1)}, u32[]{:S(2)}) copy-start(bf16[4,16,16,128]{3,2,1,0:T(8,128)(2,1)} %refs_5_.5) | copy-start | bytes 786436
  0.7 11.6 %copy-start.1 = (bf16[4,3,16,16,128]{4,3,2,1,0:T(8,128)(2,1)S(1)}, bf16[4,3,16,16,128]{4,3,2,1,0:T(8,128)(2,1)}, u32[]{:S(2)}) copy-start(bf16[4,3,16,16,128]{4,3,2,1,0:T(8,128)(2,1)} %refs_4_.5) | copy-start | bytes 2359300
  0.7 11.6 %copy-start.2 = (bf16[4,16,16,128]{3,2,1,0:T(8,128)(2,1)S(1)}, bf16[4,16,16,128]{3,2,1,0:T(8,128)(2,1)}, u32[]{:S(2)}) copy-start(bf16[4,16,16,128]{3,2,1,0:T(8,128)(2,1)} %refs_3_.5) | copy-start | bytes 786436
  0.7 11.6 %copy-start = (f32[7,16,16,128]{3,2,1,0:T(8,128)S(1)}, f32[7,16,16,128]{3,2,1,0:T(8,128)}, u32[]{:S(2)}) copy-start(f32[7,16,16,128]{3,2,1,0:T(8,128)} %refs_2_.5) | copy-start | bytes 2752516
  5.8 6.4 %collective-permute-start = (f32[42,8,128]{2,1,0:T(8,128)}, f32[42,8,128]{2,1,0:T(8,128)S(1)}, u32[]{:S(2)}, u32[]{:S(2)}) collective-permute-start(f32[42,8,128]{2,1,0:T(8,128)} %pack_column.1), channel_id=1, source_target_pairs={{0,1},{1,0},{2,3},{3,2},{4,5},{5,4},{6,7},{7,6},{8,9},{9,8},{10,11... | collective-permute-start | bytes 516104 | tf_op jit(solution)/shard_map/ppermute | solution.py:482
  20.4 22.6 %collective-permute-start.1 = (f32[118,16,128]{2,1,0:T(8,128)}, f32[118,16,128]{2,1,0:T(8,128)S(1)}, u32[]{:S(2)}, u32[]{:S(2)}) collective-permute-start(f32[118,16,128]{2,1,0:T(8,128)} %get-tuple-element.8), channel_id=1, source_target_pairs={{0,2},{2,4},{4,6},{1,3},{3,5},{5,7},{8,10},{10,12},{12,14},{9,11},... | collective-permute-start | bytes 2899976 | tf_op jit(solution)/shard_map/ppermute | solution.py:467
  23.6 23.0 %collective-permute-start.2 = (f32[118,16,128]{2,1,0:T(8,128)S(1)}, f32[118,16,128]{2,1,0:T(8,128)S(1)}, u32[]{:S(2)}, u32[]{:S(2)}) collective-permute-start(f32[118,16,128]{2,1,0:T(8,128)S(1)} %get-tuple-element.9), channel_id=1, source_target_pairs={{2,0},{4,2},{6,4},{3,1},{5,3},{7,5},{10,8},{12,10},{14,12},{11,9},... | collective-permute-start | bytes 2899976 | tf_op jit(solution)/shard_map/ppermute | solution.py:467
  24.9 29.8 %collective-permute-start.3 = (f32[118,16,128]{2,1,0:T(8,128)}, f32[118,16,128]{2,1,0:T(8,128)S(1)}, u32[]{:S(2)}, u32[]{:S(2)}) collective-permute-start(f32[118,16,128]{2,1,0:T(8,128)} %get-tuple-element.10), channel_id=1, source_target_pairs={{0,8},{8,16},{16,24},{1,9},{9,17},{17,25},{2,10},{10,18},{18,26},{... | collective-permute-start | bytes 2899976 | tf_op jit(solution)/shard_map/ppermute | solution.py:467
  29.8 24.9 %collective-permute-start.4 = (f32[118,16,128]{2,1,0:T(8,128)}, f32[118,16,128]{2,1,0:T(8,128)S(1)}, u32[]{:S(2)}, u32[]{:S(2)}) collective-permute-start(f32[118,16,128]{2,1,0:T(8,128)} %get-tuple-element.11), channel_id=1, source_target_pairs={{8,0},{16,8},{24,16},{9,1},{17,9},{25,17},{10,2},{18,10},{26,18},{... | collective-permute-start | bytes 2899976 | tf_op jit(solution)/shard_map/ppermute | solution.py:467
  47.0 11.4 %collective-permute-start.5 = (f32[944,128]{1,0:T(8,128)S(1)}, f32[944,128]{1,0:T(8,128)S(1)}, u32[]{:S(2)}, u32[]{:S(2)}) collective-permute-start(f32[944,128]{1,0:T(8,128)S(1)} %get-tuple-element.12), channel_id=1, source_target_pairs={{0,8},{8,16},{16,24},{1,9},{9,17},{17,25},{2,10},{10,18},{18,26},{... | collective-permute-start | bytes 1449992 | tf_op jit(solution)/shard_map/ppermute | solution.py:467
  52.7 10.1 %collective-permute-start.6 = (f32[944,128]{1,0:T(8,128)S(1)}, f32[944,128]{1,0:T(8,128)S(1)}, u32[]{:S(2)}, u32[]{:S(2)}) collective-permute-start(f32[944,128]{1,0:T(8,128)S(1)} %get-tuple-element.13), channel_id=1, source_target_pairs={{8,0},{16,8},{24,16},{9,1},{17,9},{25,17},{10,2},{18,10},{26,18},{... | collective-permute-start | bytes 1449992 | tf_op jit(solution)/shard_map/ppermute | solution.py:467
  54.7 8.1 %copy-start.6 = (f32[118,16,128]{2,1,0:T(8,128)}, f32[118,16,128]{2,1,0:T(8,128)S(1)}, u32[]{:S(2)}) copy-start(f32[118,16,128]{2,1,0:T(8,128)S(1)} %collective-permute-done.4.x_high) | copy-start | bytes 2899972

commit v3 on v2

--- a/solution.py
+++ b/solution.py
@@ -85,23 +85,6 @@
     return [(length - w, jnp.int32(depth - w)), (jnp.int32(0), length)]
 
 
-def for_channels(plan, arrays, held, sems, body, steps):
-    copies = fetch(arrays, held, sems)
-    flow, solute, density, velocity, level, solid = held
-    copies[0].wait()
-    body(0, NF, lambda i, x: flow[i, x])
-    for copy in copies[1:]:
-        copy.wait()
-    body(NF, NS, lambda i, x: solute[i, x])
-    body(SOLID, 1, lambda i, x: solid[x].astype(F32))
-    for s in steps:
-        t = plan.steps - 1 - s
-        at = AUX + NA * s
-        body(at, 1, lambda i, x, t=t: density[t, x].astype(F32))
-        body(at + 1, 1, lambda i, x, t=t: level[t, x].astype(F32))
-        body(at + 2, 3, lambda i, x, t=t: velocity[t, i, x].astype(F32))
-
-
 def each(number, body, unroll=4):
     def several(i, carry):
         for u in range(unroll):
@@ -124,105 +107,150 @@
     return copies
 
 
+def gather(plan, arrays, held, wide, sems, steps, body):
+    copies = fetch(arrays, held, sems)
+    flow, solute, density, velocity, level, solid = held
+    ny = plan.ny
+    copies[0].wait()
+    body(0, NF, flow)
+    for copy in copies[1:]:
+        copy.wait()
+    body(NF, NS, solute)
+    sources = [(solid, 0)]
+    for s in range(steps):
+        t = plan.steps - 1 - s
+        sources += [(density, t), (level, t), (velocity, 3 * t), (velocity, 3 * t + 1), (velocity, 3 * t + 2)]
+
+    for c, (ref, i) in enumerate(sources):
+        for x in range(plan.nx):
+            wide[c, x * ny : (x + 1) * ny, :] = ref[i, x * ny : (x + 1) * ny, :].astype(F32)
+    body(SOLID, len(sources), wide)
+
+
+def tiles_of(plan):
+    return [(y * (plan.nx // 8) + h, y, 8 * h) for y in range(plan.ny) for h in range(plan.nx // 8)]
+
+
 def pack_kernel(plan, ring, parts, *refs):
-    owner, arrays, outs, held, sems = refs[0], refs[1:7], refs[7 : 7 + parts], refs[7 + parts : 13 + parts], refs[-1]
-    w, depth = plan.halo, plan.depth
+    owner, arrays, outs, held, wide, sems = refs[0], refs[1:7], refs[7 : 7 + parts], refs[7 + parts : 13 + parts], refs[-2], refs[-1]
+    w, depth, ny = plan.halo, plan.depth, plan.ny
     length = occupied(owner)
     group = lanes(depth) // w
     places = z_places(plan, length, ring)
-    tall = plan.ny // 8
-    shifts = [[(w * n + depth - start) & (depth - 1) for n in range(plan.nx * tall)] for start, _ in places]
-
-    def body(at, number, read):
+    shifts = [{n: (w * n + depth - start) & (depth - 1) for n, _, _ in tiles_of(plan)} for start, _ in places]
+
+    def body(at, number, ref):
         def one(i):
             packed = [None] * parts
-            for x in range(plan.nx):
-                row = read(i, x)
-                for h in range(tall):
-                    n = x * tall + h
-                    for p in range(parts):
-                        moved = pltpu.roll(row[8 * h : 8 * h + 8], shifts[p][n], 1)
-                        packed[p] = moved if n == 0 else jnp.where(group == n, moved, packed[p])
+            for n, y, x in tiles_of(plan):
+                tile = ref[i, pl.ds(x * ny + y, 8, stride=ny), :]
+                for p in range(parts):
+                    moved = pltpu.roll(tile, shifts[p][n], 1)
+                    packed[p] = moved if n == 0 else jnp.where(group == n, moved, packed[p])
             for p in range(parts):
                 outs[p][at + i] = packed[p]
 
         each(number, one, 3)
 
-    for_channels(plan, arrays, held, sems, body, range(plan.steps - 1))
-
-
-def unpack(plan, ring, owner, arrays, held, sems, received, write, steps):
+    gather(plan, arrays, held, wide, sems, plan.steps - 1, body)
+
+
+def faces_kernel(plan, *refs):
+    arrays, (y_low, y_high), held, wide, sems = refs[:6], refs[7:9], refs[9:15], refs[15], refs[16]
+    w, nx, ny = plan.halo, plan.nx, plan.ny
+
+    def body(at, number, ref):
+        def row(c, y):
+            return ref[c, pl.ds(y, nx, stride=ny), :]
+
+        for k in range(1, w):
+
+            def one(c, k=k):
+                y_low[plan.base[k] + at + c] = row(c, k - 1)
+                y_high[plan.base[k] + at + c] = row(c, ny - k)
+
+            each(min(number, plan.count[k] - at), one)
+        for out, sign, y in ((y_low, 1, w - 1), (y_high, -1, ny - w)):
+            for j, c in enumerate(plan.last(1, sign)):
+                if at <= c < at + number:
+                    out[plan.base[w] + j] = row(c - at, y)
+
+    gather(plan, arrays, held, wide, sems, plan.steps - 1, body)
+
+
+def column(plan, ring, owner, received):
     w, depth = plan.halo, plan.depth
     length = occupied(owner)
     lane = lanes(depth)
     live = lane < length
-    places = z_places(plan, length, ring)
-    halos = [((lane - to) & (depth - 1)) < w for _, to in places]
-    tall = plan.ny // 8
-
-    def body(at, number, read):
-        def one(i):
-            slabs = []
-            if not isinstance(at, int) or at < plan.sent:
-                slabs = [pltpu.roll(r[at + i], to, 1) for r, (_, to) in zip(received, places)]
-            for x in range(plan.nx):
-                row = read(i, x)
-                for h in range(tall):
-                    tile = jnp.where(live, row[8 * h : 8 * h + 8], 0.0)
-                    back = (depth - w * (x * tall + h)) % depth
-                    for slab, halo in zip(slabs, halos):
-                        tile = jnp.where(halo, pltpu.roll(slab, back, 1) if back else slab, tile)
-                    write(at + i, x, h, tile)
-
-        each(number, one, 3)
-
-    for_channels(plan, arrays, held, sems, body, steps)
-
-
-def faces_kernel(plan, ring, parts, *refs):
-    owner, arrays, received, rest = refs[0], refs[1:7], refs[7 : 7 + parts], refs[7 + parts :]
-    (y_low, y_high, x_low, x_high, cells), held, sems = rest[:5], rest[5:11], rest[11]
-    w, nx, ny = plan.halo, plan.nx, plan.ny
-
-    def write(c, x, h, tile):
-        cells[c, x * ny + 8 * h : x * ny + 8 * h + 8, :] = tile
-
-    unpack(plan, ring, owner, arrays, held, sems, received, write, range(plan.steps - 1))
-
-    def y_row(c, y):
-        return cells[c, pl.ds(y, nx, stride=ny), :]
-
-    def x_row(c, x):
-        return cells[c, x * ny : (x + 1) * ny, :]
+    places = [to for _, to in z_places(plan, length, ring)]
+    halos = [((lane - to) & (depth - 1)) < w for to in places]
+    shifts = [{n: (to + depth - w * n) & (depth - 1) for n, _, _ in tiles_of(plan)} for to in places]
+
+    def put(tile, slabs, n):
+        tile = jnp.where(live, tile, 0.0)
+        for slab, halo, shift in zip(slabs, halos, shifts):
+            tile = jnp.where(halo, pltpu.roll(slab, shift[n], 1), tile)
+        return tile
+
+    return put
+
+
+def insert_kernel(plan, ring, parts, owner, low, high, *rest):
+    received, (y_low, y_high) = rest[:parts], rest[parts:]
+    put = column(plan, ring, owner, received)
+    w, ny = plan.halo, plan.ny
+    tall = plan.nx // 8
+
+    def one(raw, out, j, c, y):
+        slabs = [r[c] for r in received]
+        for h in range(tall):
+            out[j, 8 * h : 8 * h + 8, :] = put(raw[j, 8 * h : 8 * h + 8, :], slabs, y * tall + h)
 
     for k in range(1, w):
-        base = plan.base[k]
-
-        def one(c, base=base, k=k):
-            y_low[base + c] = y_row(c, k - 1)
-            y_high[base + c] = y_row(c, ny - k)
-            x_low[base + c] = x_row(c, k - 1)
-            x_high[base + c] = x_row(c, nx - k)
-
-        each(plan.count[k], one)
-    for j in range(7):
-        at = plan.base[w] + j
-        y_low[at] = y_row(plan.last(1, 1)[j], w - 1)
-        y_high[at] = y_row(plan.last(1, -1)[j], ny - w)
-        x_low[at] = x_row(plan.last(0, 1)[j], w - 1)
-        x_high[at] = x_row(plan.last(0, -1)[j], nx - w)
+
+        def both(c, k=k):
+            one(low, y_low, plan.base[k] + c, c, k - 1)
+            one(high, y_high, plan.base[k] + c, c, ny - k)
+
+        each(plan.count[k], both)
+    for raw, out, sign, y in ((low, y_low, 1, w - 1), (high, y_high, -1, ny - w)):
+        for j, c in enumerate(plan.last(1, sign)):
+            one(raw, out, plan.base[w] + j, c, y)
 
 
 def inner_kernel(plan, ring, parts, *refs):
     owner, arrays, received, rest = refs[0], refs[1:7], refs[7 : 7 + parts], refs[7 + parts :]
-    out, held, sems = rest[0], rest[1:7], rest[7]
-    w, pitch = plan.halo, plan.pitch
-
-    def write(c, x, h, tile):
-        row = x * pitch + w + 8 * h
-        out[c, row : row + 8, :] = tile
-
-    unpack(plan, ring, owner, arrays, held, sems, received, write, range(plan.steps))
+    (out, x_low, x_high), held, wide, sems = rest[:3], rest[3:9], rest[9], rest[10]
+    w, nx, ny, pitch = plan.halo, plan.nx, plan.ny, plan.pitch
+    put = column(plan, ring, owner, received)
+
+    def body(at, number, ref):
+        def one(i, sent=True):
+            slabs = [r[at + i] for r in received] if sent else []
+            for n, y, x in tiles_of(plan):
+                tile = ref[i, pl.ds(x * ny + y, 8, stride=ny), :]
+                out[at + i, pl.ds(x * pitch + w + y, 8, stride=pitch), :] = put(tile, slabs, n)
+
+        within = min(number, plan.sent - at)
+        each(within, one, 3)
+        each(number - within, lambda i: one(within + i, False), 1)
+
+    gather(plan, arrays, held, wide, sems, plan.steps, body)
+
+    def row(c, x):
+        return out[c, x * pitch + w : x * pitch + w + ny, :]
+
+    for k in range(1, w):
+
+        def both(c, k=k):
+            x_low[plan.base[k] + c] = row(c, k - 1)
+            x_high[plan.base[k] + c] = row(c, nx - k)
+
+        each(plan.count[k], both)
+    for slab, sign, x in ((x_low, 1, w - 1), (x_high, -1, nx - w)):
+        for j, c in enumerate(plan.last(0, sign)):
+            slab[plan.base[w] + j] = row(c, x)
 
 
 def corners_kernel(plan, from_low, from_high, inner, low, high):
@@ -460,22 +488,26 @@
     plan = Plan(steps, nx, ny, depth)
     ring = lax.axis_size("gz")
     w = plan.halo
-    fields = (flow_adjoint, solute_adjoint, flow_density, flow_velocity, solute_level, solid)
+    arguments = (flow_adjoint, solute_adjoint, flow_density, flow_velocity, solute_level, solid)
+    fields = [f.reshape(-1, nx * ny, depth) for f in arguments]
 
     def move(value, axis, by):
         size = lax.axis_size(axis)
         return lax.ppermute(value, axis, [(i, i + by) for i in range(size) if 0 <= i + by < size])
 
+    def scratch(steps):
+        held = [pltpu.VMEM(f.shape, f.dtype) for f in fields]
+        wide = pltpu.VMEM((AUX - SOLID + NA * steps, nx * ny, depth), F32)
+        return held + [wide, pltpu.SemaphoreType.DMA((len(fields),))]
+
     parts = 1 if ring == 2 else 2
-    packed_shape = jax.ShapeDtypeStruct((plan.sent, 8, depth), F32)
-    held = [pltpu.VMEM(f.shape, f.dtype) for f in fields] + [pltpu.SemaphoreType.DMA((len(fields),))]
     packed = call(
         functools.partial(pack_kernel, plan, ring, parts),
         [SMEM] + [ANY] * 6,
-        [packed_shape] * parts,
+        [jax.ShapeDtypeStruct((plan.sent, 8, depth), F32)] * parts,
         "pack_column",
         1 << 22,
-        held,
+        scratch(steps - 1),
         60 << 20,
     )(owner, *fields)
     if ring == 2:
@@ -483,29 +515,25 @@
     else:
         received = [move(packed[0], "gz", 1), move(packed[1], "gz", -1)]
 
-    def slab(rows):
-        return jax.ShapeDtypeStruct((plan.slab, rows, depth), F32)
-
-    y_low, y_high, x_low, x_high = call(
-        functools.partial(faces_kernel, plan, ring, parts),
-        [SMEM] + [ANY] * 6 + [VMEM] * parts,
-        [slab(nx), slab(nx), slab(ny), slab(ny)],
-        "faces",
-        1 << 22,
-        [pltpu.VMEM((plan.sent, nx * ny, depth), F32)] + held,
-    )(owner, *fields, *received)
+    slab = [jax.ShapeDtypeStruct((plan.slab, nx, depth), F32)] * 2
+    raw = call(functools.partial(faces_kernel, plan), [ANY] * 7, slab, "faces", 1 << 24, scratch(steps - 1), 24 << 20)(
+        *fields, packed[0]
+    )
+    y_low, y_high = call(
+        functools.partial(insert_kernel, plan, ring, parts), [SMEM] + [VMEM] * (2 + parts), slab, "insert", 1 << 22, (), 24 << 20
+    )(owner, *raw, *received)
     from_y_low = move(y_high, "gy", 1)
     from_y_high = move(y_low, "gy", -1)
+    inner, x_low, x_high = call(
+        functools.partial(inner_kernel, plan, ring, parts),
+        [SMEM] + [ANY] * 6 + [VMEM] * parts,
+        [jax.ShapeDtypeStruct((plan.chan, nx * plan.pitch, depth), F32)] + [jax.ShapeDtypeStruct((plan.slab, ny, depth), F32)] * 2,
+        "inner",
+        1 << 24,
+        scratch(steps),
+    )(owner, *fields, *received)
     from_x_low = move(x_high, "gx", 1)
     from_x_high = move(x_low, "gx", -1)
-    inner = call(
-        functools.partial(inner_kernel, plan, ring, parts),
-        [SMEM] + [ANY] * 6 + [VMEM] * parts,
-        [jax.ShapeDtypeStruct((plan.chan, nx * plan.pitch, depth), F32)],
-        "inner",
-        1 << 24,
-        held,
-    )(owner, *fields, *received)[0]
 
     def rows(value):
         return value.reshape(-1, depth)

time: 83.4 us -> 79.4 us (0.952)
  waiting for transfers between devices: 17.9 us -> 13.5 us
  local copies, waits for them, and re-layouts: 0.03 us -> 2.08 us
  Pallas kernels: 43.3 us -> 41.7 us
    ppermute x1, waiting for transfers between devices: 4.31 us -> 0.55 us  [per_device(): received = [lax.ppermute(packed[0], 'gz', [(0, 1), (1, 0)])]]
    pallas_call x1 -> x2, Pallas kernels: 8.17 us -> 4.68 us  [the longest x1 3.02 us: per_device(): call(functools.partial(insert_kernel, plan, ring, parts), [SMEM] + [VMEM]...]
    unnamed x14 -> x20, local copies, waits for them, and re-layouts: 0.03 us -> 2.08 us
    pallas_call x1, Pallas kernels: 5.08 us -> 6.27 us  [per_device(): call(functools.partial(pack_kernel, plan, ring, parts), [SMEM] + [ANY] *...]
  transfers between devices with their start and end apart: 7 -> 7, of which waited for: 5 -> 6; matrix products, arithmetic and copies ran while one was open for 0% -> 0% of each run, Pallas kernels for 12% -> 15%
where the time goes in v3:
time: 79.4 us; the launch traced here: 79.1 us
  Pallas kernels  41.7 us (53%)
  starting transfers between devices  21 us (26%)
  waiting for transfers between devices  13.5 us (17%)
  local copies, waits for them, and re-layouts  2.08 us (3%)
  between operations  0.8 us (1%)
    pallas_call x1, Pallas kernels, per_device(): call(functools.partial(steps_kernel, plan), [SMEM, ANY] + [VMEM] * 6, [ja...  20.3 us
    ppermute x6, starting transfers between devices, move(): lax.ppermute(value, axis, [(i, i + by) for i in range(size) if 0 <= i + b...  18.9 us
    ppermute x6, waiting for transfers between devices, move(): lax.ppermute(value, axis, [(i, i + by) for i in range(size) if 0 <= i + b...  13 us
    pallas_call x1, Pallas kernels, per_device(): call(functools.partial(inner_kernel, plan, ring, parts), [SMEM] + [ANY] *...  10 us
    pallas_call x1, Pallas kernels, per_device(): call(functools.partial(pack_kernel, plan, ring, parts), [SMEM] + [ANY] *...  6.27 us
    pallas_call x1, Pallas kernels, per_device(): call(functools.partial(insert_kernel, plan, ring, parts), [SMEM] + [VMEM]...  3.02 us
    ppermute x1, starting transfers between devices, per_device(): received = [lax.ppermute(packed[0], 'gz', [(0, 1), (1, 0)])]  2.13 us
    unnamed x20, local copies, waits for them, and re-layouts  2.08 us
  transfers between devices with their start and end apart: 7, of which 6 were waited for; matrix products, arithmetic and copies ran while one was open for 0% of the time, Pallas kernels for 15%

profile of v3, /device:TPU:1, one launch (start us, length us, event | category | flops | bytes accessed | tf_op | source)
XLA Modules:
  0.0 79.1 jit_solution(10986676474268197305)
XLA Ops:
  0.6 0.0 copy-start
  0.6 0.0 copy-start.1
  0.7 0.0 copy-start.4
  0.7 0.0 copy-start.5
  0.7 0.0 copy-start.6
  0.7 6.3 %pack_column.1.refs_6_ = f32[42,8,128]{2,1,0:T(8,128)} custom-call(s32[8]{0:T(128)} %owner.3, f32[19,256,128]{2,1,0:T(8,128)} %bitcast.10, f32[7,256,128]{2,1,0:T(8,128)} %bitcast.13, bf16[4,256,128]{2,1,0:T(8,128)(2,1)} %bitcast.21, bf16[12,256,128]{2,1,0:T(8,128)(2,1)} %bitcast.16, bf16[4,256,128]{2,1,0:T(8,128)(2,1)} %bitcast.24, s32[1,256,128]{2,1,0:T(8,128)} %bitcast.27), custom_call_target="tpu_custom_call" | custom-call | flops 4194304 | bytes 8388608 | tf_op jit(solution)/shard_map/pack_column/pallas_call | solution.py:504
  7.0 2.1 %collective-permute-start = (f32[42,8,128]{2,1,0:T(8,128)}, f32[42,8,128]{2,1,0:T(8,128)S(1)}, u32[]{:S(2)}, u32[]{:S(2)}) collective-permute-start(f32[42,8,128]{2,1,0:T(8,128)} %pack_column.1.refs_6_), channel_id=1, source_target_pairs={{0,1},{1,0},{2,3},{3,2},{4,5},{5,4},{6,7},{7,6},{8,9},{9,8},{10,11... | collective-permute-start | bytes 516104 | tf_op jit(solution)/shard_map/ppermute | solution.py:514
  9.1 0.0 copy-done
  9.1 0.0 copy-done.6
  9.1 0.0 copy-start.2
  9.1 1.1 %copy-done.2 = bf16[4,3,16,16,128]{4,3,2,1,0:T(8,128)(2,1)S(1)} copy-done((bf16[4,3,16,16,128]{4,3,2,1,0:T(8,128)(2,1)S(1)}, bf16[4,3,16,16,128]{4,3,2,1,0:T(8,128)(2,1)}, u32[]{:S(2)}) %copy-start.2) | copy-done | bytes 786456
  10.3 0.9 %copy-done.7 = f32[42,8,128]{2,1,0:T(8,128)S(1)} copy-done((f32[42,8,128]{2,1,0:T(8,128)S(1)}, f32[42,8,128]{2,1,0:T(8,128)}, u32[]{:S(2)}) %copy-start.7) | copy-done | bytes 172056
  11.2 1.7 %faces.1 = (f32[118,16,128]{2,1,0:T(8,128)S(1)}, f32[118,16,128]{2,1,0:T(8,128)S(1)}) custom-call(f32[19,256,128]{2,1,0:T(8,128)S(1)} %bitcast.12, f32[7,256,128]{2,1,0:T(8,128)S(1)} %bitcast.14, bf16[4,256,128]{2,1,0:T(8,128)(2,1)S(1)} %bitcast.22, bf16[12,256,128]{2,1,0:T(8,128)(2,1)S(1)} %bitcast.17, bf16[4,256,128]{2,1,0:T(8,128)(2,1)S(1)} %bitcast.25, ...), custom_call_target="tpu_custom_call" | custom-call | flops 16777216 | bytes 8388608 | tf_op jit(solution)/shard_map/faces/pallas_call | solution.py:519
  12.8 0.6 collective-permute-done.refs_7_.rest_0_
  13.4 0.0 copy-done.8
  13.4 3.0 %insert.1 = (f32[118,16,128]{2,1,0:T(8,128)S(1)}, f32[118,16,128]{2,1,0:T(8,128)S(1)}) custom-call(s32[8]{0:T(128)S(1)} %copy-done.8, f32[118,16,128]{2,1,0:T(8,128)S(1)} %get-tuple-element.12.low, f32[118,16,128]{2,1,0:T(8,128)S(1)} %get-tuple-element.13.high, f32[42,8,128]{2,1,0:T(8,128)S(1)} %collective-permute-done.refs_7_.rest_0_), custom_call_target="tpu_custom_call" | custom-call | flops 4194304 | bytes 8388608 | tf_op jit(solution)/shard_map/insert/pallas_call | solution.py:522
  16.4 3.2 %collective-permute-start.1 = (f32[118,16,128]{2,1,0:T(8,128)S(1)}, f32[118,16,128]{2,1,0:T(8,128)S(1)}, u32[]{:S(2)}, u32[]{:S(2)}) collective-permute-start(f32[118,16,128]{2,1,0:T(8,128)S(1)} %get-tuple-element.14), channel_id=1, source_target_pairs={{0,2},{2,4},{4,6},{1,3},{3,5},{5,7},{8,10},{10,12},{12,14},{9,11},... | collective-permute-start | bytes 2899976 | tf_op jit(solution)/shard_map/ppermute | solution.py:496
  19.6 1.3 %collective-permute-start.2 = (f32[118,16,128]{2,1,0:T(8,128)S(1)}, f32[118,16,128]{2,1,0:T(8,128)S(1)}, u32[]{:S(2)}, u32[]{:S(2)}) collective-permute-start(f32[118,16,128]{2,1,0:T(8,128)S(1)} %get-tuple-element.15), channel_id=1, source_target_pairs={{2,0},{4,2},{6,4},{3,1},{5,3},{7,5},{10,8},{12,10},{14,12},{11,9},... | collective-permute-start | bytes 2899976 | tf_op jit(solution)/shard_map/ppermute | solution.py:496
  20.9 10.0 %inner.1 = (f32[47,384,128]{2,1,0:T(8,128)}, f32[118,16,128]{2,1,0:T(8,128)S(1)}, f32[118,16,128]{2,1,0:T(8,128)}) custom-call(s32[8]{0:T(128)S(1)} %copy-done.8, f32[19,256,128]{2,1,0:T(8,128)} %bitcast.11, f32[7,256,128]{2,1,0:T(8,128)S(1)} %bitcast.15, bf16[4,256,128]{2,1,0:T(8,128)(2,1)S(1)} %bitcast.23, bf16[12,256,128]{2,1,0:T(8,128)(2,1)S(1)} %bitcast.18, ...), custom_call_target="tpu_custom_call" | custom-call | flops 16777216 | bytes 8388608 | tf_op jit(solution)/shard_map/inner/pallas_call | solution.py:527
  31.0 4.8 %collective-permute-start.3 = (f32[118,16,128]{2,1,0:T(8,128)}, f32[118,16,128]{2,1,0:T(8,128)S(1)}, u32[]{:S(2)}, u32[]{:S(2)}) collective-permute-start(f32[118,16,128]{2,1,0:T(8,128)} %get-tuple-element.16), channel_id=1, source_target_pairs={{0,8},{8,16},{16,24},{1,9},{9,17},{17,25},{2,10},{10,18},{18,26},{... | collective-permute-start | bytes 2899976 | tf_op jit(solution)/shard_map/ppermute | solution.py:496
  35.8 1.9 %collective-permute-start.4 = (f32[118,16,128]{2,1,0:T(8,128)S(1)}, f32[118,16,128]{2,1,0:T(8,128)S(1)}, u32[]{:S(2)}, u32[]{:S(2)}) collective-permute-start(f32[118,16,128]{2,1,0:T(8,128)S(1)} %get-tuple-element.17), channel_id=1, source_target_pairs={{8,0},{16,8},{24,16},{9,1},{17,9},{25,17},{10,2},{18,10},{26,18},{... | collective-permute-start | bytes 2899976 | tf_op jit(solution)/shard_map/ppermute | solution.py:496
  37.7 0.9 %collective-permute-done.1.y_low = f32[118,16,128]{2,1,0:T(8,128)S(1)} collective-permute-done((f32[118,16,128]{2,1,0:T(8,128)S(1)}, f32[118,16,128]{2,1,0:T(8,128)S(1)}, u32[]{:S(2)}, u32[]{:S(2)}) %collective-permute-start.1) | collective-permute-done | bytes 966688 | tf_op jit(solution)/shard_map/ppermute | solution.py:496
  38.7 3.9 %collective-permute-done.2.y_high = f32[118,16,128]{2,1,0:T(8,128)S(1)} collective-permute-done((f32[118,16,128]{2,1,0:T(8,128)S(1)}, f32[118,16,128]{2,1,0:T(8,128)S(1)}, u32[]{:S(2)}, u32[]{:S(2)}) %collective-permute-start.2) | collective-permute-done | bytes 966688 | tf_op jit(solution)/shard_map/ppermute | solution.py:496
  42.6 0.4 corners.1
  43.0 5.8 %collective-permute-start.5 = (f32[944,128]{1,0:T(8,128)S(1)}, f32[944,128]{1,0:T(8,128)S(1)}, u32[]{:S(2)}, u32[]{:S(2)}) collective-permute-start(f32[944,128]{1,0:T(8,128)S(1)} %get-tuple-element.18), channel_id=1, source_target_pairs={{0,8},{8,16},{16,24},{1,9},{9,17},{17,25},{2,10},{10,18},{18,26},{... | collective-permute-start | bytes 1449992 | tf_op jit(solution)/shard_map/ppermute | solution.py:496
  48.7 1.9 %collective-permute-start.6 = (f32[944,128]{1,0:T(8,128)S(1)}, f32[944,128]{1,0:T(8,128)S(1)}, u32[]{:S(2)}, u32[]{:S(2)}) collective-permute-start(f32[944,128]{1,0:T(8,128)S(1)} %get-tuple-element.19), channel_id=1, source_target_pairs={{8,0},{16,8},{24,16},{9,1},{17,9},{25,17},{10,2},{18,10},{26,18},{... | collective-permute-start | bytes 1449992 | tf_op jit(solution)/shard_map/ppermute | solution.py:496
  50.7 0.0 collective-permute-done.3.x_low
  50.7 0.4 collective-permute-done.4.x_high
  51.1 3.4 %collective-permute-done.5 = f32[944,128]{1,0:T(8,128)S(1)} collective-permute-done((f32[944,128]{1,0:T(8,128)S(1)}, f32[944,128]{1,0:T(8,128)S(1)}, u32[]{:S(2)}, u32[]{:S(2)}) %collective-permute-start.5) | collective-permute-done | bytes 483360 | tf_op jit(solution)/shard_map/ppermute | solution.py:496
  54.4 4.4 %collective-permute-done.6 = f32[944,128]{1,0:T(8,128)S(1)} collective-permute-done((f32[944,128]{1,0:T(8,128)S(1)}, f32[944,128]{1,0:T(8,128)S(1)}, u32[]{:S(2)}, u32[]{:S(2)}) %collective-permute-start.6) | collective-permute-done | bytes 483360 | tf_op jit(solution)/shard_map/ppermute | solution.py:496
  58.8 0.0 copy-done.9
  58.8 20.3 %steps.1 = (f32[19,16,16,128]{3,2,1,0:T(8,128)}, f32[7,16,16,128]{3,2,1,0:T(8,128)}) custom-call(s32[8]{0:T(128)S(1)} %copy-done.8, f32[47,384,128]{2,1,0:T(8,128)} %get-tuple-element.11.inner, f32[118,16,128]{2,1,0:T(8,128)S(1)} %collective-permute-done.1.y_low, f32[118,16,128]{2,1,0:T(8,128)S(1)} %collective-permute-done.2.y_high, ...), custom_call_target="tpu_custom_call" | custom-call | flops 268435456 | bytes 8388608 | tf_op jit(solution)/shard_map/steps/pallas_call | solution.py:549
  (8 shorter events, 0.0 us)
Async XLA Ops:
  0.6 8.5 %copy-start = (f32[19,16,16,128]{3,2,1,0:T(8,128)S(1)}, f32[19,16,16,128]{3,2,1,0:T(8,128)}, u32[]{:S(2)}) copy-start(f32[19,16,16,128]{3,2,1,0:T(8,128)} %param.7) | copy-start | bytes 7471108
  0.6 8.5 %copy-start.1 = (f32[7,16,16,128]{3,2,1,0:T(8,128)S(1)}, f32[7,16,16,128]{3,2,1,0:T(8,128)}, u32[]{:S(2)}) copy-start(f32[7,16,16,128]{3,2,1,0:T(8,128)} %param.8) | copy-start | bytes 2752516
  0.7 8.4 %copy-start.4 = (bf16[4,16,16,128]{3,2,1,0:T(8,128)(2,1)S(1)}, bf16[4,16,16,128]{3,2,1,0:T(8,128)(2,1)}, u32[]{:S(2)}) copy-start(bf16[4,16,16,128]{3,2,1,0:T(8,128)(2,1)} %param.9) | copy-start | bytes 786436
  0.7 8.4 %copy-start.5 = (bf16[4,16,16,128]{3,2,1,0:T(8,128)(2,1)S(1)}, bf16[4,16,16,128]{3,2,1,0:T(8,128)(2,1)}, u32[]{:S(2)}) copy-start(bf16[4,16,16,128]{3,2,1,0:T(8,128)(2,1)} %param.11) | copy-start | bytes 786436
  0.7 8.4 %copy-start.6 = (s32[16,16,128]{2,1,0:T(8,128)S(1)}, s32[16,16,128]{2,1,0:T(8,128)}, u32[]{:S(2)}) copy-start(s32[16,16,128]{2,1,0:T(8,128)} %param.12) | copy-start | bytes 393220
  7.0 6.4 %collective-permute-start = (f32[42,8,128]{2,1,0:T(8,128)}, f32[42,8,128]{2,1,0:T(8,128)S(1)}, u32[]{:S(2)}, u32[]{:S(2)}) collective-permute-start(f32[42,8,128]{2,1,0:T(8,128)} %pack_column.1.refs_6_), channel_id=1, source_target_pairs={{0,1},{1,0},{2,3},{3,2},{4,5},{5,4},{6,7},{7,6},{8,9},{9,8},{10,11... | collective-permute-start | bytes 516104 | tf_op jit(solution)/shard_map/ppermute | solution.py:514
  9.1 1.1 %copy-start.2 = (bf16[4,3,16,16,128]{4,3,2,1,0:T(8,128)(2,1)S(1)}, bf16[4,3,16,16,128]{4,3,2,1,0:T(8,128)(2,1)}, u32[]{:S(2)}) copy-start(bf16[4,3,16,16,128]{4,3,2,1,0:T(8,128)(2,1)} %param.10) | copy-start | bytes 2359300
  10.3 0.9 %copy-start.7 = (f32[42,8,128]{2,1,0:T(8,128)S(1)}, f32[42,8,128]{2,1,0:T(8,128)}, u32[]{:S(2)}) copy-start(f32[42,8,128]{2,1,0:T(8,128)} %pack_column.1.refs_6_) | copy-start | bytes 516100
  11.2 2.2 %copy-start.8 = (s32[8]{0:T(128)S(1)}, s32[8]{0:T(128)}, u32[]{:S(2)}) copy-start(s32[8]{0:T(128)} %owner.3) | copy-start | bytes 100
  11.2 9.7 %copy-start.3 = (bf16[4,3,16,16,128]{4,3,2,1,0:T(8,128)(2,1)S(1)}, bf16[4,3,16,16,128]{4,3,2,1,0:T(8,128)(2,1)}, u32[]{:S(2)}) copy-start(bf16[4,3,16,16,128]{4,3,2,1,0:T(8,128)(2,1)} %param.10) | copy-start | bytes 2359300
  16.4 22.2 %collective-permute-start.1 = (f32[118,16,128]{2,1,0:T(8,128)S(1)}, f32[118,16,128]{2,1,0:T(8,128)S(1)}, u32[]{:S(2)}, u32[]{:S(2)}) collective-permute-start(f32[118,16,128]{2,1,0:T(8,128)S(1)} %get-tuple-element.14), channel_id=1, source_target_pairs={{0,2},{2,4},{4,6},{1,3},{3,5},{5,7},{8,10},{10,12},{12,14},{9,11},... | collective-permute-start | bytes 2899976 | tf_op jit(solution)/shard_map/ppermute | solution.py:496
  19.6 23.0 %collective-permute-start.2 = (f32[118,16,128]{2,1,0:T(8,128)S(1)}, f32[118,16,128]{2,1,0:T(8,128)S(1)}, u32[]{:S(2)}, u32[]{:S(2)}) collective-permute-start(f32[118,16,128]{2,1,0:T(8,128)S(1)} %get-tuple-element.15), channel_id=1, source_target_pairs={{2,0},{4,2},{6,4},{3,1},{5,3},{7,5},{10,8},{12,10},{14,12},{11,9},... | collective-permute-start | bytes 2899976 | tf_op jit(solution)/shard_map/ppermute | solution.py:496
  31.0 19.7 %collective-permute-start.3 = (f32[118,16,128]{2,1,0:T(8,128)}, f32[118,16,128]{2,1,0:T(8,128)S(1)}, u32[]{:S(2)}, u32[]{:S(2)}) collective-permute-start(f32[118,16,128]{2,1,0:T(8,128)} %get-tuple-element.16), channel_id=1, source_target_pairs={{0,8},{8,16},{16,24},{1,9},{9,17},{17,25},{2,10},{10,18},{18,26},{... | collective-permute-start | bytes 2899976 | tf_op jit(solution)/shard_map/ppermute | solution.py:496
  35.8 15.2 %collective-permute-start.4 = (f32[118,16,128]{2,1,0:T(8,128)S(1)}, f32[118,16,128]{2,1,0:T(8,128)S(1)}, u32[]{:S(2)}, u32[]{:S(2)}) collective-permute-start(f32[118,16,128]{2,1,0:T(8,128)S(1)} %get-tuple-element.17), channel_id=1, source_target_pairs={{8,0},{16,8},{24,16},{9,1},{17,9},{25,17},{10,2},{18,10},{26,18},{... | collective-permute-start | bytes 2899976 | tf_op jit(solution)/shard_map/ppermute | solution.py:496
  43.0 11.4 %collective-permute-start.5 = (f32[944,128]{1,0:T(8,128)S(1)}, f32[944,128]{1,0:T(8,128)S(1)}, u32[]{:S(2)}, u32[]{:S(2)}) collective-permute-start(f32[944,128]{1,0:T(8,128)S(1)} %get-tuple-element.18), channel_id=1, source_target_pairs={{0,8},{8,16},{16,24},{1,9},{9,17},{17,25},{2,10},{10,18},{18,26},{... | collective-permute-start | bytes 1449992 | tf_op jit(solution)/shard_map/ppermute | solution.py:496
  48.7 10.1 %collective-permute-start.6 = (f32[944,128]{1,0:T(8,128)S(1)}, f32[944,128]{1,0:T(8,128)S(1)}, u32[]{:S(2)}, u32[]{:S(2)}) collective-permute-start(f32[944,128]{1,0:T(8,128)S(1)} %get-tuple-element.19), channel_id=1, source_target_pairs={{8,0},{16,8},{24,16},{9,1},{17,9},{25,17},{10,2},{18,10},{26,18},{... | collective-permute-start | bytes 1449992 | tf_op jit(solution)/shard_map/ppermute | solution.py:496
  51.1 7.8 %copy-start.9 = (f32[118,16,128]{2,1,0:T(8,128)}, f32[118,16,128]{2,1,0:T(8,128)S(1)}, u32[]{:S(2)}) copy-start(f32[118,16,128]{2,1,0:T(8,128)S(1)} %collective-permute-done.4.x_high) | copy-start | bytes 2899972

commit v4 on v3

--- a/solution.py
+++ b/solution.py
@@ -39,7 +39,7 @@
 flow_omega = 1.25
 solute_omega = 1.6
 langmuir_rate = 0.05
-VMEM_LIMIT = 50 * 1024 * 1024
+VMEM_LIMIT = 24 << 20
 F32 = jnp.float32
 
 
@@ -213,7 +213,7 @@
             one(low, y_low, plan.base[k] + c, c, k - 1)
             one(high, y_high, plan.base[k] + c, c, ny - k)
 
-        each(plan.count[k], both)
+        each(plan.count[k], both, 10)
     for raw, out, sign, y in ((low, y_low, 1, w - 1), (high, y_high, -1, ny - w)):
         for j, c in enumerate(plan.last(1, sign)):
             one(raw, out, plan.base[w] + j, c, y)
@@ -282,8 +282,30 @@
 PAD = 8
 
 
-def steps_kernel(plan, owner, inner, y_low, y_high, x_low, x_high, c_low, c_high, flow_out, solute_out, cells, other, fields, masks, sems):
-    w, nx, ny, depth, pitch = plan.halo, plan.nx, plan.ny, plan.depth, plan.pitch
+def channels(cells, fields, number, body):
+    each(SOLID, lambda c: body(cells, c, c))
+    each(number - SOLID, lambda c: body(fields, c, SOLID + c))
+
+
+def insert_layers(plan, cells, fields, axis, parts, put):
+    w = plan.halo
+    for k in range(1, w + 1):
+        for part, sign in zip(parts, (-1, 1)):
+            if k < w:
+                channels(
+                    cells,
+                    fields,
+                    plan.count[k],
+                    lambda ref, c, j, k=k, part=part, sign=sign: put(ref, c, part, plan.base[k] + j, k, sign),
+                )
+                continue
+            for j, c in enumerate(plan.last(axis, sign)):
+                ref, at = (cells, c) if c < SOLID else (fields, c - SOLID)
+                put(ref, at, part, plan.base[w] + j, k, sign)
+
+
+def first_kernel(plan, owner, inner, y_low, y_high, x_low, x_high, cells, fields, other, masks, sems):
+    w, nx, ny, pitch = plan.halo, plan.nx, plan.ny, plan.pitch
     middle = pl.ds(PAD + w * pitch, nx * pitch)
     copies = [
         pltpu.make_async_copy(inner.at[pl.ds(0, SOLID)], cells.at[:, middle, :], sems.at[0]),
@@ -292,42 +314,60 @@
     for copy in copies:
         copy.start()
 
-    def channels(number, body):
-        each(SOLID, lambda c: body(cells, c, c))
-        each(number - SOLID, lambda c: body(fields, c, SOLID + c))
-
-    def channel(c):
-        return (cells, c) if c < SOLID else (fields, c - SOLID)
-
-    for k in range(1, w + 1):
-        for x_part, c_part, x, sign in ((x_low, c_low, w - k, -1), (x_high, c_high, w + nx - 1 + k, 1)):
-            row = PAD + x * pitch
-
-            def one(ref, c, j, row=row, x_part=x_part, c_part=c_part):
-                ref[c, row : row + w, :] = c_part[j, 0:w, :]
-                ref[c, row + w : row + w + ny, :] = x_part[j]
-                ref[c, row + w + ny : row + w + ny + w, :] = c_part[j, w : 2 * w, :]
-
-            if k < w:
-                channels(plan.count[k], lambda ref, c, j, one=one, k=k: one(ref, c, plan.base[k] + j))
-            else:
-                for j, c in enumerate(plan.last(0, sign)):
-                    one(*channel(c), plan.base[w] + j)
+    def put_x(ref, c, part, j, k, sign):
+        row = PAD + (w - k if sign < 0 else w + nx - 1 + k) * pitch + w
+        ref[c, row : row + ny, :] = part[j]
+
+    insert_layers(plan, cells, fields, 0, (x_low, x_high), put_x)
     for copy in copies:
         copy.wait()
-    for m in range(1, w + 1):
-        for part, y, sign in ((y_low, w - m, -1), (y_high, w + ny - 1 + m, 1)):
-            row = PAD + w * pitch + y
-
-            def one(ref, c, j, row=row, part=part):
-                ref[c, pl.ds(row, nx, stride=pitch), :] = part[j]
-
-            if m < w:
-                channels(plan.count[m], lambda ref, c, j, one=one, m=m: one(ref, c, plan.base[m] + j))
-            else:
-                for j, c in enumerate(plan.last(1, sign)):
-                    one(*channel(c), plan.base[w] + j)
-
+
+    def put_y(ref, c, part, j, m, sign):
+        row = PAD + w * pitch + (w - m if sign < 0 else w + ny - 1 + m)
+        ref[c, pl.ds(row, nx, stride=pitch), :] = part[j]
+
+    insert_layers(plan, cells, fields, 1, (y_low, y_high), put_y)
+    prepare(plan, owner, fields, masks, w, w + nx)
+    sweep(plan, owner, cells, other, fields, masks, 0, w + 1, w + nx - 1)
+
+
+def steps_kernel(plan, owner, cells, fields, other, masks, c_low, c_high, flow_out, solute_out):
+    w, nx, ny, pitch = plan.halo, plan.nx, plan.ny, plan.pitch
+
+    def put(ref, c, part, j, k, sign):
+        row = PAD + (w - k if sign < 0 else w + nx - 1 + k) * pitch
+        ref[c, row : row + w, :] = part[j, 0:w, :]
+        ref[c, row + w + ny : row + w + ny + w, :] = part[j, w : 2 * w, :]
+
+    insert_layers(plan, cells, fields, 0, (c_low, c_high), put)
+    prepare(plan, owner, fields, masks, 0, w)
+    prepare(plan, owner, fields, masks, w + nx, plan.wide)
+    sweep(plan, owner, cells, other, fields, masks, 0, 1, w + 1)
+    sweep(plan, owner, cells, other, fields, masks, 0, w + nx - 1, plan.wide - 1)
+    buffers = [cells, other]
+    for s in range(1, plan.steps - 1):
+        sweep(plan, owner, buffers[s % 2], buffers[(s + 1) % 2], fields, masks, s, 1 + s, plan.wide - 1 - s)
+    s = plan.steps - 1
+    source = buffers[s % 2]
+
+    def last(x, carry):
+        for h in range(ny // 8):
+            row = PAD + (x + w) * pitch + w + 8 * h
+
+            def write(c, value, h=h):
+                if c < NF:
+                    flow_out[c, x, 8 * h : 8 * h + 8, :] = value
+                else:
+                    solute_out[c - NF, x, 8 * h : 8 * h + 8, :] = value
+
+            advance(plan, owner, source, fields, masks, s, row, write)
+        return carry
+
+    lax.fori_loop(0, nx, last, 0)
+
+
+def prepare(plan, owner, fields, masks, from_x, to_x):
+    w, nx, ny, depth, pitch = plan.halo, plan.nx, plan.ny, plan.depth, plan.pitch
     length = occupied(owner)
     lane = lanes(depth)
     gx, gy, gz = (lax.axis_index(a) for a in ("gx", "gy", "gz"))
@@ -341,7 +381,7 @@
     x_end = jnp.where(gx < last_x, nx + 2 * w, w + nx)
     sub = lax.broadcasted_iota(jnp.int32, (8, depth), 0)
 
-    def prepare(x, carry):
+    def one(x, carry):
         in_x = ((x >= x_first) & (x < x_end)).astype(F32)
         for h in range(pitch // 8):
             row = pl.multiple_of(PAD + x * pitch + 8 * h, 8)
@@ -353,115 +393,96 @@
             masks[2, pl.ds(row, 8), :] = jnp.where(inside, in_x, 0.0)
         return carry
 
-    lax.fori_loop(0, plan.wide, prepare, 0)
-
-    live = lane < length
-
-    def tile(source, s, row, write):
-        def field(ref, c, move=0):
-            return ref[c, pl.ds(row + move, 8), :]
-
-        blocked = {}
-
-        def reads(first, number):
-            result = []
-            for i in range(number):
-                sx, sy, sz = FLOW_DIRS[i]
-                if i == 0:
-                    result.append(field(source, first))
-                    continue
-                move = sx * pitch + sy
-                near = field(source, first + i, move)
-                if sz:
-                    near = pltpu.roll(near, (depth - sz) % depth, 1)
-                if i not in blocked:
-                    flags = field(fields, 0, move) if sz == 0 else field(masks, 0 if sz == 1 else 1, move)
-                    blocked[i] = flags != 0.0
-                result.append(jnp.where(blocked[i], field(source, first + OPPOSITE[i]), near))
-            return result
-
-        valid = field(masks, 2)
-        if s == plan.steps - 1:
-            valid = jnp.where(live, valid, 0.0)
-        aux = AUX - SOLID + NA * s
-        density, level, ux, uy, uz = (field(fields, aux + n) for n in range(NA))
-
-        h = reads(NF, NS)
-        px, py, pz = h[1] - h[2], h[3] - h[4], h[5] - h[6]
-        p0 = 0.25 * h[0] + 0.125 * ((h[1] + h[2]) + (h[3] + h[4]) + (h[5] + h[6]))
-        grown = 1.0 + level
-        uptake = langmuir_rate / (grown * grown)
-        common = valid * (
-            (solute_omega - uptake) * p0 + (solute_omega * 0.5) * (px * ux + py * uy + pz * uz)
-        )
-        keep = (1.0 - solute_omega) * valid
-        for i in range(NS):
-            write(NF + i, keep * h[i] + common)
-        factor = (0.5 * solute_omega) * level / jnp.maximum(density, 0.5)
-        fx, fy, fz = factor * px, factor * py, factor * pz
-
-        g = reads(0, NF)
-        a = {i: g[i] + g[i + 1] for i in range(1, NF, 2)}
-        d = {i: g[i] - g[i + 1] for i in range(1, NF, 2)}
-        m1x = (d[1] + d[1]) + (d[7] + d[9]) + (d[11] + d[13])
-        m1y = (d[3] + d[3]) + (d[7] - d[9]) + (d[15] + d[17])
-        m1z = (d[5] + d[5]) + (d[11] - d[13]) + (d[15] - d[17])
-        exy, exz, eyz = a[7] + a[9], a[11] + a[13], a[15] + a[17]
-        tx, ty, tz = a[1] + a[1], a[3] + a[3], a[5] + a[5]
-        mxx, myy, mzz = tx + exy + exz, ty + exy + eyz, tz + exz + eyz
-        mxy, mxz, myz = a[7] - a[9], a[11] - a[13], a[15] - a[17]
-        m0 = 12.0 * g[0] + (tx + ty + tz) + (exy + exz + eyz)
-        qx = mxx * ux + mxy * uy + mxz * uz
-        qy = mxy * ux + myy * uy + myz * uz
-        qz = mxz * ux + myz * uy + mzz * uz
-        square = ux * ux + uy * uy + uz * uz
-        scaled = flow_omega / 36.0
-        zero = m0 * (scaled + (1.5 * scaled) * square) - (4.5 * scaled) * (qx * ux + qy * uy + qz * uz)
-        zero = valid * (zero - (fx * ux + fy * uy + fz * uz))
-        bx = valid * ((3.0 * scaled) * (m1x + 3.0 * qx - m0 * ux) + fx)
-        by = valid * ((3.0 * scaled) * (m1y + 3.0 * qy - m0 * uy) + fy)
-        bz = valid * ((3.0 * scaled) * (m1z + 3.0 * qz - m0 * uz) + fz)
-        keep = (1.0 - flow_omega) * valid
-        write(0, keep * g[0] + zero)
-        moves = {1: bx, 3: by, 5: bz, 7: bx + by, 9: bx - by, 11: bx + bz, 13: bx - bz, 15: by + bz, 17: by - bz}
-        for i, move in moves.items():
-            write(i, keep * g[i] + (zero + move))
-            write(i + 1, keep * g[i + 1] + (zero - move))
-
-    buffers = [cells, other]
-    for s in range(plan.steps - 1):
-        source, target = buffers[s % 2], buffers[(s + 1) % 2]
-        first = PAD + (1 + s) * pitch
-
-        def body(n, carry, source=source, target=target, first=first, s=s):
-            for h in range(pitch // 8):
-                row = pl.multiple_of(first + pitch * n + 8 * h, 8)
-
-                def write(c, value, row=row):
-                    target[c, pl.ds(row, 8), :] = value
-
-                tile(source, s, row, write)
-            return carry
-
-        lax.fori_loop(0, plan.wide - 2 - 2 * s, body, 0)
-
-    s = plan.steps - 1
-    source = buffers[s % 2]
-
-    def last(x, carry):
-        for h in range(ny // 8):
-            row = PAD + (x + w) * pitch + w + 8 * h
-
-            def write(c, value, h=h):
-                if c < NF:
-                    flow_out[c, x, 8 * h : 8 * h + 8, :] = value
-                else:
-                    solute_out[c - NF, x, 8 * h : 8 * h + 8, :] = value
-
-            tile(source, s, row, write)
+    lax.fori_loop(from_x, to_x, one, 0)
+
+
+def sweep(plan, owner, source, target, fields, masks, s, from_x, to_x):
+    pitch = plan.pitch
+
+    def body(x, carry):
+        for h in range(pitch // 8):
+            row = pl.multiple_of(PAD + pitch * x + 8 * h, 8)
+
+            def write(c, value, row=row):
+                target[c, pl.ds(row, 8), :] = value
+
+            advance(plan, owner, source, fields, masks, s, row, write)
         return carry
 
-    lax.fori_loop(0, nx, last, 0)
+    lax.fori_loop(from_x, to_x, body, 0)
+
+
+def advance(plan, owner, source, fields, masks, s, row, write):
+    depth, pitch = plan.depth, plan.pitch
+    def field(ref, c, move=0):
+        return ref[c, pl.ds(row + move, 8), :]
+
+    blocked = {}
+
+    def reads(first, number):
+        result = []
+        for i in range(number):
+            sx, sy, sz = FLOW_DIRS[i]
+            if i == 0:
+                result.append(field(source, first))
+                continue
+            move = sx * pitch + sy
+            near = field(source, first + i, move)
+            if sz:
+                near = pltpu.roll(near, (depth - sz) % depth, 1)
+            if i not in blocked:
+                flags = field(fields, 0, move) if sz == 0 else field(masks, 0 if sz == 1 else 1, move)
+                blocked[i] = flags != 0.0
+            result.append(jnp.where(blocked[i], field(source, first + OPPOSITE[i]), near))
+        return result
+
+    valid = field(masks, 2)
+    if s == plan.steps - 1:
+        valid = jnp.where(lanes(depth) < occupied(owner), valid, 0.0)
+    aux = AUX - SOLID + NA * s
+    density, level, ux, uy, uz = (field(fields, aux + n) for n in range(NA))
+
+    h = reads(NF, NS)
+    px, py, pz = h[1] - h[2], h[3] - h[4], h[5] - h[6]
+    p0 = 0.25 * h[0] + 0.125 * ((h[1] + h[2]) + (h[3] + h[4]) + (h[5] + h[6]))
+    grown = 1.0 + level
+    uptake = langmuir_rate / (grown * grown)
+    common = valid * (
+        (solute_omega - uptake) * p0 + (solute_omega * 0.5) * (px * ux + py * uy + pz * uz)
+    )
+    keep = (1.0 - solute_omega) * valid
+    for i in range(NS):
+        write(NF + i, keep * h[i] + common)
+    factor = (0.5 * solute_omega) * level / jnp.maximum(density, 0.5)
+    fx, fy, fz = factor * px, factor * py, factor * pz
+
+    g = reads(0, NF)
+    a = {i: g[i] + g[i + 1] for i in range(1, NF, 2)}
+    d = {i: g[i] - g[i + 1] for i in range(1, NF, 2)}
+    m1x = (d[1] + d[1]) + (d[7] + d[9]) + (d[11] + d[13])
+    m1y = (d[3] + d[3]) + (d[7] - d[9]) + (d[15] + d[17])
+    m1z = (d[5] + d[5]) + (d[11] - d[13]) + (d[15] - d[17])
+    exy, exz, eyz = a[7] + a[9], a[11] + a[13], a[15] + a[17]
+    tx, ty, tz = a[1] + a[1], a[3] + a[3], a[5] + a[5]
+    mxx, myy, mzz = tx + exy + exz, ty + exy + eyz, tz + exz + eyz
+    mxy, mxz, myz = a[7] - a[9], a[11] - a[13], a[15] - a[17]
+    m0 = 12.0 * g[0] + (tx + ty + tz) + (exy + exz + eyz)
+    qx = mxx * ux + mxy * uy + mxz * uz
+    qy = mxy * ux + myy * uy + myz * uz
+    qz = mxz * ux + myz * uy + mzz * uz
+    square = ux * ux + uy * uy + uz * uz
+    scaled = flow_omega / 36.0
+    zero = m0 * (scaled + (1.5 * scaled) * square) - (4.5 * scaled) * (qx * ux + qy * uy + qz * uz)
+    zero = valid * (zero - (fx * ux + fy * uy + fz * uz))
+    bx = valid * ((3.0 * scaled) * (m1x + 3.0 * qx - m0 * ux) + fx)
+    by = valid * ((3.0 * scaled) * (m1y + 3.0 * qy - m0 * uy) + fy)
+    bz = valid * ((3.0 * scaled) * (m1z + 3.0 * qz - m0 * uz) + fz)
+    keep = (1.0 - flow_omega) * valid
+    write(0, keep * g[0] + zero)
+    moves = {1: bx, 3: by, 5: bz, 7: bx + by, 9: bx - by, 11: bx + bz, 13: bx - bz, 15: by + bz, 17: by - bz}
+    for i, move in moves.items():
+        write(i, keep * g[i] + (zero + move))
+        write(i + 1, keep * g[i + 1] + (zero - move))
 
 
 VMEM = pl.BlockSpec(memory_space=pltpu.VMEM)
@@ -546,20 +567,30 @@
     from_c_low = move(c_high, "gx", 1).reshape(shape)
     from_c_high = move(c_low, "gx", -1).reshape(shape)
     height = plan.wide * plan.pitch + 2 * PAD
+    state = jax.ShapeDtypeStruct((SOLID, height, depth), F32)
+    wide = call(
+        functools.partial(first_kernel, plan),
+        [SMEM, ANY] + [VMEM] * 4,
+        [
+            state,
+            jax.ShapeDtypeStruct((plan.chan - SOLID, height, depth), F32),
+            state,
+            jax.ShapeDtypeStruct((3, height, depth), F32),
+        ],
+        "first",
+        1 << 26,
+        [pltpu.SemaphoreType.DMA((2,))],
+        8 << 20,
+    )(owner, inner, from_y_low, from_y_high, from_x_low, from_x_high)
     flow, solute = call(
         functools.partial(steps_kernel, plan),
-        [SMEM, ANY] + [VMEM] * 6,
+        [SMEM] + [VMEM] * 6,
         [jax.ShapeDtypeStruct(flow_adjoint.shape, F32), jax.ShapeDtypeStruct(solute_adjoint.shape, F32)],
         "steps",
         1 << 28,
-        [
-            pltpu.VMEM((SOLID, height, depth), F32),
-            pltpu.VMEM((SOLID, height, depth), F32),
-            pltpu.VMEM((plan.chan - SOLID, height, depth), F32),
-            pltpu.VMEM((3, height, depth), F32),
-            pltpu.SemaphoreType.DMA((2,)),
-        ],
-    )(owner, inner, from_y_low, from_y_high, from_x_low, from_x_high, from_c_low, from_c_high)
+        (),
+        10 << 20,
+    )(owner, *wide, from_c_low, from_c_high)
     return (flow, solute)
 
 

time: 79.4 us -> 76.2 us (0.960)
  Pallas kernels: 41.7 us -> 33.6 us
  local copies, waits for them, and re-layouts: 2.08 us -> 8.89 us
  starting transfers between devices: 21 us -> 19.9 us
  waiting for transfers between devices: 13.5 us -> 12.4 us
    unnamed x20 -> x26, local copies, waits for them, and re-layouts: 2.08 us -> 8.89 us
    pallas_call x1, Pallas kernels: 10 us -> 5.24 us  [per_device(): call(functools.partial(inner_kernel, plan, ring, parts), [SMEM] + [ANY] *...]
    pallas_call x1 -> x2, Pallas kernels: 20.3 us -> 18.1 us  [the longest x1 12.7 us: per_device(): call(functools.partial(steps_kernel, plan), [SMEM] + [VMEM] * 6, [jax.Sha...]
    pallas_call x1, Pallas kernels: 3.02 us -> 1.88 us  [per_device(): call(functools.partial(insert_kernel, plan, ring, parts), [SMEM] + [VMEM]...]
    ppermute x6, starting transfers between devices: 18.9 us -> 17.8 us  [move(): lax.ppermute(value, axis, [(i, i + by) for i in range(size) if 0 <= i + b...]
  transfers between devices with their start and end apart: 7 -> 7, of which waited for: 6 -> 3; matrix products, arithmetic and copies ran while one was open for 0% -> 0% of each run, Pallas kernels for 15% -> 17%
where the time goes in v4:
time: 76.2 us; the launch traced here: 75.7 us
  Pallas kernels  33.6 us (44%)
  starting transfers between devices  19.9 us (26%)
  waiting for transfers between devices  12.4 us (16%)
  local copies, waits for them, and re-layouts  8.89 us (12%)
  between operations  0.85 us (1%)
    ppermute x6, starting transfers between devices, move(): lax.ppermute(value, axis, [(i, i + by) for i in range(size) if 0 <= i + b...  17.8 us
    pallas_call x1, Pallas kernels, per_device(): call(functools.partial(steps_kernel, plan), [SMEM] + [VMEM] * 6, [jax.Sha...  12.7 us
    ppermute x6, waiting for transfers between devices, move(): lax.ppermute(value, axis, [(i, i + by) for i in range(size) if 0 <= i + b...  12.4 us
    unnamed x26, local copies, waits for them, and re-layouts  8.89 us
    pallas_call x1, Pallas kernels, per_device(): call(functools.partial(pack_kernel, plan, ring, parts), [SMEM] + [ANY] *...  6.32 us
    pallas_call x1, Pallas kernels, per_device(): call(functools.partial(first_kernel, plan), [SMEM, ANY] + [VMEM] * 4, [st...  5.35 us
    pallas_call x1, Pallas kernels, per_device(): call(functools.partial(inner_kernel, plan, ring, parts), [SMEM] + [ANY] *...  5.24 us
    ppermute x1, starting transfers between devices, per_device(): received = [lax.ppermute(packed[0], 'gz', [(0, 1), (1, 0)])]  2.13 us
  transfers between devices with their start and end apart: 7, of which 3 were waited for; matrix products, arithmetic and copies ran while one was open for 0% of the time, Pallas kernels for 17%

profile of v4, /device:TPU:1, one launch (start us, length us, event | category | flops | bytes accessed | tf_op | source)
XLA Modules:
  0.0 75.7 jit_solution(686612085664704393)
XLA Ops:
  0.6 0.0 copy-start.1
  0.6 0.0 copy-start.3
  0.7 0.0 copy-start.7
  0.7 0.0 copy-start.9
  0.7 6.3 %pack_column.1.refs_6_ = f32[42,8,128]{2,1,0:T(8,128)} custom-call(s32[8]{0:T(128)} %owner.5, f32[19,256,128]{2,1,0:T(8,128)} %bitcast.10, f32[7,256,128]{2,1,0:T(8,128)} %bitcast.13, bf16[4,256,128]{2,1,0:T(8,128)(2,1)} %bitcast.21, bf16[12,256,128]{2,1,0:T(8,128)(2,1)} %bitcast.16, bf16[4,256,128]{2,1,0:T(8,128)(2,1)} %bitcast.24, s32[1,256,128]{2,1,0:T(8,128)} %bitcast.27), custom_call_target="tpu_custom_call" | custom-call | flops 4194304 | bytes 8388608 | tf_op jit(solution)/shard_map/pack_column/pallas_call | solution.py:525
  7.0 2.1 %collective-permute-start = (f32[42,8,128]{2,1,0:T(8,128)}, f32[42,8,128]{2,1,0:T(8,128)S(1)}, u32[]{:S(2)}, u32[]{:S(2)}) collective-permute-start(f32[42,8,128]{2,1,0:T(8,128)} %pack_column.1.refs_6_), channel_id=1, source_target_pairs={{0,1},{1,0},{2,3},{3,2},{4,5},{5,4},{6,7},{7,6},{8,9},{9,8},{10,11... | collective-permute-start | bytes 516104 | tf_op jit(solution)/shard_map/ppermute | solution.py:535
  9.2 1.7 %copy-done = f32[19,16,16,128]{3,2,1,0:T(8,128)S(1)} copy-done((f32[19,16,16,128]{3,2,1,0:T(8,128)S(1)}, f32[19,16,16,128]{3,2,1,0:T(8,128)}, u32[]{:S(2)}) %copy-start) | copy-done | bytes 2490392
  10.9 1.2 %copy-done.2 = f32[7,16,16,128]{3,2,1,0:T(8,128)S(1)} copy-done((f32[7,16,16,128]{3,2,1,0:T(8,128)S(1)}, f32[7,16,16,128]{3,2,1,0:T(8,128)}, u32[]{:S(2)}) %copy-start.2) | copy-done | bytes 917528
  12.0 1.1 %copy-done.4 = bf16[4,3,16,16,128]{4,3,2,1,0:T(8,128)(2,1)S(1)} copy-done((bf16[4,3,16,16,128]{4,3,2,1,0:T(8,128)(2,1)S(1)}, bf16[4,3,16,16,128]{4,3,2,1,0:T(8,128)(2,1)}, u32[]{:S(2)}) %copy-start.4) | copy-done | bytes 786456
  13.2 0.9 %copy-done.6 = bf16[4,16,16,128]{3,2,1,0:T(8,128)(2,1)S(1)} copy-done((bf16[4,16,16,128]{3,2,1,0:T(8,128)(2,1)S(1)}, bf16[4,16,16,128]{3,2,1,0:T(8,128)(2,1)}, u32[]{:S(2)}) %copy-start.6) | copy-done | bytes 262168
  14.1 0.9 %copy-done.8 = bf16[4,16,16,128]{3,2,1,0:T(8,128)(2,1)S(1)} copy-done((bf16[4,16,16,128]{3,2,1,0:T(8,128)(2,1)S(1)}, bf16[4,16,16,128]{3,2,1,0:T(8,128)(2,1)}, u32[]{:S(2)}) %copy-start.8) | copy-done | bytes 262168
  15.1 0.9 %copy-done.10 = s32[16,16,128]{2,1,0:T(8,128)S(1)} copy-done((s32[16,16,128]{2,1,0:T(8,128)S(1)}, s32[16,16,128]{2,1,0:T(8,128)}, u32[]{:S(2)}) %copy-start.10) | copy-done | bytes 131096
  16.0 0.9 %copy-done.11 = f32[42,8,128]{2,1,0:T(8,128)S(1)} copy-done((f32[42,8,128]{2,1,0:T(8,128)S(1)}, f32[42,8,128]{2,1,0:T(8,128)}, u32[]{:S(2)}) %copy-start.11) | copy-done | bytes 172056
  16.9 1.7 %faces.1 = (f32[118,16,128]{2,1,0:T(8,128)S(1)}, f32[118,16,128]{2,1,0:T(8,128)S(1)}) custom-call(f32[19,256,128]{2,1,0:T(8,128)S(1)} %bitcast.11, f32[7,256,128]{2,1,0:T(8,128)S(1)} %bitcast.14, bf16[4,256,128]{2,1,0:T(8,128)(2,1)S(1)} %bitcast.22, bf16[12,256,128]{2,1,0:T(8,128)(2,1)S(1)} %bitcast.17, bf16[4,256,128]{2,1,0:T(8,128)(2,1)S(1)} %bitcast.25, ...), custom_call_target="tpu_custom_call" | custom-call | flops 16777216 | bytes 8388608 | tf_op jit(solution)/shard_map/faces/pallas_call | solution.py:540
  18.6 0.0 collective-permute-done.refs_7_.rest_0_
  18.6 1.9 %insert.1 = (f32[118,16,128]{2,1,0:T(8,128)S(1)}, f32[118,16,128]{2,1,0:T(8,128)S(1)}) custom-call(s32[8]{0:T(128)S(1)} %copy-done.12, f32[118,16,128]{2,1,0:T(8,128)S(1)} %get-tuple-element.16.low, f32[118,16,128]{2,1,0:T(8,128)S(1)} %get-tuple-element.17.high, f32[42,8,128]{2,1,0:T(8,128)S(1)} %collective-permute-done.refs_7_.rest_0_), custom_call_target="tpu_custom_call" | custom-call | flops 4194304 | bytes 8388608 | tf_op jit(solution)/shard_map/insert/pallas_call | solution.py:543
  20.5 3.3 %collective-permute-start.1 = (f32[118,16,128]{2,1,0:T(8,128)S(1)}, f32[118,16,128]{2,1,0:T(8,128)S(1)}, u32[]{:S(2)}, u32[]{:S(2)}) collective-permute-start(f32[118,16,128]{2,1,0:T(8,128)S(1)} %get-tuple-element.18), channel_id=1, source_target_pairs={{0,2},{2,4},{4,6},{1,3},{3,5},{5,7},{8,10},{10,12},{12,14},{9,11},... | collective-permute-start | bytes 2899976 | tf_op jit(solution)/shard_map/ppermute | solution.py:517
  23.7 1.3 %collective-permute-start.2 = (f32[118,16,128]{2,1,0:T(8,128)S(1)}, f32[118,16,128]{2,1,0:T(8,128)S(1)}, u32[]{:S(2)}, u32[]{:S(2)}) collective-permute-start(f32[118,16,128]{2,1,0:T(8,128)S(1)} %get-tuple-element.19), channel_id=1, source_target_pairs={{2,0},{4,2},{6,4},{3,1},{5,3},{7,5},{10,8},{12,10},{14,12},{11,9},... | collective-permute-start | bytes 2899976 | tf_op jit(solution)/shard_map/ppermute | solution.py:517
  25.1 0.0 copy-start.5
  25.1 1.1 %copy-done.5 = bf16[4,3,16,16,128]{4,3,2,1,0:T(8,128)(2,1)S(1)} copy-done((bf16[4,3,16,16,128]{4,3,2,1,0:T(8,128)(2,1)S(1)}, bf16[4,3,16,16,128]{4,3,2,1,0:T(8,128)(2,1)}, u32[]{:S(2)}) %copy-start.5) | copy-done | bytes 786456
  26.2 5.2 %inner.1 = (f32[47,384,128]{2,1,0:T(8,128)S(1)}, f32[118,16,128]{2,1,0:T(8,128)S(1)}, f32[118,16,128]{2,1,0:T(8,128)S(1)}) custom-call(s32[8]{0:T(128)S(1)} %copy-done.12, f32[19,256,128]{2,1,0:T(8,128)S(1)} %bitcast.12, f32[7,256,128]{2,1,0:T(8,128)S(1)} %bitcast.15, bf16[4,256,128]{2,1,0:T(8,128)(2,1)S(1)} %bitcast.23, bf16[12,256,128]{2,1,0:T(8,128)(2,1)S(1)} %bitcast.18, ...), custom_call_target="tpu_custom_call" | custom-call | flops 16777216 | bytes 8388608 | tf_op jit(solution)/shard_map/inner/pallas_call | solution.py:548
  31.5 4.2 %collective-permute-start.3 = (f32[118,16,128]{2,1,0:T(8,128)S(1)}, f32[118,16,128]{2,1,0:T(8,128)S(1)}, u32[]{:S(2)}, u32[]{:S(2)}) collective-permute-start(f32[118,16,128]{2,1,0:T(8,128)S(1)} %get-tuple-element.20), channel_id=1, source_target_pairs={{0,8},{8,16},{16,24},{1,9},{9,17},{17,25},{2,10},{10,18},{18,26},{... | collective-permute-start | bytes 2899976 | tf_op jit(solution)/shard_map/ppermute | solution.py:517
  35.7 1.9 %collective-permute-start.4 = (f32[118,16,128]{2,1,0:T(8,128)S(1)}, f32[118,16,128]{2,1,0:T(8,128)S(1)}, u32[]{:S(2)}, u32[]{:S(2)}) collective-permute-start(f32[118,16,128]{2,1,0:T(8,128)S(1)} %get-tuple-element.21), channel_id=1, source_target_pairs={{8,0},{16,8},{24,16},{9,1},{17,9},{25,17},{10,2},{18,10},{26,18},{... | collective-permute-start | bytes 2899976 | tf_op jit(solution)/shard_map/ppermute | solution.py:517
  37.6 5.8 %collective-permute-done.1.y_low = f32[118,16,128]{2,1,0:T(8,128)S(1)} collective-permute-done((f32[118,16,128]{2,1,0:T(8,128)S(1)}, f32[118,16,128]{2,1,0:T(8,128)S(1)}, u32[]{:S(2)}, u32[]{:S(2)}) %collective-permute-start.1) | collective-permute-done | bytes 966688 | tf_op jit(solution)/shard_map/ppermute | solution.py:517
  43.4 3.9 %collective-permute-done.2.y_high = f32[118,16,128]{2,1,0:T(8,128)S(1)} collective-permute-done((f32[118,16,128]{2,1,0:T(8,128)S(1)}, f32[118,16,128]{2,1,0:T(8,128)S(1)}, u32[]{:S(2)}, u32[]{:S(2)}) %collective-permute-start.2) | collective-permute-done | bytes 966688 | tf_op jit(solution)/shard_map/ppermute | solution.py:517
  47.3 0.4 corners.1
  47.7 5.2 %collective-permute-start.5 = (f32[944,128]{1,0:T(8,128)S(1)}, f32[944,128]{1,0:T(8,128)S(1)}, u32[]{:S(2)}, u32[]{:S(2)}) collective-permute-start(f32[944,128]{1,0:T(8,128)S(1)} %get-tuple-element.26), channel_id=1, source_target_pairs={{0,8},{8,16},{16,24},{1,9},{9,17},{17,25},{2,10},{10,18},{18,26},{... | collective-permute-start | bytes 1449992 | tf_op jit(solution)/shard_map/ppermute | solution.py:517
  52.9 1.9 %collective-permute-start.6 = (f32[944,128]{1,0:T(8,128)S(1)}, f32[944,128]{1,0:T(8,128)S(1)}, u32[]{:S(2)}, u32[]{:S(2)}) collective-permute-start(f32[944,128]{1,0:T(8,128)S(1)} %get-tuple-element.27), channel_id=1, source_target_pairs={{8,0},{16,8},{24,16},{9,1},{17,9},{25,17},{10,2},{18,10},{26,18},{... | collective-permute-start | bytes 1449992 | tf_op jit(solution)/shard_map/ppermute | solution.py:517
  54.8 0.0 collective-permute-done.4.x_high
  54.8 5.4 %first.1 = (f32[26,592,128]{2,1,0:T(8,128)S(1)}, f32[21,592,128]{2,1,0:T(8,128)S(1)}, f32[26,592,128]{2,1,0:T(8,128)S(1)}, f32[3,592,128]{2,1,0:T(8,128)S(1)}) custom-call(s32[8]{0:T(128)S(1)} %copy-done.12, f32[47,384,128]{2,1,0:T(8,128)S(1)} %get-tuple-element.15.inner, f32[118,16,128]{2,1,0:T(8,128)S(1)} %collective-permute-done.1.y_low, ...), custom_call_target="tpu_custom_call" | custom-call | flops 67108864 | bytes 8388608 | tf_op jit(solution)/shard_map/first/pallas_call | solution.py:571
  60.2 2.7 %collective-permute-done.6 = f32[944,128]{1,0:T(8,128)S(1)} collective-permute-done((f32[944,128]{1,0:T(8,128)S(1)}, f32[944,128]{1,0:T(8,128)S(1)}, u32[]{:S(2)}, u32[]{:S(2)}) %collective-permute-start.6) | collective-permute-done | bytes 483360 | tf_op jit(solution)/shard_map/ppermute | solution.py:517
  62.9 12.7 %steps.1 = (f32[19,16,16,128]{3,2,1,0:T(8,128)}, f32[7,16,16,128]{3,2,1,0:T(8,128)}) custom-call(s32[8]{0:T(128)S(1)} %copy-done.12, f32[26,592,128]{2,1,0:T(8,128)S(1)} %get-tuple-element.22.cells, f32[21,592,128]{2,1,0:T(8,128)S(1)} %get-tuple-element.23.fields, f32[26,592,128]{2,1,0:T(8,128)S(1)} %get-tuple-element.24.other, ...), custom_call_target="tpu_custom_call" | custom-call | flops 268435456 | bytes 8388608 | tf_op jit(solution)/shard_map/steps/pallas_call | solution.py:585
  (15 shorter events, 0.0 us)
Async XLA Ops:
  0.6 24.4 %copy-start.1 = (f32[19,16,16,128]{3,2,1,0:T(8,128)S(1)}, f32[19,16,16,128]{3,2,1,0:T(8,128)}, u32[]{:S(2)}) copy-start(f32[19,16,16,128]{3,2,1,0:T(8,128)} %param.7) | copy-start | bytes 7471108
  0.6 24.4 %copy-start.3 = (f32[7,16,16,128]{3,2,1,0:T(8,128)S(1)}, f32[7,16,16,128]{3,2,1,0:T(8,128)}, u32[]{:S(2)}) copy-start(f32[7,16,16,128]{3,2,1,0:T(8,128)} %param.8) | copy-start | bytes 2752516
  0.7 24.4 %copy-start.7 = (bf16[4,16,16,128]{3,2,1,0:T(8,128)(2,1)S(1)}, bf16[4,16,16,128]{3,2,1,0:T(8,128)(2,1)}, u32[]{:S(2)}) copy-start(bf16[4,16,16,128]{3,2,1,0:T(8,128)(2,1)} %param.9) | copy-start | bytes 786436
  0.7 24.4 %copy-start.9 = (bf16[4,16,16,128]{3,2,1,0:T(8,128)(2,1)S(1)}, bf16[4,16,16,128]{3,2,1,0:T(8,128)(2,1)}, u32[]{:S(2)}) copy-start(bf16[4,16,16,128]{3,2,1,0:T(8,128)(2,1)} %param.11) | copy-start | bytes 786436
  0.7 17.9 %copy-start.12 = (s32[8]{0:T(128)S(1)}, s32[8]{0:T(128)}, u32[]{:S(2)}) copy-start(s32[8]{0:T(128)} %owner.5) | copy-start | bytes 100
  7.0 11.6 %collective-permute-start = (f32[42,8,128]{2,1,0:T(8,128)}, f32[42,8,128]{2,1,0:T(8,128)S(1)}, u32[]{:S(2)}, u32[]{:S(2)}) collective-permute-start(f32[42,8,128]{2,1,0:T(8,128)} %pack_column.1.refs_6_), channel_id=1, source_target_pairs={{0,1},{1,0},{2,3},{3,2},{4,5},{5,4},{6,7},{7,6},{8,9},{9,8},{10,11... | collective-permute-start | bytes 516104 | tf_op jit(solution)/shard_map/ppermute | solution.py:535
  9.2 1.7 %copy-start = (f32[19,16,16,128]{3,2,1,0:T(8,128)S(1)}, f32[19,16,16,128]{3,2,1,0:T(8,128)}, u32[]{:S(2)}) copy-start(f32[19,16,16,128]{3,2,1,0:T(8,128)} %param.7) | copy-start | bytes 7471108
  10.9 1.2 %copy-start.2 = (f32[7,16,16,128]{3,2,1,0:T(8,128)S(1)}, f32[7,16,16,128]{3,2,1,0:T(8,128)}, u32[]{:S(2)}) copy-start(f32[7,16,16,128]{3,2,1,0:T(8,128)} %param.8) | copy-start | bytes 2752516
  12.0 1.1 %copy-start.4 = (bf16[4,3,16,16,128]{4,3,2,1,0:T(8,128)(2,1)S(1)}, bf16[4,3,16,16,128]{4,3,2,1,0:T(8,128)(2,1)}, u32[]{:S(2)}) copy-start(bf16[4,3,16,16,128]{4,3,2,1,0:T(8,128)(2,1)} %param.10) | copy-start | bytes 2359300
  13.2 0.9 %copy-start.6 = (bf16[4,16,16,128]{3,2,1,0:T(8,128)(2,1)S(1)}, bf16[4,16,16,128]{3,2,1,0:T(8,128)(2,1)}, u32[]{:S(2)}) copy-start(bf16[4,16,16,128]{3,2,1,0:T(8,128)(2,1)} %param.9) | copy-start | bytes 786436
  14.1 0.9 %copy-start.8 = (bf16[4,16,16,128]{3,2,1,0:T(8,128)(2,1)S(1)}, bf16[4,16,16,128]{3,2,1,0:T(8,128)(2,1)}, u32[]{:S(2)}) copy-start(bf16[4,16,16,128]{3,2,1,0:T(8,128)(2,1)} %param.11) | copy-start | bytes 786436
  15.1 0.9 %copy-start.10 = (s32[16,16,128]{2,1,0:T(8,128)S(1)}, s32[16,16,128]{2,1,0:T(8,128)}, u32[]{:S(2)}) copy-start(s32[16,16,128]{2,1,0:T(8,128)} %param.12) | copy-start | bytes 393220
  16.0 0.9 %copy-start.11 = (f32[42,8,128]{2,1,0:T(8,128)S(1)}, f32[42,8,128]{2,1,0:T(8,128)}, u32[]{:S(2)}) copy-start(f32[42,8,128]{2,1,0:T(8,128)} %pack_column.1.refs_6_) | copy-start | bytes 516100
  20.5 22.9 %collective-permute-start.1 = (f32[118,16,128]{2,1,0:T(8,128)S(1)}, f32[118,16,128]{2,1,0:T(8,128)S(1)}, u32[]{:S(2)}, u32[]{:S(2)}) collective-permute-start(f32[118,16,128]{2,1,0:T(8,128)S(1)} %get-tuple-element.18), channel_id=1, source_target_pairs={{0,2},{2,4},{4,6},{1,3},{3,5},{5,7},{8,10},{10,12},{12,14},{9,11},... | collective-permute-start | bytes 2899976 | tf_op jit(solution)/shard_map/ppermute | solution.py:517
  23.7 23.6 %collective-permute-start.2 = (f32[118,16,128]{2,1,0:T(8,128)S(1)}, f32[118,16,128]{2,1,0:T(8,128)S(1)}, u32[]{:S(2)}, u32[]{:S(2)}) collective-permute-start(f32[118,16,128]{2,1,0:T(8,128)S(1)} %get-tuple-element.19), channel_id=1, source_target_pairs={{2,0},{4,2},{6,4},{3,1},{5,3},{7,5},{10,8},{12,10},{14,12},{11,9},... | collective-permute-start | bytes 2899976 | tf_op jit(solution)/shard_map/ppermute | solution.py:517
  25.1 1.1 %copy-start.5 = (bf16[4,3,16,16,128]{4,3,2,1,0:T(8,128)(2,1)S(1)}, bf16[4,3,16,16,128]{4,3,2,1,0:T(8,128)(2,1)}, u32[]{:S(2)}) copy-start(bf16[4,3,16,16,128]{4,3,2,1,0:T(8,128)(2,1)} %param.10) | copy-start | bytes 2359300
  31.5 23.3 %collective-permute-start.3 = (f32[118,16,128]{2,1,0:T(8,128)S(1)}, f32[118,16,128]{2,1,0:T(8,128)S(1)}, u32[]{:S(2)}, u32[]{:S(2)}) collective-permute-start(f32[118,16,128]{2,1,0:T(8,128)S(1)} %get-tuple-element.20), channel_id=1, source_target_pairs={{0,8},{8,16},{16,24},{1,9},{9,17},{17,25},{2,10},{10,18},{18,26},{... | collective-permute-start | bytes 2899976 | tf_op jit(solution)/shard_map/ppermute | solution.py:517
  35.7 19.1 %collective-permute-start.4 = (f32[118,16,128]{2,1,0:T(8,128)S(1)}, f32[118,16,128]{2,1,0:T(8,128)S(1)}, u32[]{:S(2)}, u32[]{:S(2)}) collective-permute-start(f32[118,16,128]{2,1,0:T(8,128)S(1)} %get-tuple-element.21), channel_id=1, source_target_pairs={{8,0},{16,8},{24,16},{9,1},{17,9},{25,17},{10,2},{18,10},{26,18},{... | collective-permute-start | bytes 2899976 | tf_op jit(solution)/shard_map/ppermute | solution.py:517
  47.7 12.5 %collective-permute-start.5 = (f32[944,128]{1,0:T(8,128)S(1)}, f32[944,128]{1,0:T(8,128)S(1)}, u32[]{:S(2)}, u32[]{:S(2)}) collective-permute-start(f32[944,128]{1,0:T(8,128)S(1)} %get-tuple-element.26), channel_id=1, source_target_pairs={{0,8},{8,16},{16,24},{1,9},{9,17},{17,25},{2,10},{10,18},{18,26},{... | collective-permute-start | bytes 1449992 | tf_op jit(solution)/shard_map/ppermute | solution.py:517
  52.9 10.1 %collective-permute-start.6 = (f32[944,128]{1,0:T(8,128)S(1)}, f32[944,128]{1,0:T(8,128)S(1)}, u32[]{:S(2)}, u32[]{:S(2)}) collective-permute-start(f32[944,128]{1,0:T(8,128)S(1)} %get-tuple-element.27), channel_id=1, source_target_pairs={{8,0},{16,8},{24,16},{9,1},{17,9},{25,17},{10,2},{18,10},{26,18},{... | collective-permute-start | bytes 1449992 | tf_op jit(solution)/shard_map/ppermute | solution.py:517

commit v5 on v4

--- a/solution.py
+++ b/solution.py
@@ -100,72 +100,74 @@
         body(i)
 
 
-def fetch(arrays, held, sems):
-    copies = [pltpu.make_async_copy(a, b, sems.at[i]) for i, (a, b) in enumerate(zip(arrays, held))]
+def tiles_of(plan):
+    return [(y * (plan.nx // 8) + h, y, 8 * h) for y in range(plan.ny) for h in range(plan.nx // 8)]
+
+
+def pack_kernel(plan, ring, parts, owner, flow, solute, density, velocity, level, solid, *refs):
+    outs, (flow_out, solute_out, wide), (density_in, velocity_in, level_in, solid_in, sems) = (
+        refs[:parts],
+        refs[parts : parts + 3],
+        refs[parts + 3 :],
+    )
+    w, depth, nx, ny = plan.halo, plan.depth, plan.nx, plan.ny
+    cuts = [0, 7, 13, NF]
+    flows = [pl.ds(a, b - a) for a, b in zip(cuts, cuts[1:])]
+    pairs = [(flow.at[cut], flow_out.at[cut]) for cut in flows] + [
+        (solute, solute_out),
+        (solid, solid_in),
+        (density, density_in),
+        (level, level_in),
+        (velocity, velocity_in),
+    ]
+    copies = [pltpu.make_async_copy(a, b, sems.at[i]) for i, (a, b) in enumerate(pairs)]
     for copy in copies:
         copy.start()
-    return copies
-
-
-def gather(plan, arrays, held, wide, sems, steps, body):
-    copies = fetch(arrays, held, sems)
-    flow, solute, density, velocity, level, solid = held
-    ny = plan.ny
-    copies[0].wait()
-    body(0, NF, flow)
-    for copy in copies[1:]:
-        copy.wait()
-    body(NF, NS, solute)
-    sources = [(solid, 0)]
-    for s in range(steps):
-        t = plan.steps - 1 - s
-        sources += [(density, t), (level, t), (velocity, 3 * t), (velocity, 3 * t + 1), (velocity, 3 * t + 2)]
-
-    for c, (ref, i) in enumerate(sources):
-        for x in range(plan.nx):
-            wide[c, x * ny : (x + 1) * ny, :] = ref[i, x * ny : (x + 1) * ny, :].astype(F32)
-    body(SOLID, len(sources), wide)
-
-
-def tiles_of(plan):
-    return [(y * (plan.nx // 8) + h, y, 8 * h) for y in range(plan.ny) for h in range(plan.nx // 8)]
-
-
-def pack_kernel(plan, ring, parts, *refs):
-    owner, arrays, outs, held, wide, sems = refs[0], refs[1:7], refs[7 : 7 + parts], refs[7 + parts : 13 + parts], refs[-2], refs[-1]
-    w, depth, ny = plan.halo, plan.depth, plan.ny
+
     length = occupied(owner)
     group = lanes(depth) // w
     places = z_places(plan, length, ring)
     shifts = [{n: (w * n + depth - start) & (depth - 1) for n, _, _ in tiles_of(plan)} for start, _ in places]
 
-    def body(at, number, ref):
+    def pack(at, first, number, ref):
         def one(i):
             packed = [None] * parts
             for n, y, x in tiles_of(plan):
-                tile = ref[i, pl.ds(x * ny + y, 8, stride=ny), :]
+                tile = ref[first + i, pl.ds(x * ny + y, 8, stride=ny), :]
                 for p in range(parts):
                     moved = pltpu.roll(tile, shifts[p][n], 1)
                     packed[p] = moved if n == 0 else jnp.where(group == n, moved, packed[p])
             for p in range(parts):
-                outs[p][at + i] = packed[p]
-
-        each(number, one, 3)
-
-    gather(plan, arrays, held, wide, sems, plan.steps - 1, body)
-
-
-def faces_kernel(plan, *refs):
-    arrays, (y_low, y_high), held, wide, sems = refs[:6], refs[7:9], refs[9:15], refs[15], refs[16]
+                outs[p][at + first + i] = packed[p]
+
+        each(number, one, 6)
+
+    for copy, a, b in zip(copies, cuts, cuts[1:]):
+        copy.wait()
+        pack(0, a, b - a, flow_out)
+    for copy in copies[3:]:
+        copy.wait()
+    pack(NF, 0, NS, solute_out)
+    sources = [(solid_in, 0)]
+    for s in range(plan.steps):
+        t = plan.steps - 1 - s
+        sources += [(density_in, t), (level_in, t)] + [(velocity_in, 3 * t + i) for i in range(3)]
+    for c, (ref, i) in enumerate(sources):
+        for x in range(nx):
+            wide[c, x * ny : (x + 1) * ny, :] = ref[i, x * ny : (x + 1) * ny, :].astype(F32)
+    pack(SOLID, 0, plan.sent - SOLID, wide)
+
+
+def faces_kernel(plan, flow, solute, wide, packed, y_low, y_high):
     w, nx, ny = plan.halo, plan.nx, plan.ny
-
-    def body(at, number, ref):
-        def row(c, y):
+    for at, number, ref in ((0, NF, flow), (NF, NS, solute), (SOLID, plan.sent - SOLID, wide)):
+
+        def row(c, y, ref=ref):
             return ref[c, pl.ds(y, nx, stride=ny), :]
 
         for k in range(1, w):
 
-            def one(c, k=k):
+            def one(c, k=k, at=at, row=row):
                 y_low[plan.base[k] + at + c] = row(c, k - 1)
                 y_high[plan.base[k] + at + c] = row(c, ny - k)
 
@@ -174,8 +176,6 @@
             for j, c in enumerate(plan.last(1, sign)):
                 if at <= c < at + number:
                     out[plan.base[w] + j] = row(c - at, y)
-
-    gather(plan, arrays, held, wide, sems, plan.steps - 1, body)
 
 
 def column(plan, ring, owner, received):
@@ -219,14 +219,13 @@
             one(raw, out, plan.base[w] + j, c, y)
 
 
-def inner_kernel(plan, ring, parts, *refs):
-    owner, arrays, received, rest = refs[0], refs[1:7], refs[7 : 7 + parts], refs[7 + parts :]
-    (out, x_low, x_high), held, wide, sems = rest[:3], rest[3:9], rest[9], rest[10]
+def inner_kernel(plan, ring, parts, owner, flow, solute, wide, *rest):
+    received, (out, x_low, x_high) = rest[:parts], rest[parts:]
     w, nx, ny, pitch = plan.halo, plan.nx, plan.ny, plan.pitch
     put = column(plan, ring, owner, received)
-
-    def body(at, number, ref):
-        def one(i, sent=True):
+    for at, number, ref in ((0, NF, flow), (NF, NS, solute), (SOLID, plan.chan - SOLID, wide)):
+
+        def one(i, sent=True, at=at, ref=ref):
             slabs = [r[at + i] for r in received] if sent else []
             for n, y, x in tiles_of(plan):
                 tile = ref[i, pl.ds(x * ny + y, 8, stride=ny), :]
@@ -234,9 +233,7 @@
 
         within = min(number, plan.sent - at)
         each(within, one, 3)
-        each(number - within, lambda i: one(within + i, False), 1)
-
-    gather(plan, arrays, held, wide, sems, plan.steps, body)
+        each(number - within, lambda i, one=one, within=within: one(within + i, False), 1)
 
     def row(c, x):
         return out[c, x * pitch + w : x * pitch + w + ny, :]
@@ -488,6 +485,7 @@
 VMEM = pl.BlockSpec(memory_space=pltpu.VMEM)
 SMEM = pl.BlockSpec(memory_space=pltpu.SMEM)
 ANY = pl.BlockSpec(memory_space=pl.ANY)
+HBM = pl.BlockSpec(memory_space=pltpu.HBM)
 
 
 def call(kernel, ins, outs, name, cost, scratch=(), limit=VMEM_LIMIT):
@@ -511,34 +509,34 @@
     w = plan.halo
     arguments = (flow_adjoint, solute_adjoint, flow_density, flow_velocity, solute_level, solid)
     fields = [f.reshape(-1, nx * ny, depth) for f in arguments]
+    owner, *fields = (pltpu.with_memory_space_constraint(f, pltpu.HBM) for f in (owner, *fields))
 
     def move(value, axis, by):
         size = lax.axis_size(axis)
         return lax.ppermute(value, axis, [(i, i + by) for i in range(size) if 0 <= i + by < size])
 
-    def scratch(steps):
-        held = [pltpu.VMEM(f.shape, f.dtype) for f in fields]
-        wide = pltpu.VMEM((AUX - SOLID + NA * steps, nx * ny, depth), F32)
-        return held + [wide, pltpu.SemaphoreType.DMA((len(fields),))]
-
     parts = 1 if ring == 2 else 2
-    packed = call(
+
+    def like(channels):
+        return jax.ShapeDtypeStruct((channels, nx * ny, depth), F32)
+
+    *packed, flow, solute, wide = call(
         functools.partial(pack_kernel, plan, ring, parts),
-        [SMEM] + [ANY] * 6,
-        [jax.ShapeDtypeStruct((plan.sent, 8, depth), F32)] * parts,
+        [SMEM] + [HBM] * 6,
+        [jax.ShapeDtypeStruct((plan.sent, 8, depth), F32)] * parts + [like(NF), like(NS), like(plan.chan - SOLID)],
         "pack_column",
         1 << 22,
-        scratch(steps - 1),
-        60 << 20,
+        [pltpu.VMEM(f.shape, f.dtype) for f in fields[2:]] + [pltpu.SemaphoreType.DMA((8,))],
     )(owner, *fields)
+    loaded = (flow, solute, wide)
     if ring == 2:
         received = [lax.ppermute(packed[0], "gz", [(0, 1), (1, 0)])]
     else:
         received = [move(packed[0], "gz", 1), move(packed[1], "gz", -1)]
 
     slab = [jax.ShapeDtypeStruct((plan.slab, nx, depth), F32)] * 2
-    raw = call(functools.partial(faces_kernel, plan), [ANY] * 7, slab, "faces", 1 << 24, scratch(steps - 1), 24 << 20)(
-        *fields, packed[0]
+    raw = call(functools.partial(faces_kernel, plan), [VMEM] * 3 + [ANY], slab, "faces", 1 << 24)(
+        *loaded, packed[0]
     )
     y_low, y_high = call(
         functools.partial(insert_kernel, plan, ring, parts), [SMEM] + [VMEM] * (2 + parts), slab, "insert", 1 << 22, (), 24 << 20
@@ -547,12 +545,11 @@
     from_y_high = move(y_low, "gy", -1)
     inner, x_low, x_high = call(
         functools.partial(inner_kernel, plan, ring, parts),
-        [SMEM] + [ANY] * 6 + [VMEM] * parts,
+        [SMEM] + [VMEM] * (3 + parts),
         [jax.ShapeDtypeStruct((plan.chan, nx * plan.pitch, depth), F32)] + [jax.ShapeDtypeStruct((plan.slab, ny, depth), F32)] * 2,
         "inner",
         1 << 24,
-        scratch(steps),
-    )(owner, *fields, *received)
+    )(owner, *loaded, *received)
     from_x_low = move(x_high, "gx", 1)
     from_x_high = move(x_low, "gx", -1)
 

time: 76.2 us -> 68.7 us (0.902)
  local copies, waits for them, and re-layouts: 8.89 us -> 0 us
  waiting for transfers between devices: 12.4 us -> 16.5 us
  Pallas kernels: 33.6 us -> 30.2 us
  starting transfers between devices: 19.9 us -> 21 us
    unnamed x26 -> x0, local copies, waits for them, and re-layouts: 8.89 us -> none
    pallas_call x3, Pallas kernels: 13.2 us -> 9.46 us  [the longest x1 4.45 us: per_device(): call(functools.partial(inner_kernel, plan, ring, parts), [SMEM] + [VMEM]...]
    ppermute x1, waiting for transfers between devices: 0.01 us -> 3.44 us  [per_device(): received = [lax.ppermute(packed[0], 'gz', [(0, 1), (1, 0)])]]
    ppermute x6, starting transfers between devices: 17.8 us -> 18.9 us  [move(): lax.ppermute(value, axis, [(i, i + by) for i in range(size) if 0 <= i + b...]
  transfers between devices with their start and end apart: 7 -> 7, of which waited for: 3 -> 4; matrix products, arithmetic and copies ran while one was open for 0% -> 0% of each run, Pallas kernels for 17% -> 16%
where the time goes in v5:
time: 68.7 us; the launch traced here: 68.4 us
  Pallas kernels  30.2 us (44%)
  starting transfers between devices  21 us (31%)
  waiting for transfers between devices  16.5 us (24%)
  between operations  0.75 us (1%)
    ppermute x6, starting transfers between devices, move(): lax.ppermute(value, axis, [(i, i + by) for i in range(size) if 0 <= i + b...  18.9 us
    ppermute x6, waiting for transfers between devices, move(): lax.ppermute(value, axis, [(i, i + by) for i in range(size) if 0 <= i + b...  13.1 us
    pallas_call x1, Pallas kernels, per_device(): call(functools.partial(steps_kernel, plan), [SMEM] + [VMEM] * 6, [jax.Sha...  12.8 us
    pallas_call x1, Pallas kernels, per_device(): call(functools.partial(first_kernel, plan), [SMEM, ANY] + [VMEM] * 4, [st...  5.48 us
    pallas_call x1, Pallas kernels, per_device(): call(functools.partial(inner_kernel, plan, ring, parts), [SMEM] + [VMEM]...  4.45 us
    pallas_call x1, Pallas kernels, per_device(): call(functools.partial(pack_kernel, plan, ring, parts), [SMEM] + [HBM] *...  4.36 us
    ppermute x1, waiting for transfers between devices, per_device(): received = [lax.ppermute(packed[0], 'gz', [(0, 1), (1, 0)])]  3.44 us
    ppermute x1, starting transfers between devices, per_device(): received = [lax.ppermute(packed[0], 'gz', [(0, 1), (1, 0)])]  2.13 us
  transfers between devices with their start and end apart: 7, of which 4 were waited for; matrix products, arithmetic and copies ran while one was open for 0% of the time, Pallas kernels for 16%

profile of v5, /device:TPU:1, one launch (start us, length us, event | category | flops | bytes accessed | tf_op | source)
XLA Modules:
  0.0 68.4 jit_solution(10746111363852357242)
XLA Ops:
  0.6 4.4 %pack_column.1 = (f32[42,8,128]{2,1,0:T(8,128)S(1)}, f32[19,256,128]{2,1,0:T(8,128)S(1)}, f32[7,256,128]{2,1,0:T(8,128)S(1)}, f32[21,256,128]{2,1,0:T(8,128)S(1)}) custom-call(s32[8]{0:T(128)} %owner.9, f32[19,256,128]{2,1,0:T(8,128)} %bitcast.14, f32[7,256,128]{2,1,0:T(8,128)} %bitcast.15, bf16[4,256,128]{2,1,0:T(8,128)(2,1)} %bitcast.17, ...), custom_call_target="tpu_custom_call" | custom-call | flops 4194304 | bytes 8388608 | tf_op jit(solution)/shard_map/pack_column/pallas_call | solution.py:523
  5.0 2.1 %collective-permute-start = (f32[42,8,128]{2,1,0:T(8,128)S(1)}, f32[42,8,128]{2,1,0:T(8,128)S(1)}, u32[]{:S(2)}, u32[]{:S(2)}) collective-permute-start(f32[42,8,128]{2,1,0:T(8,128)S(1)} %get-tuple-element.22.packed), channel_id=1, source_target_pairs={{0,1},{1,0},{2,3},{3,2},{4,5},{5,4},{6,7},{7,6},{8,9},{9,8},{10,11... | collective-permute-start | bytes 516104 | tf_op jit(solution)/shard_map/ppermute | solution.py:533
  7.1 0.7 faces.1
  7.8 3.4 %collective-permute-done.rest_0_ = f32[42,8,128]{2,1,0:T(8,128)S(1)} collective-permute-done((f32[42,8,128]{2,1,0:T(8,128)S(1)}, f32[42,8,128]{2,1,0:T(8,128)S(1)}, u32[]{:S(2)}, u32[]{:S(2)}) %collective-permute-start) | collective-permute-done | bytes 172064 | tf_op jit(solution)/shard_map/ppermute | solution.py:533
  11.2 2.0 %insert.1 = (f32[118,16,128]{2,1,0:T(8,128)S(1)}, f32[118,16,128]{2,1,0:T(8,128)S(1)}) custom-call(s32[8]{0:T(128)} %owner.9, f32[118,16,128]{2,1,0:T(8,128)S(1)} %get-tuple-element.24.low, f32[118,16,128]{2,1,0:T(8,128)S(1)} %get-tuple-element.25.high, f32[42,8,128]{2,1,0:T(8,128)S(1)} %collective-permute-done.rest_0_), custom_call_target="tpu_custom_call" | custom-call | flops 4194304 | bytes 8388608 | tf_op jit(solution)/shard_map/insert/pallas_call | solution.py:541
  13.2 3.2 %collective-permute-start.1 = (f32[118,16,128]{2,1,0:T(8,128)S(1)}, f32[118,16,128]{2,1,0:T(8,128)S(1)}, u32[]{:S(2)}, u32[]{:S(2)}) collective-permute-start(f32[118,16,128]{2,1,0:T(8,128)S(1)} %get-tuple-element.26), channel_id=1, source_target_pairs={{0,2},{2,4},{4,6},{1,3},{3,5},{5,7},{8,10},{10,12},{12,14},{9,11},... | collective-permute-start | bytes 2899976 | tf_op jit(solution)/shard_map/ppermute | solution.py:516
  16.4 1.3 %collective-permute-start.2 = (f32[118,16,128]{2,1,0:T(8,128)S(1)}, f32[118,16,128]{2,1,0:T(8,128)S(1)}, u32[]{:S(2)}, u32[]{:S(2)}) collective-permute-start(f32[118,16,128]{2,1,0:T(8,128)S(1)} %get-tuple-element.27), channel_id=1, source_target_pairs={{2,0},{4,2},{6,4},{3,1},{5,3},{7,5},{10,8},{12,10},{14,12},{11,9},... | collective-permute-start | bytes 2899976 | tf_op jit(solution)/shard_map/ppermute | solution.py:516
  17.7 4.4 %inner.1 = (f32[47,384,128]{2,1,0:T(8,128)S(1)}, f32[118,16,128]{2,1,0:T(8,128)S(1)}, f32[118,16,128]{2,1,0:T(8,128)S(1)}) custom-call(s32[8]{0:T(128)} %owner.9, f32[19,256,128]{2,1,0:T(8,128)S(1)} %get-tuple-element.19.flow, f32[7,256,128]{2,1,0:T(8,128)S(1)} %get-tuple-element.20.solute, f32[21,256,128]{2,1,0:T(8,128)S(1)} %get-tuple-element.21.wide, ...), custom_call_target="tpu_custom_call" | custom-call | flops 16777216 | bytes 8388608 | tf_op jit(solution)/shard_map/inner/pallas_call | solution.py:546
  22.2 4.8 %collective-permute-start.3 = (f32[118,16,128]{2,1,0:T(8,128)S(1)}, f32[118,16,128]{2,1,0:T(8,128)S(1)}, u32[]{:S(2)}, u32[]{:S(2)}) collective-permute-start(f32[118,16,128]{2,1,0:T(8,128)S(1)} %get-tuple-element.28), channel_id=1, source_target_pairs={{0,8},{8,16},{16,24},{1,9},{9,17},{17,25},{2,10},{10,18},{18,26},{... | collective-permute-start | bytes 2899976 | tf_op jit(solution)/shard_map/ppermute | solution.py:516
  27.0 1.9 %collective-permute-start.4 = (f32[118,16,128]{2,1,0:T(8,128)S(1)}, f32[118,16,128]{2,1,0:T(8,128)S(1)}, u32[]{:S(2)}, u32[]{:S(2)}) collective-permute-start(f32[118,16,128]{2,1,0:T(8,128)S(1)} %get-tuple-element.29), channel_id=1, source_target_pairs={{8,0},{16,8},{24,16},{9,1},{17,9},{25,17},{10,2},{18,10},{26,18},{... | collective-permute-start | bytes 2899976 | tf_op jit(solution)/shard_map/ppermute | solution.py:516
  28.9 6.5 %collective-permute-done.1.y_low = f32[118,16,128]{2,1,0:T(8,128)S(1)} collective-permute-done((f32[118,16,128]{2,1,0:T(8,128)S(1)}, f32[118,16,128]{2,1,0:T(8,128)S(1)}, u32[]{:S(2)}, u32[]{:S(2)}) %collective-permute-start.1) | collective-permute-done | bytes 966688 | tf_op jit(solution)/shard_map/ppermute | solution.py:516
  35.5 3.9 %collective-permute-done.2.y_high = f32[118,16,128]{2,1,0:T(8,128)S(1)} collective-permute-done((f32[118,16,128]{2,1,0:T(8,128)S(1)}, f32[118,16,128]{2,1,0:T(8,128)S(1)}, u32[]{:S(2)}, u32[]{:S(2)}) %collective-permute-start.2) | collective-permute-done | bytes 966688 | tf_op jit(solution)/shard_map/ppermute | solution.py:516
  39.4 0.4 corners.1
  39.8 5.8 %collective-permute-start.5 = (f32[944,128]{1,0:T(8,128)S(1)}, f32[944,128]{1,0:T(8,128)S(1)}, u32[]{:S(2)}, u32[]{:S(2)}) collective-permute-start(f32[944,128]{1,0:T(8,128)S(1)} %get-tuple-element.34), channel_id=1, source_target_pairs={{0,8},{8,16},{16,24},{1,9},{9,17},{17,25},{2,10},{10,18},{18,26},{... | collective-permute-start | bytes 1449992 | tf_op jit(solution)/shard_map/ppermute | solution.py:516
  45.5 1.9 %collective-permute-start.6 = (f32[944,128]{1,0:T(8,128)S(1)}, f32[944,128]{1,0:T(8,128)S(1)}, u32[]{:S(2)}, u32[]{:S(2)}) collective-permute-start(f32[944,128]{1,0:T(8,128)S(1)} %get-tuple-element.35), channel_id=1, source_target_pairs={{8,0},{16,8},{24,16},{9,1},{17,9},{25,17},{10,2},{18,10},{26,18},{... | collective-permute-start | bytes 1449992 | tf_op jit(solution)/shard_map/ppermute | solution.py:516
  47.5 0.0 collective-permute-done.3.x_low
  47.5 0.0 collective-permute-done.4.x_high
  47.5 5.5 %first.1 = (f32[26,592,128]{2,1,0:T(8,128)S(1)}, f32[21,592,128]{2,1,0:T(8,128)S(1)}, f32[26,592,128]{2,1,0:T(8,128)S(1)}, f32[3,592,128]{2,1,0:T(8,128)S(1)}) custom-call(s32[8]{0:T(128)} %owner.9, f32[47,384,128]{2,1,0:T(8,128)S(1)} %get-tuple-element.23.inner, f32[118,16,128]{2,1,0:T(8,128)S(1)} %collective-permute-done.1.y_low, ...), custom_call_target="tpu_custom_call" | custom-call | flops 67108864 | bytes 8388608 | tf_op jit(solution)/shard_map/first/pallas_call | solution.py:568
  53.0 0.0 collective-permute-done.5
  53.0 2.6 %collective-permute-done.6 = f32[944,128]{1,0:T(8,128)S(1)} collective-permute-done((f32[944,128]{1,0:T(8,128)S(1)}, f32[944,128]{1,0:T(8,128)S(1)}, u32[]{:S(2)}, u32[]{:S(2)}) %collective-permute-start.6) | collective-permute-done | bytes 483360 | tf_op jit(solution)/shard_map/ppermute | solution.py:516
  55.6 12.8 %steps.1 = (f32[19,16,16,128]{3,2,1,0:T(8,128)}, f32[7,16,16,128]{3,2,1,0:T(8,128)}) custom-call(s32[8]{0:T(128)} %owner.9, f32[26,592,128]{2,1,0:T(8,128)S(1)} %get-tuple-element.30.cells, f32[21,592,128]{2,1,0:T(8,128)S(1)} %get-tuple-element.31.fields, f32[26,592,128]{2,1,0:T(8,128)S(1)} %get-tuple-element.32.other, ...), custom_call_target="tpu_custom_call" | custom-call | flops 268435456 | bytes 8388608 | tf_op jit(solution)/shard_map/steps/pallas_call | solution.py:582
Async XLA Ops:
  5.0 6.2 %collective-permute-start = (f32[42,8,128]{2,1,0:T(8,128)S(1)}, f32[42,8,128]{2,1,0:T(8,128)S(1)}, u32[]{:S(2)}, u32[]{:S(2)}) collective-permute-start(f32[42,8,128]{2,1,0:T(8,128)S(1)} %get-tuple-element.22.packed), channel_id=1, source_target_pairs={{0,1},{1,0},{2,3},{3,2},{4,5},{5,4},{6,7},{7,6},{8,9},{9,8},{10,11... | collective-permute-start | bytes 516104 | tf_op jit(solution)/shard_map/ppermute | solution.py:533
  13.2 22.2 %collective-permute-start.1 = (f32[118,16,128]{2,1,0:T(8,128)S(1)}, f32[118,16,128]{2,1,0:T(8,128)S(1)}, u32[]{:S(2)}, u32[]{:S(2)}) collective-permute-start(f32[118,16,128]{2,1,0:T(8,128)S(1)} %get-tuple-element.26), channel_id=1, source_target_pairs={{0,2},{2,4},{4,6},{1,3},{3,5},{5,7},{8,10},{10,12},{12,14},{9,11},... | collective-permute-start | bytes 2899976 | tf_op jit(solution)/shard_map/ppermute | solution.py:516
  16.4 23.0 %collective-permute-start.2 = (f32[118,16,128]{2,1,0:T(8,128)S(1)}, f32[118,16,128]{2,1,0:T(8,128)S(1)}, u32[]{:S(2)}, u32[]{:S(2)}) collective-permute-start(f32[118,16,128]{2,1,0:T(8,128)S(1)} %get-tuple-element.27), channel_id=1, source_target_pairs={{2,0},{4,2},{6,4},{3,1},{5,3},{7,5},{10,8},{12,10},{14,12},{11,9},... | collective-permute-start | bytes 2899976 | tf_op jit(solution)/shard_map/ppermute | solution.py:516
  22.2 25.3 %collective-permute-start.3 = (f32[118,16,128]{2,1,0:T(8,128)S(1)}, f32[118,16,128]{2,1,0:T(8,128)S(1)}, u32[]{:S(2)}, u32[]{:S(2)}) collective-permute-start(f32[118,16,128]{2,1,0:T(8,128)S(1)} %get-tuple-element.28), channel_id=1, source_target_pairs={{0,8},{8,16},{16,24},{1,9},{9,17},{17,25},{2,10},{10,18},{18,26},{... | collective-permute-start | bytes 2899976 | tf_op jit(solution)/shard_map/ppermute | solution.py:516
  27.0 20.5 %collective-permute-start.4 = (f32[118,16,128]{2,1,0:T(8,128)S(1)}, f32[118,16,128]{2,1,0:T(8,128)S(1)}, u32[]{:S(2)}, u32[]{:S(2)}) collective-permute-start(f32[118,16,128]{2,1,0:T(8,128)S(1)} %get-tuple-element.29), channel_id=1, source_target_pairs={{8,0},{16,8},{24,16},{9,1},{17,9},{25,17},{10,2},{18,10},{26,18},{... | collective-permute-start | bytes 2899976 | tf_op jit(solution)/shard_map/ppermute | solution.py:516
  39.8 13.2 %collective-permute-start.5 = (f32[944,128]{1,0:T(8,128)S(1)}, f32[944,128]{1,0:T(8,128)S(1)}, u32[]{:S(2)}, u32[]{:S(2)}) collective-permute-start(f32[944,128]{1,0:T(8,128)S(1)} %get-tuple-element.34), channel_id=1, source_target_pairs={{0,8},{8,16},{16,24},{1,9},{9,17},{17,25},{2,10},{10,18},{18,26},{... | collective-permute-start | bytes 1449992 | tf_op jit(solution)/shard_map/ppermute | solution.py:516
  45.5 10.1 %collective-permute-start.6 = (f32[944,128]{1,0:T(8,128)S(1)}, f32[944,128]{1,0:T(8,128)S(1)}, u32[]{:S(2)}, u32[]{:S(2)}) collective-permute-start(f32[944,128]{1,0:T(8,128)S(1)} %get-tuple-element.35), channel_id=1, source_target_pairs={{8,0},{16,8},{24,16},{9,1},{17,9},{25,17},{10,2},{18,10},{26,18},{... | collective-permute-start | bytes 1449992 | tf_op jit(solution)/shard_map/ppermute | solution.py:516

commit v6 on v5

--- a/solution.py
+++ b/solution.py
@@ -41,6 +41,7 @@
 langmuir_rate = 0.05
 VMEM_LIMIT = 24 << 20
 F32 = jnp.float32
+PAD = 8
 
 
 class Plan:
@@ -51,6 +52,10 @@
         self.sent = AUX + NA * (steps - 1)
         self.pitch = -(-(ny + 2 * w) // 8) * 8
         self.wide = nx + 2 * w
+        self.height = self.wide * self.pitch + 2 * PAD
+        self.tiles = list(range(self.pitch // 8))
+        self.inside = [h for h in self.tiles if 8 * h > w and 8 * h + 8 < w + ny]
+        self.outside = [h for h in self.tiles if h not in self.inside]
         self.count = {k: AUX + NA * (steps - k) for k in range(1, w)}
         self.base, at = {}, 0
         for k in range(1, w):
@@ -220,37 +225,49 @@
 
 
 def inner_kernel(plan, ring, parts, owner, flow, solute, wide, *rest):
-    received, (out, x_low, x_high) = rest[:parts], rest[parts:]
+    received, (cells, fields, x_low, x_high) = rest[:parts], rest[parts:]
     w, nx, ny, pitch = plan.halo, plan.nx, plan.ny, plan.pitch
     put = column(plan, ring, owner, received)
-    for at, number, ref in ((0, NF, flow), (NF, NS, solute), (SOLID, plan.chan - SOLID, wide)):
-
-        def one(i, sent=True, at=at, ref=ref):
+    for at, number, ref, out, to in (
+        (0, NF, flow, cells, 0),
+        (NF, NS, solute, cells, NF),
+        (SOLID, plan.chan - SOLID, wide, fields, 0),
+    ):
+
+        def one(i, sent=True, at=at, ref=ref, out=out, to=to):
             slabs = [r[at + i] for r in received] if sent else []
             for n, y, x in tiles_of(plan):
                 tile = ref[i, pl.ds(x * ny + y, 8, stride=ny), :]
-                out[at + i, pl.ds(x * pitch + w + y, 8, stride=pitch), :] = put(tile, slabs, n)
+                out[to + i, pl.ds(PAD + (w + x) * pitch + w + y, 8, stride=pitch), :] = put(tile, slabs, n)
 
         within = min(number, plan.sent - at)
         each(within, one, 3)
         each(number - within, lambda i, one=one, within=within: one(within + i, False), 1)
 
-    def row(c, x):
-        return out[c, x * pitch + w : x * pitch + w + ny, :]
+    def row(ref, c, x):
+        at = PAD + (w + x) * pitch + w
+        return ref[c, at : at + ny, :]
 
     for k in range(1, w):
 
-        def both(c, k=k):
-            x_low[plan.base[k] + c] = row(c, k - 1)
-            x_high[plan.base[k] + c] = row(c, nx - k)
-
-        each(plan.count[k], both)
+        def both(ref, c, j, k=k):
+            x_low[plan.base[k] + j] = row(ref, c, k - 1)
+            x_high[plan.base[k] + j] = row(ref, c, nx - k)
+
+        channels(cells, fields, plan.count[k], both)
     for slab, sign, x in ((x_low, 1, w - 1), (x_high, -1, nx - w)):
         for j, c in enumerate(plan.last(0, sign)):
-            slab[plan.base[w] + j] = row(c, x)
-
-
-def corners_kernel(plan, from_low, from_high, inner, low, high):
+            ref, at = (cells, c) if c < SOLID else (fields, c - SOLID)
+            slab[plan.base[w] + j] = row(ref, at, x)
+
+
+def middle_kernel(plan, owner, cells, fields, other, masks):
+    w, nx = plan.halo, plan.nx
+    prepare(plan, owner, fields, masks, w, w + nx)
+    sweep(plan, owner, cells, other, fields, masks, 0, w + 1, w + nx - 1, plan.inside)
+
+
+def corners_kernel(plan, from_low, from_high, masks, low, high):
     w, nx, ny = plan.halo, plan.nx, plan.ny
     low[...] = jnp.zeros(low.shape, F32)
     high[...] = jnp.zeros(high.shape, F32)
@@ -276,9 +293,6 @@
                         out[to * tall + row : to * tall + row + 1, :] = source[at * nx + x : at * nx + x + 1, :]
 
 
-PAD = 8
-
-
 def channels(cells, fields, number, body):
     each(SOLID, lambda c: body(cells, c, c))
     each(number - SOLID, lambda c: body(fields, c, SOLID + c))
@@ -301,23 +315,15 @@
                 put(ref, at, part, plan.base[w] + j, k, sign)
 
 
-def first_kernel(plan, owner, inner, y_low, y_high, x_low, x_high, cells, fields, other, masks, sems):
+def first_kernel(plan, owner, y_low, y_high, x_low, x_high, *refs):
+    cells, fields, other, masks = refs[4:]
     w, nx, ny, pitch = plan.halo, plan.nx, plan.ny, plan.pitch
-    middle = pl.ds(PAD + w * pitch, nx * pitch)
-    copies = [
-        pltpu.make_async_copy(inner.at[pl.ds(0, SOLID)], cells.at[:, middle, :], sems.at[0]),
-        pltpu.make_async_copy(inner.at[pl.ds(SOLID, plan.chan - SOLID)], fields.at[:, middle, :], sems.at[1]),
-    ]
-    for copy in copies:
-        copy.start()
 
     def put_x(ref, c, part, j, k, sign):
         row = PAD + (w - k if sign < 0 else w + nx - 1 + k) * pitch + w
         ref[c, row : row + ny, :] = part[j]
 
     insert_layers(plan, cells, fields, 0, (x_low, x_high), put_x)
-    for copy in copies:
-        copy.wait()
 
     def put_y(ref, c, part, j, m, sign):
         row = PAD + w * pitch + (w - m if sign < 0 else w + ny - 1 + m)
@@ -325,10 +331,10 @@
 
     insert_layers(plan, cells, fields, 1, (y_low, y_high), put_y)
     prepare(plan, owner, fields, masks, w, w + nx)
-    sweep(plan, owner, cells, other, fields, masks, 0, w + 1, w + nx - 1)
-
-
-def steps_kernel(plan, owner, cells, fields, other, masks, c_low, c_high, flow_out, solute_out):
+    sweep(plan, owner, cells, other, fields, masks, 0, w + 1, w + nx - 1, plan.outside)
+
+
+def steps_kernel(plan, owner, cells, fields, other, masks, c_low, c_high, flow_hbm, solute_hbm, flow_out, solute_out, sems):
     w, nx, ny, pitch = plan.halo, plan.nx, plan.ny, plan.pitch
 
     def put(ref, c, part, j, k, sign):
@@ -347,6 +353,12 @@
     s = plan.steps - 1
     source = buffers[s % 2]
 
+    def leave(x):
+        return [
+            pltpu.make_async_copy(ref.at[:, x], to.at[:, x], sems.at[n, x])
+            for n, (ref, to) in enumerate(((flow_out, flow_hbm), (solute_out, solute_hbm)))
+        ]
+
     def last(x, carry):
         for h in range(ny // 8):
             row = PAD + (x + w) * pitch + w + 8 * h
@@ -358,9 +370,14 @@
                     solute_out[c - NF, x, 8 * h : 8 * h + 8, :] = value
 
             advance(plan, owner, source, fields, masks, s, row, write)
+        for copy in leave(x):
+            copy.start()
         return carry
 
     lax.fori_loop(0, nx, last, 0)
+    for x in range(nx):
+        for copy in leave(x):
+            copy.wait()
 
 
 def prepare(plan, owner, fields, masks, from_x, to_x):
@@ -393,11 +410,11 @@
     lax.fori_loop(from_x, to_x, one, 0)
 
 
-def sweep(plan, owner, source, target, fields, masks, s, from_x, to_x):
+def sweep(plan, owner, source, target, fields, masks, s, from_x, to_x, tiles=None):
     pitch = plan.pitch
 
     def body(x, carry):
-        for h in range(pitch // 8):
+        for h in tiles or plan.tiles:
             row = pl.multiple_of(PAD + pitch * x + 8 * h, 8)
 
             def write(c, value, row=row):
@@ -488,12 +505,13 @@
 HBM = pl.BlockSpec(memory_space=pltpu.HBM)
 
 
-def call(kernel, ins, outs, name, cost, scratch=(), limit=VMEM_LIMIT):
+def call(kernel, ins, outs, name, cost, scratch=(), limit=VMEM_LIMIT, place=VMEM, aliases={}):
     return pl.pallas_call(
         kernel,
         in_specs=ins,
         out_shape=outs,
-        out_specs=[VMEM] * len(outs),
+        out_specs=[place] * len(outs),
+        input_output_aliases=aliases,
         scratch_shapes=list(scratch),
         name=name,
         cost_estimate=pl.CostEstimate(flops=cost, bytes_accessed=1 << 23, transcendentals=0),
@@ -543,15 +561,21 @@
     )(owner, *raw, *received)
     from_y_low = move(y_high, "gy", 1)
     from_y_high = move(y_low, "gy", -1)
-    inner, x_low, x_high = call(
+    state = jax.ShapeDtypeStruct((SOLID, plan.height, depth), F32)
+    saved = jax.ShapeDtypeStruct((plan.chan - SOLID, plan.height, depth), F32)
+    flags = jax.ShapeDtypeStruct((3, plan.height, depth), F32)
+    cells, kept, x_low, x_high = call(
         functools.partial(inner_kernel, plan, ring, parts),
         [SMEM] + [VMEM] * (3 + parts),
-        [jax.ShapeDtypeStruct((plan.chan, nx * plan.pitch, depth), F32)] + [jax.ShapeDtypeStruct((plan.slab, ny, depth), F32)] * 2,
+        [state, saved] + [jax.ShapeDtypeStruct((plan.slab, ny, depth), F32)] * 2,
         "inner",
         1 << 24,
     )(owner, *loaded, *received)
     from_x_low = move(x_high, "gx", 1)
     from_x_high = move(x_low, "gx", -1)
+    other, masks = call(
+        functools.partial(middle_kernel, plan), [SMEM] + [VMEM] * 2, [state, flags], "middle", 1 << 24, (), 8 << 20
+    )(owner, cells, kept)
 
     def rows(value):
         return value.reshape(-1, depth)
@@ -559,35 +583,35 @@
     corner = jax.ShapeDtypeStruct((plan.slab * 2 * w, depth), F32)
     c_low, c_high = call(
         functools.partial(corners_kernel, plan), [VMEM] * 2 + [ANY], [corner, corner], "corners", 1 << 20
-    )(rows(from_y_low), rows(from_y_high), inner)
+    )(rows(from_y_low), rows(from_y_high), masks)
     shape = (plan.slab, 2 * w, depth)
     from_c_low = move(c_high, "gx", 1).reshape(shape)
     from_c_high = move(c_low, "gx", -1).reshape(shape)
-    height = plan.wide * plan.pitch + 2 * PAD
-    state = jax.ShapeDtypeStruct((SOLID, height, depth), F32)
-    wide = call(
+    assembled = [pltpu.with_memory_space_constraint(a, pltpu.VMEM) for a in (cells, kept, other, masks)]
+    assembled = call(
         functools.partial(first_kernel, plan),
-        [SMEM, ANY] + [VMEM] * 4,
-        [
-            state,
-            jax.ShapeDtypeStruct((plan.chan - SOLID, height, depth), F32),
-            state,
-            jax.ShapeDtypeStruct((3, height, depth), F32),
-        ],
+        [SMEM] + [VMEM] * 8,
+        [state, saved, state, flags],
         "first",
         1 << 26,
-        [pltpu.SemaphoreType.DMA((2,))],
+        (),
         8 << 20,
-    )(owner, inner, from_y_low, from_y_high, from_x_low, from_x_high)
+        aliases={5: 0, 6: 1, 7: 2, 8: 3},
+    )(owner, from_y_low, from_y_high, from_x_low, from_x_high, *assembled)
     flow, solute = call(
         functools.partial(steps_kernel, plan),
         [SMEM] + [VMEM] * 6,
         [jax.ShapeDtypeStruct(flow_adjoint.shape, F32), jax.ShapeDtypeStruct(solute_adjoint.shape, F32)],
         "steps",
         1 << 28,
-        (),
+        [
+            pltpu.VMEM((NF, nx, ny, depth), F32),
+            pltpu.VMEM((NS, nx, ny, depth), F32),
+            pltpu.SemaphoreType.DMA((2, nx)),
+        ],
         10 << 20,
-    )(owner, *wide, from_c_low, from_c_high)
+        ANY,
+    )(owner, *assembled, from_c_low, from_c_high)
     return (flow, solute)
 
 

time: 68.7 us -> 67.9 us (0.988)
  waiting for transfers between devices: 16.5 us -> 14.3 us
  Pallas kernels: 30.2 us -> 31.5 us
    pallas_call x1 -> x2, Pallas kernels: 5.48 us -> 7.72 us  [the longest x1 4.46 us: per_device(): call(functools.partial(first_kernel, plan), [SMEM] + [VMEM] * 8, [state,...]
    ppermute x6, waiting for transfers between devices: 13.1 us -> 10.9 us  [move(): lax.ppermute(value, axis, [(i, i + by) for i in range(size) if 0 <= i + b...]
    pallas_call x1, Pallas kernels: 12.8 us -> 11.9 us  [per_device(): call(functools.partial(steps_kernel, plan), [SMEM] + [VMEM] * 6, [jax.Sha...]
  transfers between devices with their start and end apart: 7 -> 7, of which waited for: 4 -> 4; matrix products, arithmetic and copies ran while one was open for 0% -> 0% of each run, Pallas kernels for 16% -> 19%
where the time goes in v6:
time: 67.9 us; the launch traced here: 67.6 us
  Pallas kernels  31.5 us (46%)
  starting transfers between devices  21 us (31%)
  waiting for transfers between devices  14.3 us (21%)
  between operations  0.76 us (1%)
    ppermute x6, starting transfers between devices, move(): lax.ppermute(value, axis, [(i, i + by) for i in range(size) if 0 <= i + b...  18.9 us
    pallas_call x1, Pallas kernels, per_device(): call(functools.partial(steps_kernel, plan), [SMEM] + [VMEM] * 6, [jax.Sha...  11.9 us
    ppermute x6, waiting for transfers between devices, move(): lax.ppermute(value, axis, [(i, i + by) for i in range(size) if 0 <= i + b...  10.9 us
    pallas_call x1, Pallas kernels, per_device(): call(functools.partial(first_kernel, plan), [SMEM] + [VMEM] * 8, [state,...  4.46 us
    pallas_call x1, Pallas kernels, per_device(): call(functools.partial(inner_kernel, plan, ring, parts), [SMEM] + [VMEM]...  4.4 us
    pallas_call x1, Pallas kernels, per_device(): call(functools.partial(pack_kernel, plan, ring, parts), [SMEM] + [HBM] *...  4.36 us
    ppermute x1, waiting for transfers between devices, per_device(): received = [lax.ppermute(packed[0], 'gz', [(0, 1), (1, 0)])]  3.44 us
    pallas_call x1, Pallas kernels, per_device(): call(functools.partial(middle_kernel, plan), [SMEM] + [VMEM] * 2, [state,...  3.26 us
  transfers between devices with their start and end apart: 7, of which 4 were waited for; matrix products, arithmetic and copies ran while one was open for 0% of the time, Pallas kernels for 19%

profile of v6, /device:TPU:1, one launch (start us, length us, event | category | flops | bytes accessed | tf_op | source)
XLA Modules:
  0.0 67.6 jit_solution(5811179991314890131)
XLA Ops:
  0.6 4.4 %pack_column.1 = (f32[42,8,128]{2,1,0:T(8,128)S(1)}, f32[19,256,128]{2,1,0:T(8,128)S(1)}, f32[7,256,128]{2,1,0:T(8,128)S(1)}, f32[21,256,128]{2,1,0:T(8,128)S(1)}) custom-call(s32[8]{0:T(128)} %owner.11, f32[19,256,128]{2,1,0:T(8,128)} %bitcast.14, f32[7,256,128]{2,1,0:T(8,128)} %bitcast.15, bf16[4,256,128]{2,1,0:T(8,128)(2,1)} %bitcast.17, ...), custom_call_target="tpu_custom_call" | custom-call | flops 4194304 | bytes 8388608 | tf_op jit(solution)/shard_map/pack_column/pallas_call | solution.py:541
  5.0 2.1 %collective-permute-start = (f32[42,8,128]{2,1,0:T(8,128)S(1)}, f32[42,8,128]{2,1,0:T(8,128)S(1)}, u32[]{:S(2)}, u32[]{:S(2)}) collective-permute-start(f32[42,8,128]{2,1,0:T(8,128)S(1)} %get-tuple-element.25.packed), channel_id=1, source_target_pairs={{0,1},{1,0},{2,3},{3,2},{4,5},{5,4},{6,7},{7,6},{8,9},{9,8},{10,11... | collective-permute-start | bytes 516104 | tf_op jit(solution)/shard_map/ppermute | solution.py:551
  7.1 0.7 faces.1
  7.8 3.4 %collective-permute-done.rest_0_ = f32[42,8,128]{2,1,0:T(8,128)S(1)} collective-permute-done((f32[42,8,128]{2,1,0:T(8,128)S(1)}, f32[42,8,128]{2,1,0:T(8,128)S(1)}, u32[]{:S(2)}, u32[]{:S(2)}) %collective-permute-start) | collective-permute-done | bytes 172064 | tf_op jit(solution)/shard_map/ppermute | solution.py:551
  11.2 2.0 %insert.1 = (f32[118,16,128]{2,1,0:T(8,128)S(1)}, f32[118,16,128]{2,1,0:T(8,128)S(1)}) custom-call(s32[8]{0:T(128)} %owner.11, f32[118,16,128]{2,1,0:T(8,128)S(1)} %get-tuple-element.26.low, f32[118,16,128]{2,1,0:T(8,128)S(1)} %get-tuple-element.27.high, f32[42,8,128]{2,1,0:T(8,128)S(1)} %collective-permute-done.rest_0_), custom_call_target="tpu_custom_call" | custom-call | flops 4194304 | bytes 8388608 | tf_op jit(solution)/shard_map/insert/pallas_call | solution.py:559
  13.2 3.2 %collective-permute-start.1 = (f32[118,16,128]{2,1,0:T(8,128)S(1)}, f32[118,16,128]{2,1,0:T(8,128)S(1)}, u32[]{:S(2)}, u32[]{:S(2)}) collective-permute-start(f32[118,16,128]{2,1,0:T(8,128)S(1)} %get-tuple-element.28), channel_id=1, source_target_pairs={{0,2},{2,4},{4,6},{1,3},{3,5},{5,7},{8,10},{10,12},{12,14},{9,11},... | collective-permute-start | bytes 2899976 | tf_op jit(solution)/shard_map/ppermute | solution.py:534
  16.4 1.3 %collective-permute-start.2 = (f32[118,16,128]{2,1,0:T(8,128)S(1)}, f32[118,16,128]{2,1,0:T(8,128)S(1)}, u32[]{:S(2)}, u32[]{:S(2)}) collective-permute-start(f32[118,16,128]{2,1,0:T(8,128)S(1)} %get-tuple-element.29), channel_id=1, source_target_pairs={{2,0},{4,2},{6,4},{3,1},{5,3},{7,5},{10,8},{12,10},{14,12},{11,9},... | collective-permute-start | bytes 2899976 | tf_op jit(solution)/shard_map/ppermute | solution.py:534
  17.7 4.4 %inner.1 = (f32[26,592,128]{2,1,0:T(8,128)S(1)}, f32[21,592,128]{2,1,0:T(8,128)S(1)}, f32[118,16,128]{2,1,0:T(8,128)S(1)}, f32[118,16,128]{2,1,0:T(8,128)S(1)}) custom-call(s32[8]{0:T(128)} %owner.11, f32[19,256,128]{2,1,0:T(8,128)S(1)} %get-tuple-element.22.flow, f32[7,256,128]{2,1,0:T(8,128)S(1)} %get-tuple-element.23.solute, ...), custom_call_target="tpu_custom_call" | custom-call | flops 16777216 | bytes 8388608 | tf_op jit(solution)/shard_map/inner/pallas_call | solution.py:567
  22.1 4.8 %collective-permute-start.3 = (f32[118,16,128]{2,1,0:T(8,128)S(1)}, f32[118,16,128]{2,1,0:T(8,128)S(1)}, u32[]{:S(2)}, u32[]{:S(2)}) collective-permute-start(f32[118,16,128]{2,1,0:T(8,128)S(1)} %get-tuple-element.30), channel_id=1, source_target_pairs={{0,8},{8,16},{16,24},{1,9},{9,17},{17,25},{2,10},{10,18},{18,26},{... | collective-permute-start | bytes 2899976 | tf_op jit(solution)/shard_map/ppermute | solution.py:534
  27.0 1.9 %collective-permute-start.4 = (f32[118,16,128]{2,1,0:T(8,128)S(1)}, f32[118,16,128]{2,1,0:T(8,128)S(1)}, u32[]{:S(2)}, u32[]{:S(2)}) collective-permute-start(f32[118,16,128]{2,1,0:T(8,128)S(1)} %get-tuple-element.31), channel_id=1, source_target_pairs={{8,0},{16,8},{24,16},{9,1},{17,9},{25,17},{10,2},{18,10},{26,18},{... | collective-permute-start | bytes 2899976 | tf_op jit(solution)/shard_map/ppermute | solution.py:534
  28.9 3.3 %middle.1 = (f32[26,592,128]{2,1,0:T(8,128)S(1)}, f32[3,592,128]{2,1,0:T(8,128)S(1)}) custom-call(s32[8]{0:T(128)} %owner.11, f32[26,592,128]{2,1,0:T(8,128)S(1)} %get-tuple-element.32.cells.refs_0_, f32[21,592,128]{2,1,0:T(8,128)S(1)} %get-tuple-element.33.fields.refs_1_), custom_call_target="tpu_custom_call" | custom-call | flops 16777216 | bytes 8388608 | tf_op jit(solution)/shard_map/middle/pallas_call | solution.py:576
  32.2 3.3 %collective-permute-done.1.y_low = f32[118,16,128]{2,1,0:T(8,128)S(1)} collective-permute-done((f32[118,16,128]{2,1,0:T(8,128)S(1)}, f32[118,16,128]{2,1,0:T(8,128)S(1)}, u32[]{:S(2)}, u32[]{:S(2)}) %collective-permute-start.1) | collective-permute-done | bytes 966688 | tf_op jit(solution)/shard_map/ppermute | solution.py:534
  35.5 3.9 %collective-permute-done.2.y_high = f32[118,16,128]{2,1,0:T(8,128)S(1)} collective-permute-done((f32[118,16,128]{2,1,0:T(8,128)S(1)}, f32[118,16,128]{2,1,0:T(8,128)S(1)}, u32[]{:S(2)}, u32[]{:S(2)}) %collective-permute-start.2) | collective-permute-done | bytes 966688 | tf_op jit(solution)/shard_map/ppermute | solution.py:534
  39.4 0.4 corners.1
  39.8 5.8 %collective-permute-start.5 = (f32[944,128]{1,0:T(8,128)S(1)}, f32[944,128]{1,0:T(8,128)S(1)}, u32[]{:S(2)}, u32[]{:S(2)}) collective-permute-start(f32[944,128]{1,0:T(8,128)S(1)} %get-tuple-element.40), channel_id=1, source_target_pairs={{0,8},{8,16},{16,24},{1,9},{9,17},{17,25},{2,10},{10,18},{18,26},{... | collective-permute-start | bytes 1449992 | tf_op jit(solution)/shard_map/ppermute | solution.py:534
  45.5 1.9 %collective-permute-start.6 = (f32[944,128]{1,0:T(8,128)S(1)}, f32[944,128]{1,0:T(8,128)S(1)}, u32[]{:S(2)}, u32[]{:S(2)}) collective-permute-start(f32[944,128]{1,0:T(8,128)S(1)} %get-tuple-element.41), channel_id=1, source_target_pairs={{8,0},{16,8},{24,16},{9,1},{17,9},{25,17},{10,2},{18,10},{26,18},{... | collective-permute-start | bytes 1449992 | tf_op jit(solution)/shard_map/ppermute | solution.py:534
  47.5 0.0 collective-permute-done.3.x_low
  47.5 0.0 collective-permute-done.4.x_high
  47.5 4.5 %first.1 = (f32[26,592,128]{2,1,0:T(8,128)S(1)}, f32[21,592,128]{2,1,0:T(8,128)S(1)}, f32[26,592,128]{2,1,0:T(8,128)S(1)}, f32[3,592,128]{2,1,0:T(8,128)S(1)}) custom-call(s32[8]{0:T(128)} %owner.11, f32[118,16,128]{2,1,0:T(8,128)S(1)} %collective-permute-done.1.y_low, ...), custom_call_target="tpu_custom_call", output_to_operand_aliasing={{0}: (5, {}), {1}: (6, {}), {2}: (7, {}), {3}: (8, {})} | custom-call | flops 67108864 | bytes 8388608 | tf_op jit(solution)/shard_map/first/pallas_call | solution.py:591
  52.0 0.0 collective-permute-done.5
  52.0 3.6 %collective-permute-done.6 = f32[944,128]{1,0:T(8,128)S(1)} collective-permute-done((f32[944,128]{1,0:T(8,128)S(1)}, f32[944,128]{1,0:T(8,128)S(1)}, u32[]{:S(2)}, u32[]{:S(2)}) %collective-permute-start.6) | collective-permute-done | bytes 483360 | tf_op jit(solution)/shard_map/ppermute | solution.py:534
  55.6 11.9 %steps.1 = (f32[19,16,16,128]{3,2,1,0:T(8,128)}, f32[7,16,16,128]{3,2,1,0:T(8,128)}) custom-call(s32[8]{0:T(128)} %owner.11, f32[26,592,128]{2,1,0:T(8,128)S(1)} %get-tuple-element.36.cells, f32[21,592,128]{2,1,0:T(8,128)S(1)} %get-tuple-element.37.fields, f32[26,592,128]{2,1,0:T(8,128)S(1)} %get-tuple-element.38.other, ...), custom_call_target="tpu_custom_call" | custom-call | flops 268435456 | bytes 8388608 | tf_op jit(solution)/shard_map/steps/pallas_call | solution.py:601
Async XLA Ops:
  5.0 6.2 %collective-permute-start = (f32[42,8,128]{2,1,0:T(8,128)S(1)}, f32[42,8,128]{2,1,0:T(8,128)S(1)}, u32[]{:S(2)}, u32[]{:S(2)}) collective-permute-start(f32[42,8,128]{2,1,0:T(8,128)S(1)} %get-tuple-element.25.packed), channel_id=1, source_target_pairs={{0,1},{1,0},{2,3},{3,2},{4,5},{5,4},{6,7},{7,6},{8,9},{9,8},{10,11... | collective-permute-start | bytes 516104 | tf_op jit(solution)/shard_map/ppermute | solution.py:551
  13.2 22.2 %collective-permute-start.1 = (f32[118,16,128]{2,1,0:T(8,128)S(1)}, f32[118,16,128]{2,1,0:T(8,128)S(1)}, u32[]{:S(2)}, u32[]{:S(2)}) collective-permute-start(f32[118,16,128]{2,1,0:T(8,128)S(1)} %get-tuple-element.28), channel_id=1, source_target_pairs={{0,2},{2,4},{4,6},{1,3},{3,5},{5,7},{8,10},{10,12},{12,14},{9,11},... | collective-permute-start | bytes 2899976 | tf_op jit(solution)/shard_map/ppermute | solution.py:534
  16.4 23.0 %collective-permute-start.2 = (f32[118,16,128]{2,1,0:T(8,128)S(1)}, f32[118,16,128]{2,1,0:T(8,128)S(1)}, u32[]{:S(2)}, u32[]{:S(2)}) collective-permute-start(f32[118,16,128]{2,1,0:T(8,128)S(1)} %get-tuple-element.29), channel_id=1, source_target_pairs={{2,0},{4,2},{6,4},{3,1},{5,3},{7,5},{10,8},{12,10},{14,12},{11,9},... | collective-permute-start | bytes 2899976 | tf_op jit(solution)/shard_map/ppermute | solution.py:534
  22.1 25.4 %collective-permute-start.3 = (f32[118,16,128]{2,1,0:T(8,128)S(1)}, f32[118,16,128]{2,1,0:T(8,128)S(1)}, u32[]{:S(2)}, u32[]{:S(2)}) collective-permute-start(f32[118,16,128]{2,1,0:T(8,128)S(1)} %get-tuple-element.30), channel_id=1, source_target_pairs={{0,8},{8,16},{16,24},{1,9},{9,17},{17,25},{2,10},{10,18},{18,26},{... | collective-permute-start | bytes 2899976 | tf_op jit(solution)/shard_map/ppermute | solution.py:534
  27.0 20.5 %collective-permute-start.4 = (f32[118,16,128]{2,1,0:T(8,128)S(1)}, f32[118,16,128]{2,1,0:T(8,128)S(1)}, u32[]{:S(2)}, u32[]{:S(2)}) collective-permute-start(f32[118,16,128]{2,1,0:T(8,128)S(1)} %get-tuple-element.31), channel_id=1, source_target_pairs={{8,0},{16,8},{24,16},{9,1},{17,9},{25,17},{10,2},{18,10},{26,18},{... | collective-permute-start | bytes 2899976 | tf_op jit(solution)/shard_map/ppermute | solution.py:534
  39.8 12.2 %collective-permute-start.5 = (f32[944,128]{1,0:T(8,128)S(1)}, f32[944,128]{1,0:T(8,128)S(1)}, u32[]{:S(2)}, u32[]{:S(2)}) collective-permute-start(f32[944,128]{1,0:T(8,128)S(1)} %get-tuple-element.40), channel_id=1, source_target_pairs={{0,8},{8,16},{16,24},{1,9},{9,17},{17,25},{2,10},{10,18},{18,26},{... | collective-permute-start | bytes 1449992 | tf_op jit(solution)/shard_map/ppermute | solution.py:534
  45.5 10.1 %collective-permute-start.6 = (f32[944,128]{1,0:T(8,128)S(1)}, f32[944,128]{1,0:T(8,128)S(1)}, u32[]{:S(2)}, u32[]{:S(2)}) collective-permute-start(f32[944,128]{1,0:T(8,128)S(1)} %get-tuple-element.41), channel_id=1, source_target_pairs={{8,0},{16,8},{24,16},{9,1},{17,9},{25,17},{10,2},{18,10},{26,18},{... | collective-permute-start | bytes 1449992 | tf_op jit(solution)/shard_map/ppermute | solution.py:534

commit v7 on v6

--- a/solution.py
+++ b/solution.py
@@ -330,8 +330,11 @@
         ref[c, pl.ds(row, nx, stride=pitch), :] = part[j]
 
     insert_layers(plan, cells, fields, 1, (y_low, y_high), put_y)
-    prepare(plan, owner, fields, masks, w, w + nx)
+    prepare(plan, owner, fields, masks, w, w + nx, plan.outside)
     sweep(plan, owner, cells, other, fields, masks, 0, w + 1, w + nx - 1, plan.outside)
+    buffers = [cells, other]
+    for s in range(1, plan.steps - 1):
+        sweep(plan, owner, buffers[s % 2], buffers[(s + 1) % 2], fields, masks, s, w + 1 + s, w + nx - 1 - s)
 
 
 def steps_kernel(plan, owner, cells, fields, other, masks, c_low, c_high, flow_hbm, solute_hbm, flow_out, solute_out, sems):
@@ -345,11 +348,11 @@
     insert_layers(plan, cells, fields, 0, (c_low, c_high), put)
     prepare(plan, owner, fields, masks, 0, w)
     prepare(plan, owner, fields, masks, w + nx, plan.wide)
-    sweep(plan, owner, cells, other, fields, masks, 0, 1, w + 1)
-    sweep(plan, owner, cells, other, fields, masks, 0, w + nx - 1, plan.wide - 1)
     buffers = [cells, other]
-    for s in range(1, plan.steps - 1):
-        sweep(plan, owner, buffers[s % 2], buffers[(s + 1) % 2], fields, masks, s, 1 + s, plan.wide - 1 - s)
+    for s in range(plan.steps - 1):
+        source, target = buffers[s % 2], buffers[(s + 1) % 2]
+        sweep(plan, owner, source, target, fields, masks, s, 1 + s, w + 1 + s)
+        sweep(plan, owner, source, target, fields, masks, s, w + nx - 1 - s, plan.wide - 1 - s)
     s = plan.steps - 1
     source = buffers[s % 2]
 
@@ -380,7 +383,7 @@
             copy.wait()
 
 
-def prepare(plan, owner, fields, masks, from_x, to_x):
+def prepare(plan, owner, fields, masks, from_x, to_x, tiles=None):
     w, nx, ny, depth, pitch = plan.halo, plan.nx, plan.ny, plan.depth, plan.pitch
     length = occupied(owner)
     lane = lanes(depth)
@@ -395,9 +398,10 @@
     x_end = jnp.where(gx < last_x, nx + 2 * w, w + nx)
     sub = lax.broadcasted_iota(jnp.int32, (8, depth), 0)
 
-    def one(x, carry):
+    def one(i):
+        x = from_x + i
         in_x = ((x >= x_first) & (x < x_end)).astype(F32)
-        for h in range(pitch // 8):
+        for h in tiles or plan.tiles:
             row = pl.multiple_of(PAD + x * pitch + 8 * h, 8)
             flags = fields[0, pl.ds(row, 8), :]
             y = sub + 8 * h
@@ -405,9 +409,8 @@
             masks[1, pl.ds(row, 8), :] = pltpu.roll(flags, 1, 1)
             inside = in_z & (y >= y_first) & (y < y_end) & (flags == 0.0)
             masks[2, pl.ds(row, 8), :] = jnp.where(inside, in_x, 0.0)
-        return carry
-
-    lax.fori_loop(from_x, to_x, one, 0)
+
+    each(to_x - from_x, one)
 
 
 def sweep(plan, owner, source, target, fields, masks, s, from_x, to_x, tiles=None):

time: 67.9 us -> 63.9 us (0.941)
  Pallas kernels: 31.5 us -> 29.3 us
  waiting for transfers between devices: 14.3 us -> 12.6 us
    pallas_call x1, Pallas kernels: 11.9 us -> 8.02 us  [per_device(): call(functools.partial(steps_kernel, plan), [SMEM] + [VMEM] * 6, [jax.Sha...]
    pallas_call x1, Pallas kernels: 4.46 us -> 6.99 us  [per_device(): call(functools.partial(first_kernel, plan), [SMEM] + [VMEM] * 8, [state,...]
    ppermute x6, waiting for transfers between devices: 10.9 us -> 9.14 us  [move(): lax.ppermute(value, axis, [(i, i + by) for i in range(size) if 0 <= i + b...]
    pallas_call x1, Pallas kernels: 3.26 us -> 2.45 us  [per_device(): call(functools.partial(middle_kernel, plan), [SMEM] + [VMEM] * 2, [state,...]
  transfers between devices with their start and end apart: 7 -> 7, of which waited for: 4 -> 4; matrix products, arithmetic and copies ran while one was open for 0% -> 0% of each run, Pallas kernels for 19% -> 23%
where the time goes in v7:
time: 63.9 us; the launch traced here: 63.6 us
  Pallas kernels  29.3 us (46%)
  starting transfers between devices  21 us (33%)
  waiting for transfers between devices  12.6 us (20%)
  between operations  0.76 us (1%)
    ppermute x6, starting transfers between devices, move(): lax.ppermute(value, axis, [(i, i + by) for i in range(size) if 0 <= i + b...  18.9 us
    ppermute x6, waiting for transfers between devices, move(): lax.ppermute(value, axis, [(i, i + by) for i in range(size) if 0 <= i + b...  9.14 us
    pallas_call x1, Pallas kernels, per_device(): call(functools.partial(steps_kernel, plan), [SMEM] + [VMEM] * 6, [jax.Sha...  8.02 us
    pallas_call x1, Pallas kernels, per_device(): call(functools.partial(first_kernel, plan), [SMEM] + [VMEM] * 8, [state,...  6.99 us
    pallas_call x1, Pallas kernels, per_device(): call(functools.partial(inner_kernel, plan, ring, parts), [SMEM] + [VMEM]...  4.4 us
    pallas_call x1, Pallas kernels, per_device(): call(functools.partial(pack_kernel, plan, ring, parts), [SMEM] + [HBM] *...  4.36 us
    ppermute x1, waiting for transfers between devices, per_device(): received = [lax.ppermute(packed[0], 'gz', [(0, 1), (1, 0)])]  3.44 us
    pallas_call x1, Pallas kernels, per_device(): call(functools.partial(middle_kernel, plan), [SMEM] + [VMEM] * 2, [state,...  2.45 us
  transfers between devices with their start and end apart: 7, of which 4 were waited for; matrix products, arithmetic and copies ran while one was open for 0% of the time, Pallas kernels for 23%

profile of v7, /device:TPU:1, one launch (start us, length us, event | category | flops | bytes accessed | tf_op | source)
XLA Modules:
  0.0 63.6 jit_solution(539932742561060582)
XLA Ops:
  0.6 4.4 %pack_column.1 = (f32[42,8,128]{2,1,0:T(8,128)S(1)}, f32[19,256,128]{2,1,0:T(8,128)S(1)}, f32[7,256,128]{2,1,0:T(8,128)S(1)}, f32[21,256,128]{2,1,0:T(8,128)S(1)}) custom-call(s32[8]{0:T(128)} %owner.11, f32[19,256,128]{2,1,0:T(8,128)} %bitcast.14, f32[7,256,128]{2,1,0:T(8,128)} %bitcast.15, bf16[4,256,128]{2,1,0:T(8,128)(2,1)} %bitcast.17, ...), custom_call_target="tpu_custom_call" | custom-call | flops 4194304 | bytes 8388608 | tf_op jit(solution)/shard_map/pack_column/pallas_call | solution.py:544
  5.0 2.1 %collective-permute-start = (f32[42,8,128]{2,1,0:T(8,128)S(1)}, f32[42,8,128]{2,1,0:T(8,128)S(1)}, u32[]{:S(2)}, u32[]{:S(2)}) collective-permute-start(f32[42,8,128]{2,1,0:T(8,128)S(1)} %get-tuple-element.25.packed), channel_id=1, source_target_pairs={{0,1},{1,0},{2,3},{3,2},{4,5},{5,4},{6,7},{7,6},{8,9},{9,8},{10,11... | collective-permute-start | bytes 516104 | tf_op jit(solution)/shard_map/ppermute | solution.py:554
  7.1 0.7 %faces.1 = (f32[118,16,128]{2,1,0:T(8,128)S(1)}, f32[118,16,128]{2,1,0:T(8,128)S(1)}) custom-call(f32[19,256,128]{2,1,0:T(8,128)S(1)} %get-tuple-element.22.flow, f32[7,256,128]{2,1,0:T(8,128)S(1)} %get-tuple-element.23.solute, f32[21,256,128]{2,1,0:T(8,128)S(1)} %get-tuple-element.24.wide, f32[42,8,128]{2,1,0:T(8,128)S(1)} %get-tuple-element.25.packed), custom_call_target="tpu_custom_call" | custom-call | flops 16777216 | bytes 8388608 | tf_op jit(solution)/shard_map/faces/pallas_call | solution.py:559
  7.8 3.4 %collective-permute-done.rest_0_ = f32[42,8,128]{2,1,0:T(8,128)S(1)} collective-permute-done((f32[42,8,128]{2,1,0:T(8,128)S(1)}, f32[42,8,128]{2,1,0:T(8,128)S(1)}, u32[]{:S(2)}, u32[]{:S(2)}) %collective-permute-start) | collective-permute-done | bytes 172064 | tf_op jit(solution)/shard_map/ppermute | solution.py:554
  11.2 2.0 %insert.1 = (f32[118,16,128]{2,1,0:T(8,128)S(1)}, f32[118,16,128]{2,1,0:T(8,128)S(1)}) custom-call(s32[8]{0:T(128)} %owner.11, f32[118,16,128]{2,1,0:T(8,128)S(1)} %get-tuple-element.26.low, f32[118,16,128]{2,1,0:T(8,128)S(1)} %get-tuple-element.27.high, f32[42,8,128]{2,1,0:T(8,128)S(1)} %collective-permute-done.rest_0_), custom_call_target="tpu_custom_call" | custom-call | flops 4194304 | bytes 8388608 | tf_op jit(solution)/shard_map/insert/pallas_call | solution.py:562
  13.2 3.2 %collective-permute-start.1 = (f32[118,16,128]{2,1,0:T(8,128)S(1)}, f32[118,16,128]{2,1,0:T(8,128)S(1)}, u32[]{:S(2)}, u32[]{:S(2)}) collective-permute-start(f32[118,16,128]{2,1,0:T(8,128)S(1)} %get-tuple-element.28), channel_id=1, source_target_pairs={{0,2},{2,4},{4,6},{1,3},{3,5},{5,7},{8,10},{10,12},{12,14},{9,11},... | collective-permute-start | bytes 2899976 | tf_op jit(solution)/shard_map/ppermute | solution.py:537
  16.4 1.3 %collective-permute-start.2 = (f32[118,16,128]{2,1,0:T(8,128)S(1)}, f32[118,16,128]{2,1,0:T(8,128)S(1)}, u32[]{:S(2)}, u32[]{:S(2)}) collective-permute-start(f32[118,16,128]{2,1,0:T(8,128)S(1)} %get-tuple-element.29), channel_id=1, source_target_pairs={{2,0},{4,2},{6,4},{3,1},{5,3},{7,5},{10,8},{12,10},{14,12},{11,9},... | collective-permute-start | bytes 2899976 | tf_op jit(solution)/shard_map/ppermute | solution.py:537
  17.7 4.4 %inner.1 = (f32[26,592,128]{2,1,0:T(8,128)S(1)}, f32[21,592,128]{2,1,0:T(8,128)S(1)}, f32[118,16,128]{2,1,0:T(8,128)S(1)}, f32[118,16,128]{2,1,0:T(8,128)S(1)}) custom-call(s32[8]{0:T(128)} %owner.11, f32[19,256,128]{2,1,0:T(8,128)S(1)} %get-tuple-element.22.flow, f32[7,256,128]{2,1,0:T(8,128)S(1)} %get-tuple-element.23.solute, ...), custom_call_target="tpu_custom_call" | custom-call | flops 16777216 | bytes 8388608 | tf_op jit(solution)/shard_map/inner/pallas_call | solution.py:570
  22.1 4.8 %collective-permute-start.3 = (f32[118,16,128]{2,1,0:T(8,128)S(1)}, f32[118,16,128]{2,1,0:T(8,128)S(1)}, u32[]{:S(2)}, u32[]{:S(2)}) collective-permute-start(f32[118,16,128]{2,1,0:T(8,128)S(1)} %get-tuple-element.30), channel_id=1, source_target_pairs={{0,8},{8,16},{16,24},{1,9},{9,17},{17,25},{2,10},{10,18},{18,26},{... | collective-permute-start | bytes 2899976 | tf_op jit(solution)/shard_map/ppermute | solution.py:537
  27.0 1.9 %collective-permute-start.4 = (f32[118,16,128]{2,1,0:T(8,128)S(1)}, f32[118,16,128]{2,1,0:T(8,128)S(1)}, u32[]{:S(2)}, u32[]{:S(2)}) collective-permute-start(f32[118,16,128]{2,1,0:T(8,128)S(1)} %get-tuple-element.31), channel_id=1, source_target_pairs={{8,0},{16,8},{24,16},{9,1},{17,9},{25,17},{10,2},{18,10},{26,18},{... | collective-permute-start | bytes 2899976 | tf_op jit(solution)/shard_map/ppermute | solution.py:537
  28.9 2.4 %middle.1 = (f32[26,592,128]{2,1,0:T(8,128)S(1)}, f32[3,592,128]{2,1,0:T(8,128)S(1)}) custom-call(s32[8]{0:T(128)} %owner.11, f32[26,592,128]{2,1,0:T(8,128)S(1)} %get-tuple-element.32.cells.refs_0_, f32[21,592,128]{2,1,0:T(8,128)S(1)} %get-tuple-element.33.fields.refs_1_), custom_call_target="tpu_custom_call" | custom-call | flops 16777216 | bytes 8388608 | tf_op jit(solution)/shard_map/middle/pallas_call | solution.py:579
  31.4 4.1 %collective-permute-done.1.y_low = f32[118,16,128]{2,1,0:T(8,128)S(1)} collective-permute-done((f32[118,16,128]{2,1,0:T(8,128)S(1)}, f32[118,16,128]{2,1,0:T(8,128)S(1)}, u32[]{:S(2)}, u32[]{:S(2)}) %collective-permute-start.1) | collective-permute-done | bytes 966688 | tf_op jit(solution)/shard_map/ppermute | solution.py:537
  35.5 3.9 %collective-permute-done.2.y_high = f32[118,16,128]{2,1,0:T(8,128)S(1)} collective-permute-done((f32[118,16,128]{2,1,0:T(8,128)S(1)}, f32[118,16,128]{2,1,0:T(8,128)S(1)}, u32[]{:S(2)}, u32[]{:S(2)}) %collective-permute-start.2) | collective-permute-done | bytes 966688 | tf_op jit(solution)/shard_map/ppermute | solution.py:537
  39.4 0.4 corners.1
  39.8 5.8 %collective-permute-start.5 = (f32[944,128]{1,0:T(8,128)S(1)}, f32[944,128]{1,0:T(8,128)S(1)}, u32[]{:S(2)}, u32[]{:S(2)}) collective-permute-start(f32[944,128]{1,0:T(8,128)S(1)} %get-tuple-element.40), channel_id=1, source_target_pairs={{0,8},{8,16},{16,24},{1,9},{9,17},{17,25},{2,10},{10,18},{18,26},{... | collective-permute-start | bytes 1449992 | tf_op jit(solution)/shard_map/ppermute | solution.py:537
  45.5 1.9 %collective-permute-start.6 = (f32[944,128]{1,0:T(8,128)S(1)}, f32[944,128]{1,0:T(8,128)S(1)}, u32[]{:S(2)}, u32[]{:S(2)}) collective-permute-start(f32[944,128]{1,0:T(8,128)S(1)} %get-tuple-element.41), channel_id=1, source_target_pairs={{8,0},{16,8},{24,16},{9,1},{17,9},{25,17},{10,2},{18,10},{26,18},{... | collective-permute-start | bytes 1449992 | tf_op jit(solution)/shard_map/ppermute | solution.py:537
  47.5 0.0 collective-permute-done.3.x_low
  47.5 0.0 collective-permute-done.4.x_high
  47.5 7.0 %first.1 = (f32[26,592,128]{2,1,0:T(8,128)S(1)}, f32[21,592,128]{2,1,0:T(8,128)S(1)}, f32[26,592,128]{2,1,0:T(8,128)S(1)}, f32[3,592,128]{2,1,0:T(8,128)S(1)}) custom-call(s32[8]{0:T(128)} %owner.11, f32[118,16,128]{2,1,0:T(8,128)S(1)} %collective-permute-done.1.y_low, ...), custom_call_target="tpu_custom_call", output_to_operand_aliasing={{0}: (5, {}), {1}: (6, {}), {2}: (7, {}), {3}: (8, {})} | custom-call | flops 67108864 | bytes 8388608 | tf_op jit(solution)/shard_map/first/pallas_call | solution.py:594
  54.5 0.0 collective-permute-done.5
  54.5 1.1 %collective-permute-done.6 = f32[944,128]{1,0:T(8,128)S(1)} collective-permute-done((f32[944,128]{1,0:T(8,128)S(1)}, f32[944,128]{1,0:T(8,128)S(1)}, u32[]{:S(2)}, u32[]{:S(2)}) %collective-permute-start.6) | collective-permute-done | bytes 483360 | tf_op jit(solution)/shard_map/ppermute | solution.py:537
  55.6 8.0 %steps.1 = (f32[19,16,16,128]{3,2,1,0:T(8,128)}, f32[7,16,16,128]{3,2,1,0:T(8,128)}) custom-call(s32[8]{0:T(128)} %owner.11, f32[26,592,128]{2,1,0:T(8,128)S(1)} %get-tuple-element.36.cells, f32[21,592,128]{2,1,0:T(8,128)S(1)} %get-tuple-element.37.fields, f32[26,592,128]{2,1,0:T(8,128)S(1)} %get-tuple-element.38.other, ...), custom_call_target="tpu_custom_call" | custom-call | flops 268435456 | bytes 8388608 | tf_op jit(solution)/shard_map/steps/pallas_call | solution.py:604
Async XLA Ops:
  5.0 6.2 %collective-permute-start = (f32[42,8,128]{2,1,0:T(8,128)S(1)}, f32[42,8,128]{2,1,0:T(8,128)S(1)}, u32[]{:S(2)}, u32[]{:S(2)}) collective-permute-start(f32[42,8,128]{2,1,0:T(8,128)S(1)} %get-tuple-element.25.packed), channel_id=1, source_target_pairs={{0,1},{1,0},{2,3},{3,2},{4,5},{5,4},{6,7},{7,6},{8,9},{9,8},{10,11... | collective-permute-start | bytes 516104 | tf_op jit(solution)/shard_map/ppermute | solution.py:554
  13.2 22.2 %collective-permute-start.1 = (f32[118,16,128]{2,1,0:T(8,128)S(1)}, f32[118,16,128]{2,1,0:T(8,128)S(1)}, u32[]{:S(2)}, u32[]{:S(2)}) collective-permute-start(f32[118,16,128]{2,1,0:T(8,128)S(1)} %get-tuple-element.28), channel_id=1, source_target_pairs={{0,2},{2,4},{4,6},{1,3},{3,5},{5,7},{8,10},{10,12},{12,14},{9,11},... | collective-permute-start | bytes 2899976 | tf_op jit(solution)/shard_map/ppermute | solution.py:537
  16.4 23.0 %collective-permute-start.2 = (f32[118,16,128]{2,1,0:T(8,128)S(1)}, f32[118,16,128]{2,1,0:T(8,128)S(1)}, u32[]{:S(2)}, u32[]{:S(2)}) collective-permute-start(f32[118,16,128]{2,1,0:T(8,128)S(1)} %get-tuple-element.29), channel_id=1, source_target_pairs={{2,0},{4,2},{6,4},{3,1},{5,3},{7,5},{10,8},{12,10},{14,12},{11,9},... | collective-permute-start | bytes 2899976 | tf_op jit(solution)/shard_map/ppermute | solution.py:537
  22.1 25.4 %collective-permute-start.3 = (f32[118,16,128]{2,1,0:T(8,128)S(1)}, f32[118,16,128]{2,1,0:T(8,128)S(1)}, u32[]{:S(2)}, u32[]{:S(2)}) collective-permute-start(f32[118,16,128]{2,1,0:T(8,128)S(1)} %get-tuple-element.30), channel_id=1, source_target_pairs={{0,8},{8,16},{16,24},{1,9},{9,17},{17,25},{2,10},{10,18},{18,26},{... | collective-permute-start | bytes 2899976 | tf_op jit(solution)/shard_map/ppermute | solution.py:537
  27.0 20.5 %collective-permute-start.4 = (f32[118,16,128]{2,1,0:T(8,128)S(1)}, f32[118,16,128]{2,1,0:T(8,128)S(1)}, u32[]{:S(2)}, u32[]{:S(2)}) collective-permute-start(f32[118,16,128]{2,1,0:T(8,128)S(1)} %get-tuple-element.31), channel_id=1, source_target_pairs={{8,0},{16,8},{24,16},{9,1},{17,9},{25,17},{10,2},{18,10},{26,18},{... | collective-permute-start | bytes 2899976 | tf_op jit(solution)/shard_map/ppermute | solution.py:537
  39.8 14.7 %collective-permute-start.5 = (f32[944,128]{1,0:T(8,128)S(1)}, f32[944,128]{1,0:T(8,128)S(1)}, u32[]{:S(2)}, u32[]{:S(2)}) collective-permute-start(f32[944,128]{1,0:T(8,128)S(1)} %get-tuple-element.40), channel_id=1, source_target_pairs={{0,8},{8,16},{16,24},{1,9},{9,17},{17,25},{2,10},{10,18},{18,26},{... | collective-permute-start | bytes 1449992 | tf_op jit(solution)/shard_map/ppermute | solution.py:537
  45.5 10.1 %collective-permute-start.6 = (f32[944,128]{1,0:T(8,128)S(1)}, f32[944,128]{1,0:T(8,128)S(1)}, u32[]{:S(2)}, u32[]{:S(2)}) collective-permute-start(f32[944,128]{1,0:T(8,128)S(1)} %get-tuple-element.41), channel_id=1, source_target_pairs={{8,0},{16,8},{24,16},{9,1},{17,9},{25,17},{10,2},{18,10},{26,18},{... | collective-permute-start | bytes 1449992 | tf_op jit(solution)/shard_map/ppermute | solution.py:537

commit v8 on v7

--- a/solution.py
+++ b/solution.py
@@ -362,7 +362,7 @@
             for n, (ref, to) in enumerate(((flow_out, flow_hbm), (solute_out, solute_hbm)))
         ]
 
-    def last(x, carry):
+    def last(x):
         for h in range(ny // 8):
             row = PAD + (x + w) * pitch + w + 8 * h
 
@@ -375,9 +375,8 @@
             advance(plan, owner, source, fields, masks, s, row, write)
         for copy in leave(x):
             copy.start()
-        return carry
-
-    lax.fori_loop(0, nx, last, 0)
+
+    each(nx, last, 2)
     for x in range(nx):
         for copy in leave(x):
             copy.wait()
@@ -416,7 +415,8 @@
 def sweep(plan, owner, source, target, fields, masks, s, from_x, to_x, tiles=None):
     pitch = plan.pitch
 
-    def body(x, carry):
+    def body(i):
+        x = from_x + i
         for h in tiles or plan.tiles:
             row = pl.multiple_of(PAD + pitch * x + 8 * h, 8)
 
@@ -424,9 +424,8 @@
                 target[c, pl.ds(row, 8), :] = value
 
             advance(plan, owner, source, fields, masks, s, row, write)
-        return carry
-
-    lax.fori_loop(from_x, to_x, body, 0)
+
+    each(to_x - from_x, body, 2)
 
 
 def advance(plan, owner, source, fields, masks, s, row, write):

time: 63.9 us -> 63.1 us (0.987)
  Pallas kernels: 29.3 us -> 27.1 us
  waiting for transfers between devices: 12.6 us -> 13.9 us
    ppermute x6, waiting for transfers between devices: 9.14 us -> 10.5 us  [move(): lax.ppermute(value, axis, [(i, i + by) for i in range(size) if 0 <= i + b...]
    pallas_call x1, Pallas kernels: 8.02 us -> 7.16 us  [per_device(): call(functools.partial(steps_kernel, plan), [SMEM] + [VMEM] * 6, [jax.Sha...]
    pallas_call x1, Pallas kernels: 6.99 us -> 6.19 us  [per_device(): call(functools.partial(first_kernel, plan), [SMEM] + [VMEM] * 8, [state,...]
  transfers between devices with their start and end apart: 7 -> 7, of which waited for: 4 -> 4; matrix products, arithmetic and copies ran while one was open for 0% -> 0% of each run, Pallas kernels for 23% -> 22%
where the time goes in v8:
time: 63.1 us; the launch traced here: 62.8 us
  Pallas kernels  27.1 us (43%)
  starting transfers between devices  21 us (33%)
  waiting for transfers between devices  13.9 us (22%)
  between operations  0.76 us (1%)
    ppermute x6, starting transfers between devices, move(): lax.ppermute(value, axis, [(i, i + by) for i in range(size) if 0 <= i + b...  18.9 us
    ppermute x6, waiting for transfers between devices, move(): lax.ppermute(value, axis, [(i, i + by) for i in range(size) if 0 <= i + b...  10.5 us
    pallas_call x1, Pallas kernels, per_device(): call(functools.partial(steps_kernel, plan), [SMEM] + [VMEM] * 6, [jax.Sha...  7.16 us
    pallas_call x1, Pallas kernels, per_device(): call(functools.partial(first_kernel, plan), [SMEM] + [VMEM] * 8, [state,...  6.19 us
    pallas_call x1, Pallas kernels, per_device(): call(functools.partial(inner_kernel, plan, ring, parts), [SMEM] + [VMEM]...  4.4 us
    pallas_call x1, Pallas kernels, per_device(): call(functools.partial(pack_kernel, plan, ring, parts), [SMEM] + [HBM] *...  4.36 us
    ppermute x1, waiting for transfers between devices, per_device(): received = [lax.ppermute(packed[0], 'gz', [(0, 1), (1, 0)])]  3.44 us
    ppermute x1, starting transfers between devices, per_device(): received = [lax.ppermute(packed[0], 'gz', [(0, 1), (1, 0)])]  2.13 us
  transfers between devices with their start and end apart: 7, of which 4 were waited for; matrix products, arithmetic and copies ran while one was open for 0% of the time, Pallas kernels for 22%

profile of v8, /device:TPU:1, one launch (start us, length us, event | category | flops | bytes accessed | tf_op | source)
XLA Modules:
  0.0 62.8 jit_solution(11927892573327717001)
XLA Ops:
  0.6 4.4 %pack_column.1 = (f32[42,8,128]{2,1,0:T(8,128)S(1)}, f32[19,256,128]{2,1,0:T(8,128)S(1)}, f32[7,256,128]{2,1,0:T(8,128)S(1)}, f32[21,256,128]{2,1,0:T(8,128)S(1)}) custom-call(s32[8]{0:T(128)} %owner.11, f32[19,256,128]{2,1,0:T(8,128)} %bitcast.14, f32[7,256,128]{2,1,0:T(8,128)} %bitcast.15, bf16[4,256,128]{2,1,0:T(8,128)(2,1)} %bitcast.17, ...), custom_call_target="tpu_custom_call" | custom-call | flops 4194304 | bytes 8388608 | tf_op jit(solution)/shard_map/pack_column/pallas_call | solution.py:543
  5.0 2.1 %collective-permute-start = (f32[42,8,128]{2,1,0:T(8,128)S(1)}, f32[42,8,128]{2,1,0:T(8,128)S(1)}, u32[]{:S(2)}, u32[]{:S(2)}) collective-permute-start(f32[42,8,128]{2,1,0:T(8,128)S(1)} %get-tuple-element.25.packed), channel_id=1, source_target_pairs={{0,1},{1,0},{2,3},{3,2},{4,5},{5,4},{6,7},{7,6},{8,9},{9,8},{10,11... | collective-permute-start | bytes 516104 | tf_op jit(solution)/shard_map/ppermute | solution.py:553
  7.1 0.7 %faces.1 = (f32[118,16,128]{2,1,0:T(8,128)S(1)}, f32[118,16,128]{2,1,0:T(8,128)S(1)}) custom-call(f32[19,256,128]{2,1,0:T(8,128)S(1)} %get-tuple-element.22.flow, f32[7,256,128]{2,1,0:T(8,128)S(1)} %get-tuple-element.23.solute, f32[21,256,128]{2,1,0:T(8,128)S(1)} %get-tuple-element.24.wide, f32[42,8,128]{2,1,0:T(8,128)S(1)} %get-tuple-element.25.packed), custom_call_target="tpu_custom_call" | custom-call | flops 16777216 | bytes 8388608 | tf_op jit(solution)/shard_map/faces/pallas_call | solution.py:558
  7.8 3.4 %collective-permute-done.rest_0_ = f32[42,8,128]{2,1,0:T(8,128)S(1)} collective-permute-done((f32[42,8,128]{2,1,0:T(8,128)S(1)}, f32[42,8,128]{2,1,0:T(8,128)S(1)}, u32[]{:S(2)}, u32[]{:S(2)}) %collective-permute-start) | collective-permute-done | bytes 172064 | tf_op jit(solution)/shard_map/ppermute | solution.py:553
  11.2 2.0 %insert.1 = (f32[118,16,128]{2,1,0:T(8,128)S(1)}, f32[118,16,128]{2,1,0:T(8,128)S(1)}) custom-call(s32[8]{0:T(128)} %owner.11, f32[118,16,128]{2,1,0:T(8,128)S(1)} %get-tuple-element.26.low, f32[118,16,128]{2,1,0:T(8,128)S(1)} %get-tuple-element.27.high, f32[42,8,128]{2,1,0:T(8,128)S(1)} %collective-permute-done.rest_0_), custom_call_target="tpu_custom_call" | custom-call | flops 4194304 | bytes 8388608 | tf_op jit(solution)/shard_map/insert/pallas_call | solution.py:561
  13.2 3.2 %collective-permute-start.1 = (f32[118,16,128]{2,1,0:T(8,128)S(1)}, f32[118,16,128]{2,1,0:T(8,128)S(1)}, u32[]{:S(2)}, u32[]{:S(2)}) collective-permute-start(f32[118,16,128]{2,1,0:T(8,128)S(1)} %get-tuple-element.28), channel_id=1, source_target_pairs={{0,2},{2,4},{4,6},{1,3},{3,5},{5,7},{8,10},{10,12},{12,14},{9,11},... | collective-permute-start | bytes 2899976 | tf_op jit(solution)/shard_map/ppermute | solution.py:536
  16.4 1.3 %collective-permute-start.2 = (f32[118,16,128]{2,1,0:T(8,128)S(1)}, f32[118,16,128]{2,1,0:T(8,128)S(1)}, u32[]{:S(2)}, u32[]{:S(2)}) collective-permute-start(f32[118,16,128]{2,1,0:T(8,128)S(1)} %get-tuple-element.29), channel_id=1, source_target_pairs={{2,0},{4,2},{6,4},{3,1},{5,3},{7,5},{10,8},{12,10},{14,12},{11,9},... | collective-permute-start | bytes 2899976 | tf_op jit(solution)/shard_map/ppermute | solution.py:536
  17.7 4.4 %inner.1 = (f32[26,592,128]{2,1,0:T(8,128)S(1)}, f32[21,592,128]{2,1,0:T(8,128)S(1)}, f32[118,16,128]{2,1,0:T(8,128)S(1)}, f32[118,16,128]{2,1,0:T(8,128)S(1)}) custom-call(s32[8]{0:T(128)} %owner.11, f32[19,256,128]{2,1,0:T(8,128)S(1)} %get-tuple-element.22.flow, f32[7,256,128]{2,1,0:T(8,128)S(1)} %get-tuple-element.23.solute, ...), custom_call_target="tpu_custom_call" | custom-call | flops 16777216 | bytes 8388608 | tf_op jit(solution)/shard_map/inner/pallas_call | solution.py:569
  22.1 4.8 %collective-permute-start.3 = (f32[118,16,128]{2,1,0:T(8,128)S(1)}, f32[118,16,128]{2,1,0:T(8,128)S(1)}, u32[]{:S(2)}, u32[]{:S(2)}) collective-permute-start(f32[118,16,128]{2,1,0:T(8,128)S(1)} %get-tuple-element.30), channel_id=1, source_target_pairs={{0,8},{8,16},{16,24},{1,9},{9,17},{17,25},{2,10},{10,18},{18,26},{... | collective-permute-start | bytes 2899976 | tf_op jit(solution)/shard_map/ppermute | solution.py:536
  27.0 1.9 %collective-permute-start.4 = (f32[118,16,128]{2,1,0:T(8,128)S(1)}, f32[118,16,128]{2,1,0:T(8,128)S(1)}, u32[]{:S(2)}, u32[]{:S(2)}) collective-permute-start(f32[118,16,128]{2,1,0:T(8,128)S(1)} %get-tuple-element.31), channel_id=1, source_target_pairs={{8,0},{16,8},{24,16},{9,1},{17,9},{25,17},{10,2},{18,10},{26,18},{... | collective-permute-start | bytes 2899976 | tf_op jit(solution)/shard_map/ppermute | solution.py:536
  28.9 1.9 %middle.1 = (f32[26,592,128]{2,1,0:T(8,128)S(1)}, f32[3,592,128]{2,1,0:T(8,128)S(1)}) custom-call(s32[8]{0:T(128)} %owner.11, f32[26,592,128]{2,1,0:T(8,128)S(1)} %get-tuple-element.32.cells.refs_0_, f32[21,592,128]{2,1,0:T(8,128)S(1)} %get-tuple-element.33.fields.refs_1_), custom_call_target="tpu_custom_call" | custom-call | flops 16777216 | bytes 8388608 | tf_op jit(solution)/shard_map/middle/pallas_call | solution.py:578
  30.8 4.7 %collective-permute-done.1.y_low = f32[118,16,128]{2,1,0:T(8,128)S(1)} collective-permute-done((f32[118,16,128]{2,1,0:T(8,128)S(1)}, f32[118,16,128]{2,1,0:T(8,128)S(1)}, u32[]{:S(2)}, u32[]{:S(2)}) %collective-permute-start.1) | collective-permute-done | bytes 966688 | tf_op jit(solution)/shard_map/ppermute | solution.py:536
  35.5 3.9 %collective-permute-done.2.y_high = f32[118,16,128]{2,1,0:T(8,128)S(1)} collective-permute-done((f32[118,16,128]{2,1,0:T(8,128)S(1)}, f32[118,16,128]{2,1,0:T(8,128)S(1)}, u32[]{:S(2)}, u32[]{:S(2)}) %collective-permute-start.2) | collective-permute-done | bytes 966688 | tf_op jit(solution)/shard_map/ppermute | solution.py:536
  39.4 0.4 corners.1
  39.8 5.8 %collective-permute-start.5 = (f32[944,128]{1,0:T(8,128)S(1)}, f32[944,128]{1,0:T(8,128)S(1)}, u32[]{:S(2)}, u32[]{:S(2)}) collective-permute-start(f32[944,128]{1,0:T(8,128)S(1)} %get-tuple-element.40), channel_id=1, source_target_pairs={{0,8},{8,16},{16,24},{1,9},{9,17},{17,25},{2,10},{10,18},{18,26},{... | collective-permute-start | bytes 1449992 | tf_op jit(solution)/shard_map/ppermute | solution.py:536
  45.5 1.9 %collective-permute-start.6 = (f32[944,128]{1,0:T(8,128)S(1)}, f32[944,128]{1,0:T(8,128)S(1)}, u32[]{:S(2)}, u32[]{:S(2)}) collective-permute-start(f32[944,128]{1,0:T(8,128)S(1)} %get-tuple-element.41), channel_id=1, source_target_pairs={{8,0},{16,8},{24,16},{9,1},{17,9},{25,17},{10,2},{18,10},{26,18},{... | collective-permute-start | bytes 1449992 | tf_op jit(solution)/shard_map/ppermute | solution.py:536
  47.5 0.0 collective-permute-done.3.x_low
  47.5 0.0 collective-permute-done.4.x_high
  47.5 6.2 %first.1 = (f32[26,592,128]{2,1,0:T(8,128)S(1)}, f32[21,592,128]{2,1,0:T(8,128)S(1)}, f32[26,592,128]{2,1,0:T(8,128)S(1)}, f32[3,592,128]{2,1,0:T(8,128)S(1)}) custom-call(s32[8]{0:T(128)} %owner.11, f32[118,16,128]{2,1,0:T(8,128)S(1)} %collective-permute-done.1.y_low, ...), custom_call_target="tpu_custom_call", output_to_operand_aliasing={{0}: (5, {}), {1}: (6, {}), {2}: (7, {}), {3}: (8, {})} | custom-call | flops 67108864 | bytes 8388608 | tf_op jit(solution)/shard_map/first/pallas_call | solution.py:593
  53.7 0.0 collective-permute-done.5
  53.7 1.9 %collective-permute-done.6 = f32[944,128]{1,0:T(8,128)S(1)} collective-permute-done((f32[944,128]{1,0:T(8,128)S(1)}, f32[944,128]{1,0:T(8,128)S(1)}, u32[]{:S(2)}, u32[]{:S(2)}) %collective-permute-start.6) | collective-permute-done | bytes 483360 | tf_op jit(solution)/shard_map/ppermute | solution.py:536
  55.6 7.2 %steps.1 = (f32[19,16,16,128]{3,2,1,0:T(8,128)}, f32[7,16,16,128]{3,2,1,0:T(8,128)}) custom-call(s32[8]{0:T(128)} %owner.11, f32[26,592,128]{2,1,0:T(8,128)S(1)} %get-tuple-element.36.cells, f32[21,592,128]{2,1,0:T(8,128)S(1)} %get-tuple-element.37.fields, f32[26,592,128]{2,1,0:T(8,128)S(1)} %get-tuple-element.38.other, ...), custom_call_target="tpu_custom_call" | custom-call | flops 268435456 | bytes 8388608 | tf_op jit(solution)/shard_map/steps/pallas_call | solution.py:603
Async XLA Ops:
  5.0 6.2 %collective-permute-start = (f32[42,8,128]{2,1,0:T(8,128)S(1)}, f32[42,8,128]{2,1,0:T(8,128)S(1)}, u32[]{:S(2)}, u32[]{:S(2)}) collective-permute-start(f32[42,8,128]{2,1,0:T(8,128)S(1)} %get-tuple-element.25.packed), channel_id=1, source_target_pairs={{0,1},{1,0},{2,3},{3,2},{4,5},{5,4},{6,7},{7,6},{8,9},{9,8},{10,11... | collective-permute-start | bytes 516104 | tf_op jit(solution)/shard_map/ppermute | solution.py:553
  13.2 22.2 %collective-permute-start.1 = (f32[118,16,128]{2,1,0:T(8,128)S(1)}, f32[118,16,128]{2,1,0:T(8,128)S(1)}, u32[]{:S(2)}, u32[]{:S(2)}) collective-permute-start(f32[118,16,128]{2,1,0:T(8,128)S(1)} %get-tuple-element.28), channel_id=1, source_target_pairs={{0,2},{2,4},{4,6},{1,3},{3,5},{5,7},{8,10},{10,12},{12,14},{9,11},... | collective-permute-start | bytes 2899976 | tf_op jit(solution)/shard_map/ppermute | solution.py:536
  16.4 23.0 %collective-permute-start.2 = (f32[118,16,128]{2,1,0:T(8,128)S(1)}, f32[118,16,128]{2,1,0:T(8,128)S(1)}, u32[]{:S(2)}, u32[]{:S(2)}) collective-permute-start(f32[118,16,128]{2,1,0:T(8,128)S(1)} %get-tuple-element.29), channel_id=1, source_target_pairs={{2,0},{4,2},{6,4},{3,1},{5,3},{7,5},{10,8},{12,10},{14,12},{11,9},... | collective-permute-start | bytes 2899976 | tf_op jit(solution)/shard_map/ppermute | solution.py:536
  22.1 25.4 %collective-permute-start.3 = (f32[118,16,128]{2,1,0:T(8,128)S(1)}, f32[118,16,128]{2,1,0:T(8,128)S(1)}, u32[]{:S(2)}, u32[]{:S(2)}) collective-permute-start(f32[118,16,128]{2,1,0:T(8,128)S(1)} %get-tuple-element.30), channel_id=1, source_target_pairs={{0,8},{8,16},{16,24},{1,9},{9,17},{17,25},{2,10},{10,18},{18,26},{... | collective-permute-start | bytes 2899976 | tf_op jit(solution)/shard_map/ppermute | solution.py:536
  27.0 20.5 %collective-permute-start.4 = (f32[118,16,128]{2,1,0:T(8,128)S(1)}, f32[118,16,128]{2,1,0:T(8,128)S(1)}, u32[]{:S(2)}, u32[]{:S(2)}) collective-permute-start(f32[118,16,128]{2,1,0:T(8,128)S(1)} %get-tuple-element.31), channel_id=1, source_target_pairs={{8,0},{16,8},{24,16},{9,1},{17,9},{25,17},{10,2},{18,10},{26,18},{... | collective-permute-start | bytes 2899976 | tf_op jit(solution)/shard_map/ppermute | solution.py:536
  39.8 13.9 %collective-permute-start.5 = (f32[944,128]{1,0:T(8,128)S(1)}, f32[944,128]{1,0:T(8,128)S(1)}, u32[]{:S(2)}, u32[]{:S(2)}) collective-permute-start(f32[944,128]{1,0:T(8,128)S(1)} %get-tuple-element.40), channel_id=1, source_target_pairs={{0,8},{8,16},{16,24},{1,9},{9,17},{17,25},{2,10},{10,18},{18,26},{... | collective-permute-start | bytes 1449992 | tf_op jit(solution)/shard_map/ppermute | solution.py:536
  45.5 10.1 %collective-permute-start.6 = (f32[944,128]{1,0:T(8,128)S(1)}, f32[944,128]{1,0:T(8,128)S(1)}, u32[]{:S(2)}, u32[]{:S(2)}) collective-permute-start(f32[944,128]{1,0:T(8,128)S(1)} %get-tuple-element.41), channel_id=1, source_target_pairs={{8,0},{16,8},{24,16},{9,1},{17,9},{25,17},{10,2},{18,10},{26,18},{... | collective-permute-start | bytes 1449992 | tf_op jit(solution)/shard_map/ppermute | solution.py:536

commit v9 on v8

--- a/solution.py
+++ b/solution.py
@@ -331,6 +331,9 @@
 
     insert_layers(plan, cells, fields, 1, (y_low, y_high), put_y)
     prepare(plan, owner, fields, masks, w, w + nx, plan.outside)
+    prepare(plan, owner, fields, masks, 0, w)
+    prepare(plan, owner, fields, masks, w + nx, plan.wide)
+    edges(plan, owner, cells, other, fields, masks, 0, plan.inside)
     sweep(plan, owner, cells, other, fields, masks, 0, w + 1, w + nx - 1, plan.outside)
     buffers = [cells, other]
     for s in range(1, plan.steps - 1):
@@ -346,13 +349,12 @@
         ref[c, row + w + ny : row + w + ny + w, :] = part[j, w : 2 * w, :]
 
     insert_layers(plan, cells, fields, 0, (c_low, c_high), put)
-    prepare(plan, owner, fields, masks, 0, w)
-    prepare(plan, owner, fields, masks, w + nx, plan.wide)
+    prepare(plan, owner, fields, masks, 0, w, plan.outside)
+    prepare(plan, owner, fields, masks, w + nx, plan.wide, plan.outside)
     buffers = [cells, other]
     for s in range(plan.steps - 1):
         source, target = buffers[s % 2], buffers[(s + 1) % 2]
-        sweep(plan, owner, source, target, fields, masks, s, 1 + s, w + 1 + s)
-        sweep(plan, owner, source, target, fields, masks, s, w + nx - 1 - s, plan.wide - 1 - s)
+        edges(plan, owner, source, target, fields, masks, s, plan.outside if s == 0 else None)
     s = plan.steps - 1
     source = buffers[s % 2]
 
@@ -412,12 +414,16 @@
     each(to_x - from_x, one)
 
 
-def sweep(plan, owner, source, target, fields, masks, s, from_x, to_x, tiles=None):
+def edges(plan, owner, source, target, fields, masks, s, tiles=None):
+    sweep(plan, owner, source, target, fields, masks, s, 1 + s, plan.halo + 1 + s, tiles, plan.nx + plan.halo - 2 * s - 2)
+
+
+def sweep(plan, owner, source, target, fields, masks, s, from_x, to_x, tiles=None, partner=None):
     pitch = plan.pitch
 
     def body(i):
-        x = from_x + i
-        for h in tiles or plan.tiles:
+        rows = [from_x + i] if partner is None else [from_x + i, from_x + i + partner]
+        for x, h in [(x, h) for x in rows for h in tiles or plan.tiles]:
             row = pl.multiple_of(PAD + pitch * x + 8 * h, 8)
 
             def write(c, value, row=row):
@@ -425,7 +431,7 @@
 
             advance(plan, owner, source, fields, masks, s, row, write)
 
-    each(to_x - from_x, body, 2)
+    each(to_x - from_x, body, 2 if partner is None else 1)
 
 
 def advance(plan, owner, source, fields, masks, s, row, write):
@@ -461,15 +467,17 @@
     h = reads(NF, NS)
     px, py, pz = h[1] - h[2], h[3] - h[4], h[5] - h[6]
     p0 = 0.25 * h[0] + 0.125 * ((h[1] + h[2]) + (h[3] + h[4]) + (h[5] + h[6]))
-    grown = 1.0 + level
-    uptake = langmuir_rate / (grown * grown)
+    grown = (1.0 + level) * (1.0 + level)
+    density = jnp.maximum(density, 0.5)
+    inverse = 1.0 / (grown * density)
+    uptake = langmuir_rate * (density * inverse)
     common = valid * (
         (solute_omega - uptake) * p0 + (solute_omega * 0.5) * (px * ux + py * uy + pz * uz)
     )
     keep = (1.0 - solute_omega) * valid
     for i in range(NS):
         write(NF + i, keep * h[i] + common)
-    factor = (0.5 * solute_omega) * level / jnp.maximum(density, 0.5)
+    factor = (0.5 * solute_omega) * level * (grown * inverse)
     fx, fy, fz = factor * px, factor * py, factor * pz
 
     g = reads(0, NF)

time: 63.1 us -> 62.8 us (level)
  transfers between devices with their start and end apart: 7 -> 7, of which waited for: 4 -> 4; matrix products, arithmetic and copies ran while one was open for 0% -> 0% of each run, Pallas kernels for 22% -> 23%
where the time goes in v9:
time: 62.8 us; the launch traced here: 62.5 us
  Pallas kernels  27.4 us (44%)
  starting transfers between devices  21 us (33%)
  waiting for transfers between devices  13.3 us (21%)
  between operations  0.76 us (1%)
    ppermute x6, starting transfers between devices, move(): lax.ppermute(value, axis, [(i, i + by) for i in range(size) if 0 <= i + b...  18.9 us
    ppermute x6, waiting for transfers between devices, move(): lax.ppermute(value, axis, [(i, i + by) for i in range(size) if 0 <= i + b...  9.86 us
    pallas_call x1, Pallas kernels, per_device(): call(functools.partial(steps_kernel, plan), [SMEM] + [VMEM] * 6, [jax.Sha...  6.87 us
    pallas_call x1, Pallas kernels, per_device(): call(functools.partial(first_kernel, plan), [SMEM] + [VMEM] * 8, [state,...  6.79 us
    pallas_call x1, Pallas kernels, per_device(): call(functools.partial(inner_kernel, plan, ring, parts), [SMEM] + [VMEM]...  4.4 us
    pallas_call x1, Pallas kernels, per_device(): call(functools.partial(pack_kernel, plan, ring, parts), [SMEM] + [HBM] *...  4.36 us
    ppermute x1, waiting for transfers between devices, per_device(): received = [lax.ppermute(packed[0], 'gz', [(0, 1), (1, 0)])]  3.44 us
    ppermute x1, starting transfers between devices, per_device(): received = [lax.ppermute(packed[0], 'gz', [(0, 1), (1, 0)])]  2.13 us
  transfers between devices with their start and end apart: 7, of which 4 were waited for; matrix products, arithmetic and copies ran while one was open for 0% of the time, Pallas kernels for 23%

profile of v9, /device:TPU:1, one launch (start us, length us, event | category | flops | bytes accessed | tf_op | source)
XLA Modules:
  0.0 62.5 jit_solution(18176413038552753646)
XLA Ops:
  0.6 4.4 %pack_column.1 = (f32[42,8,128]{2,1,0:T(8,128)S(1)}, f32[19,256,128]{2,1,0:T(8,128)S(1)}, f32[7,256,128]{2,1,0:T(8,128)S(1)}, f32[21,256,128]{2,1,0:T(8,128)S(1)}) custom-call(s32[8]{0:T(128)} %owner.11, f32[19,256,128]{2,1,0:T(8,128)} %bitcast.14, f32[7,256,128]{2,1,0:T(8,128)} %bitcast.15, bf16[4,256,128]{2,1,0:T(8,128)(2,1)} %bitcast.17, ...), custom_call_target="tpu_custom_call" | custom-call | flops 4194304 | bytes 8388608 | tf_op jit(solution)/shard_map/pack_column/pallas_call | solution.py:551
  5.0 2.1 %collective-permute-start = (f32[42,8,128]{2,1,0:T(8,128)S(1)}, f32[42,8,128]{2,1,0:T(8,128)S(1)}, u32[]{:S(2)}, u32[]{:S(2)}) collective-permute-start(f32[42,8,128]{2,1,0:T(8,128)S(1)} %get-tuple-element.25.packed), channel_id=1, source_target_pairs={{0,1},{1,0},{2,3},{3,2},{4,5},{5,4},{6,7},{7,6},{8,9},{9,8},{10,11... | collective-permute-start | bytes 516104 | tf_op jit(solution)/shard_map/ppermute | solution.py:561
  7.1 0.7 %faces.1 = (f32[118,16,128]{2,1,0:T(8,128)S(1)}, f32[118,16,128]{2,1,0:T(8,128)S(1)}) custom-call(f32[19,256,128]{2,1,0:T(8,128)S(1)} %get-tuple-element.22.flow, f32[7,256,128]{2,1,0:T(8,128)S(1)} %get-tuple-element.23.solute, f32[21,256,128]{2,1,0:T(8,128)S(1)} %get-tuple-element.24.wide, f32[42,8,128]{2,1,0:T(8,128)S(1)} %get-tuple-element.25.packed), custom_call_target="tpu_custom_call" | custom-call | flops 16777216 | bytes 8388608 | tf_op jit(solution)/shard_map/faces/pallas_call | solution.py:566
  7.8 3.4 %collective-permute-done.rest_0_ = f32[42,8,128]{2,1,0:T(8,128)S(1)} collective-permute-done((f32[42,8,128]{2,1,0:T(8,128)S(1)}, f32[42,8,128]{2,1,0:T(8,128)S(1)}, u32[]{:S(2)}, u32[]{:S(2)}) %collective-permute-start) | collective-permute-done | bytes 172064 | tf_op jit(solution)/shard_map/ppermute | solution.py:561
  11.2 2.0 %insert.1 = (f32[118,16,128]{2,1,0:T(8,128)S(1)}, f32[118,16,128]{2,1,0:T(8,128)S(1)}) custom-call(s32[8]{0:T(128)} %owner.11, f32[118,16,128]{2,1,0:T(8,128)S(1)} %get-tuple-element.26.low, f32[118,16,128]{2,1,0:T(8,128)S(1)} %get-tuple-element.27.high, f32[42,8,128]{2,1,0:T(8,128)S(1)} %collective-permute-done.rest_0_), custom_call_target="tpu_custom_call" | custom-call | flops 4194304 | bytes 8388608 | tf_op jit(solution)/shard_map/insert/pallas_call | solution.py:569
  13.2 3.2 %collective-permute-start.1 = (f32[118,16,128]{2,1,0:T(8,128)S(1)}, f32[118,16,128]{2,1,0:T(8,128)S(1)}, u32[]{:S(2)}, u32[]{:S(2)}) collective-permute-start(f32[118,16,128]{2,1,0:T(8,128)S(1)} %get-tuple-element.28), channel_id=1, source_target_pairs={{0,2},{2,4},{4,6},{1,3},{3,5},{5,7},{8,10},{10,12},{12,14},{9,11},... | collective-permute-start | bytes 2899976 | tf_op jit(solution)/shard_map/ppermute | solution.py:544
  16.4 1.3 %collective-permute-start.2 = (f32[118,16,128]{2,1,0:T(8,128)S(1)}, f32[118,16,128]{2,1,0:T(8,128)S(1)}, u32[]{:S(2)}, u32[]{:S(2)}) collective-permute-start(f32[118,16,128]{2,1,0:T(8,128)S(1)} %get-tuple-element.29), channel_id=1, source_target_pairs={{2,0},{4,2},{6,4},{3,1},{5,3},{7,5},{10,8},{12,10},{14,12},{11,9},... | collective-permute-start | bytes 2899976 | tf_op jit(solution)/shard_map/ppermute | solution.py:544
  17.7 4.4 %inner.1 = (f32[26,592,128]{2,1,0:T(8,128)S(1)}, f32[21,592,128]{2,1,0:T(8,128)S(1)}, f32[118,16,128]{2,1,0:T(8,128)S(1)}, f32[118,16,128]{2,1,0:T(8,128)S(1)}) custom-call(s32[8]{0:T(128)} %owner.11, f32[19,256,128]{2,1,0:T(8,128)S(1)} %get-tuple-element.22.flow, f32[7,256,128]{2,1,0:T(8,128)S(1)} %get-tuple-element.23.solute, ...), custom_call_target="tpu_custom_call" | custom-call | flops 16777216 | bytes 8388608 | tf_op jit(solution)/shard_map/inner/pallas_call | solution.py:577
  22.1 4.8 %collective-permute-start.3 = (f32[118,16,128]{2,1,0:T(8,128)S(1)}, f32[118,16,128]{2,1,0:T(8,128)S(1)}, u32[]{:S(2)}, u32[]{:S(2)}) collective-permute-start(f32[118,16,128]{2,1,0:T(8,128)S(1)} %get-tuple-element.30), channel_id=1, source_target_pairs={{0,8},{8,16},{16,24},{1,9},{9,17},{17,25},{2,10},{10,18},{18,26},{... | collective-permute-start | bytes 2899976 | tf_op jit(solution)/shard_map/ppermute | solution.py:544
  27.0 1.9 %collective-permute-start.4 = (f32[118,16,128]{2,1,0:T(8,128)S(1)}, f32[118,16,128]{2,1,0:T(8,128)S(1)}, u32[]{:S(2)}, u32[]{:S(2)}) collective-permute-start(f32[118,16,128]{2,1,0:T(8,128)S(1)} %get-tuple-element.31), channel_id=1, source_target_pairs={{8,0},{16,8},{24,16},{9,1},{17,9},{25,17},{10,2},{18,10},{26,18},{... | collective-permute-start | bytes 2899976 | tf_op jit(solution)/shard_map/ppermute | solution.py:544
  28.9 1.9 %middle.1 = (f32[26,592,128]{2,1,0:T(8,128)S(1)}, f32[3,592,128]{2,1,0:T(8,128)S(1)}) custom-call(s32[8]{0:T(128)} %owner.11, f32[26,592,128]{2,1,0:T(8,128)S(1)} %get-tuple-element.32.cells.refs_0_, f32[21,592,128]{2,1,0:T(8,128)S(1)} %get-tuple-element.33.fields.refs_1_), custom_call_target="tpu_custom_call" | custom-call | flops 16777216 | bytes 8388608 | tf_op jit(solution)/shard_map/middle/pallas_call | solution.py:586
  30.8 4.7 %collective-permute-done.1.y_low = f32[118,16,128]{2,1,0:T(8,128)S(1)} collective-permute-done((f32[118,16,128]{2,1,0:T(8,128)S(1)}, f32[118,16,128]{2,1,0:T(8,128)S(1)}, u32[]{:S(2)}, u32[]{:S(2)}) %collective-permute-start.1) | collective-permute-done | bytes 966688 | tf_op jit(solution)/shard_map/ppermute | solution.py:544
  35.5 3.9 %collective-permute-done.2.y_high = f32[118,16,128]{2,1,0:T(8,128)S(1)} collective-permute-done((f32[118,16,128]{2,1,0:T(8,128)S(1)}, f32[118,16,128]{2,1,0:T(8,128)S(1)}, u32[]{:S(2)}, u32[]{:S(2)}) %collective-permute-start.2) | collective-permute-done | bytes 966688 | tf_op jit(solution)/shard_map/ppermute | solution.py:544
  39.4 0.4 corners.1
  39.8 5.8 %collective-permute-start.5 = (f32[944,128]{1,0:T(8,128)S(1)}, f32[944,128]{1,0:T(8,128)S(1)}, u32[]{:S(2)}, u32[]{:S(2)}) collective-permute-start(f32[944,128]{1,0:T(8,128)S(1)} %get-tuple-element.40), channel_id=1, source_target_pairs={{0,8},{8,16},{16,24},{1,9},{9,17},{17,25},{2,10},{10,18},{18,26},{... | collective-permute-start | bytes 1449992 | tf_op jit(solution)/shard_map/ppermute | solution.py:544
  45.5 1.9 %collective-permute-start.6 = (f32[944,128]{1,0:T(8,128)S(1)}, f32[944,128]{1,0:T(8,128)S(1)}, u32[]{:S(2)}, u32[]{:S(2)}) collective-permute-start(f32[944,128]{1,0:T(8,128)S(1)} %get-tuple-element.41), channel_id=1, source_target_pairs={{8,0},{16,8},{24,16},{9,1},{17,9},{25,17},{10,2},{18,10},{26,18},{... | collective-permute-start | bytes 1449992 | tf_op jit(solution)/shard_map/ppermute | solution.py:544
  47.5 0.0 collective-permute-done.3.x_low
  47.5 0.0 collective-permute-done.4.x_high
  47.5 6.8 %first.1 = (f32[26,592,128]{2,1,0:T(8,128)S(1)}, f32[21,592,128]{2,1,0:T(8,128)S(1)}, f32[26,592,128]{2,1,0:T(8,128)S(1)}, f32[3,592,128]{2,1,0:T(8,128)S(1)}) custom-call(s32[8]{0:T(128)} %owner.11, f32[118,16,128]{2,1,0:T(8,128)S(1)} %collective-permute-done.1.y_low, ...), custom_call_target="tpu_custom_call", output_to_operand_aliasing={{0}: (5, {}), {1}: (6, {}), {2}: (7, {}), {3}: (8, {})} | custom-call | flops 67108864 | bytes 8388608 | tf_op jit(solution)/shard_map/first/pallas_call | solution.py:601
  54.3 0.0 collective-permute-done.5
  54.3 1.3 %collective-permute-done.6 = f32[944,128]{1,0:T(8,128)S(1)} collective-permute-done((f32[944,128]{1,0:T(8,128)S(1)}, f32[944,128]{1,0:T(8,128)S(1)}, u32[]{:S(2)}, u32[]{:S(2)}) %collective-permute-start.6) | collective-permute-done | bytes 483360 | tf_op jit(solution)/shard_map/ppermute | solution.py:544
  55.6 6.9 %steps.1 = (f32[19,16,16,128]{3,2,1,0:T(8,128)}, f32[7,16,16,128]{3,2,1,0:T(8,128)}) custom-call(s32[8]{0:T(128)} %owner.11, f32[26,592,128]{2,1,0:T(8,128)S(1)} %get-tuple-element.36.cells, f32[21,592,128]{2,1,0:T(8,128)S(1)} %get-tuple-element.37.fields, f32[26,592,128]{2,1,0:T(8,128)S(1)} %get-tuple-element.38.other, ...), custom_call_target="tpu_custom_call" | custom-call | flops 268435456 | bytes 8388608 | tf_op jit(solution)/shard_map/steps/pallas_call | solution.py:611
Async XLA Ops:
  5.0 6.2 %collective-permute-start = (f32[42,8,128]{2,1,0:T(8,128)S(1)}, f32[42,8,128]{2,1,0:T(8,128)S(1)}, u32[]{:S(2)}, u32[]{:S(2)}) collective-permute-start(f32[42,8,128]{2,1,0:T(8,128)S(1)} %get-tuple-element.25.packed), channel_id=1, source_target_pairs={{0,1},{1,0},{2,3},{3,2},{4,5},{5,4},{6,7},{7,6},{8,9},{9,8},{10,11... | collective-permute-start | bytes 516104 | tf_op jit(solution)/shard_map/ppermute | solution.py:561
  13.2 22.2 %collective-permute-start.1 = (f32[118,16,128]{2,1,0:T(8,128)S(1)}, f32[118,16,128]{2,1,0:T(8,128)S(1)}, u32[]{:S(2)}, u32[]{:S(2)}) collective-permute-start(f32[118,16,128]{2,1,0:T(8,128)S(1)} %get-tuple-element.28), channel_id=1, source_target_pairs={{0,2},{2,4},{4,6},{1,3},{3,5},{5,7},{8,10},{10,12},{12,14},{9,11},... | collective-permute-start | bytes 2899976 | tf_op jit(solution)/shard_map/ppermute | solution.py:544
  16.4 23.0 %collective-permute-start.2 = (f32[118,16,128]{2,1,0:T(8,128)S(1)}, f32[118,16,128]{2,1,0:T(8,128)S(1)}, u32[]{:S(2)}, u32[]{:S(2)}) collective-permute-start(f32[118,16,128]{2,1,0:T(8,128)S(1)} %get-tuple-element.29), channel_id=1, source_target_pairs={{2,0},{4,2},{6,4},{3,1},{5,3},{7,5},{10,8},{12,10},{14,12},{11,9},... | collective-permute-start | bytes 2899976 | tf_op jit(solution)/shard_map/ppermute | solution.py:544
  22.1 25.4 %collective-permute-start.3 = (f32[118,16,128]{2,1,0:T(8,128)S(1)}, f32[118,16,128]{2,1,0:T(8,128)S(1)}, u32[]{:S(2)}, u32[]{:S(2)}) collective-permute-start(f32[118,16,128]{2,1,0:T(8,128)S(1)} %get-tuple-element.30), channel_id=1, source_target_pairs={{0,8},{8,16},{16,24},{1,9},{9,17},{17,25},{2,10},{10,18},{18,26},{... | collective-permute-start | bytes 2899976 | tf_op jit(solution)/shard_map/ppermute | solution.py:544
  27.0 20.5 %collective-permute-start.4 = (f32[118,16,128]{2,1,0:T(8,128)S(1)}, f32[118,16,128]{2,1,0:T(8,128)S(1)}, u32[]{:S(2)}, u32[]{:S(2)}) collective-permute-start(f32[118,16,128]{2,1,0:T(8,128)S(1)} %get-tuple-element.31), channel_id=1, source_target_pairs={{8,0},{16,8},{24,16},{9,1},{17,9},{25,17},{10,2},{18,10},{26,18},{... | collective-permute-start | bytes 2899976 | tf_op jit(solution)/shard_map/ppermute | solution.py:544
  39.8 14.5 %collective-permute-start.5 = (f32[944,128]{1,0:T(8,128)S(1)}, f32[944,128]{1,0:T(8,128)S(1)}, u32[]{:S(2)}, u32[]{:S(2)}) collective-permute-start(f32[944,128]{1,0:T(8,128)S(1)} %get-tuple-element.40), channel_id=1, source_target_pairs={{0,8},{8,16},{16,24},{1,9},{9,17},{17,25},{2,10},{10,18},{18,26},{... | collective-permute-start | bytes 1449992 | tf_op jit(solution)/shard_map/ppermute | solution.py:544
  45.5 10.1 %collective-permute-start.6 = (f32[944,128]{1,0:T(8,128)S(1)}, f32[944,128]{1,0:T(8,128)S(1)}, u32[]{:S(2)}, u32[]{:S(2)}) collective-permute-start(f32[944,128]{1,0:T(8,128)S(1)} %get-tuple-element.41), channel_id=1, source_target_pairs={{8,0},{16,8},{24,16},{9,1},{17,9},{25,17},{10,2},{18,10},{26,18},{... | collective-permute-start | bytes 1449992 | tf_op jit(solution)/shard_map/ppermute | solution.py:544

commit v10 on v9

--- a/solution.py
+++ b/solution.py
@@ -294,7 +294,7 @@
 
 
 def channels(cells, fields, number, body):
-    each(SOLID, lambda c: body(cells, c, c))
+    each(SOLID, lambda c: body(cells, c, c), 13)
     each(number - SOLID, lambda c: body(fields, c, SOLID + c))
 
 
@@ -378,7 +378,7 @@
         for copy in leave(x):
             copy.start()
 
-    each(nx, last, 2)
+    each(nx, last, 4)
     for x in range(nx):
         for copy in leave(x):
             copy.wait()

time: 62.8 us -> 62.4 us (level)
  no operation moved by 1% of the time
where the time goes in v10:
time: 62.4 us; the launch traced here: 62.1 us
  Pallas kernels  26.9 us (43%)
  starting transfers between devices  21 us (34%)
  waiting for transfers between devices  13.5 us (22%)
  between operations  0.76 us (1%)
    ppermute x6, starting transfers between devices, move(): lax.ppermute(value, axis, [(i, i + by) for i in range(size) if 0 <= i + b...  18.9 us
    ppermute x6, waiting for transfers between devices, move(): lax.ppermute(value, axis, [(i, i + by) for i in range(size) if 0 <= i + b...  10 us
    pallas_call x1, Pallas kernels, per_device(): call(functools.partial(first_kernel, plan), [SMEM] + [VMEM] * 8, [state,...  6.7 us
    pallas_call x1, Pallas kernels, per_device(): call(functools.partial(steps_kernel, plan), [SMEM] + [VMEM] * 6, [jax.Sha...  6.51 us
    pallas_call x1, Pallas kernels, per_device(): call(functools.partial(pack_kernel, plan, ring, parts), [SMEM] + [HBM] *...  4.36 us
    pallas_call x1, Pallas kernels, per_device(): call(functools.partial(inner_kernel, plan, ring, parts), [SMEM] + [VMEM]...  4.34 us
    ppermute x1, waiting for transfers between devices, per_device(): received = [lax.ppermute(packed[0], 'gz', [(0, 1), (1, 0)])]  3.44 us
    ppermute x1, starting transfers between devices, per_device(): received = [lax.ppermute(packed[0], 'gz', [(0, 1), (1, 0)])]  2.13 us
  transfers between devices with their start and end apart: 7, of which 4 were waited for; matrix products, arithmetic and copies ran while one was open for 0% of the time, Pallas kernels for 23%

profile of v10, /device:TPU:1, one launch (start us, length us, event | category | flops | bytes accessed | tf_op | source)
XLA Modules:
  0.0 62.1 jit_solution(3863449923456950877)
XLA Ops:
  0.6 4.4 %pack_column.1 = (f32[42,8,128]{2,1,0:T(8,128)S(1)}, f32[19,256,128]{2,1,0:T(8,128)S(1)}, f32[7,256,128]{2,1,0:T(8,128)S(1)}, f32[21,256,128]{2,1,0:T(8,128)S(1)}) custom-call(s32[8]{0:T(128)} %owner.11, f32[19,256,128]{2,1,0:T(8,128)} %bitcast.14, f32[7,256,128]{2,1,0:T(8,128)} %bitcast.15, bf16[4,256,128]{2,1,0:T(8,128)(2,1)} %bitcast.17, ...), custom_call_target="tpu_custom_call" | custom-call | flops 4194304 | bytes 8388608 | tf_op jit(solution)/shard_map/pack_column/pallas_call | solution.py:551
  5.0 2.1 %collective-permute-start = (f32[42,8,128]{2,1,0:T(8,128)S(1)}, f32[42,8,128]{2,1,0:T(8,128)S(1)}, u32[]{:S(2)}, u32[]{:S(2)}) collective-permute-start(f32[42,8,128]{2,1,0:T(8,128)S(1)} %get-tuple-element.25.packed), channel_id=1, source_target_pairs={{0,1},{1,0},{2,3},{3,2},{4,5},{5,4},{6,7},{7,6},{8,9},{9,8},{10,11... | collective-permute-start | bytes 516104 | tf_op jit(solution)/shard_map/ppermute | solution.py:561
  7.1 0.7 %faces.1 = (f32[118,16,128]{2,1,0:T(8,128)S(1)}, f32[118,16,128]{2,1,0:T(8,128)S(1)}) custom-call(f32[19,256,128]{2,1,0:T(8,128)S(1)} %get-tuple-element.22.flow, f32[7,256,128]{2,1,0:T(8,128)S(1)} %get-tuple-element.23.solute, f32[21,256,128]{2,1,0:T(8,128)S(1)} %get-tuple-element.24.wide, f32[42,8,128]{2,1,0:T(8,128)S(1)} %get-tuple-element.25.packed), custom_call_target="tpu_custom_call" | custom-call | flops 16777216 | bytes 8388608 | tf_op jit(solution)/shard_map/faces/pallas_call | solution.py:566
  7.8 3.4 %collective-permute-done.rest_0_ = f32[42,8,128]{2,1,0:T(8,128)S(1)} collective-permute-done((f32[42,8,128]{2,1,0:T(8,128)S(1)}, f32[42,8,128]{2,1,0:T(8,128)S(1)}, u32[]{:S(2)}, u32[]{:S(2)}) %collective-permute-start) | collective-permute-done | bytes 172064 | tf_op jit(solution)/shard_map/ppermute | solution.py:561
  11.2 2.0 %insert.1 = (f32[118,16,128]{2,1,0:T(8,128)S(1)}, f32[118,16,128]{2,1,0:T(8,128)S(1)}) custom-call(s32[8]{0:T(128)} %owner.11, f32[118,16,128]{2,1,0:T(8,128)S(1)} %get-tuple-element.26.low, f32[118,16,128]{2,1,0:T(8,128)S(1)} %get-tuple-element.27.high, f32[42,8,128]{2,1,0:T(8,128)S(1)} %collective-permute-done.rest_0_), custom_call_target="tpu_custom_call" | custom-call | flops 4194304 | bytes 8388608 | tf_op jit(solution)/shard_map/insert/pallas_call | solution.py:569
  13.2 3.2 %collective-permute-start.1 = (f32[118,16,128]{2,1,0:T(8,128)S(1)}, f32[118,16,128]{2,1,0:T(8,128)S(1)}, u32[]{:S(2)}, u32[]{:S(2)}) collective-permute-start(f32[118,16,128]{2,1,0:T(8,128)S(1)} %get-tuple-element.28), channel_id=1, source_target_pairs={{0,2},{2,4},{4,6},{1,3},{3,5},{5,7},{8,10},{10,12},{12,14},{9,11},... | collective-permute-start | bytes 2899976 | tf_op jit(solution)/shard_map/ppermute | solution.py:544
  16.4 1.3 %collective-permute-start.2 = (f32[118,16,128]{2,1,0:T(8,128)S(1)}, f32[118,16,128]{2,1,0:T(8,128)S(1)}, u32[]{:S(2)}, u32[]{:S(2)}) collective-permute-start(f32[118,16,128]{2,1,0:T(8,128)S(1)} %get-tuple-element.29), channel_id=1, source_target_pairs={{2,0},{4,2},{6,4},{3,1},{5,3},{7,5},{10,8},{12,10},{14,12},{11,9},... | collective-permute-start | bytes 2899976 | tf_op jit(solution)/shard_map/ppermute | solution.py:544
  17.7 4.3 %inner.1 = (f32[26,592,128]{2,1,0:T(8,128)S(1)}, f32[21,592,128]{2,1,0:T(8,128)S(1)}, f32[118,16,128]{2,1,0:T(8,128)S(1)}, f32[118,16,128]{2,1,0:T(8,128)S(1)}) custom-call(s32[8]{0:T(128)} %owner.11, f32[19,256,128]{2,1,0:T(8,128)S(1)} %get-tuple-element.22.flow, f32[7,256,128]{2,1,0:T(8,128)S(1)} %get-tuple-element.23.solute, ...), custom_call_target="tpu_custom_call" | custom-call | flops 16777216 | bytes 8388608 | tf_op jit(solution)/shard_map/inner/pallas_call | solution.py:577
  22.1 4.8 %collective-permute-start.3 = (f32[118,16,128]{2,1,0:T(8,128)S(1)}, f32[118,16,128]{2,1,0:T(8,128)S(1)}, u32[]{:S(2)}, u32[]{:S(2)}) collective-permute-start(f32[118,16,128]{2,1,0:T(8,128)S(1)} %get-tuple-element.30), channel_id=1, source_target_pairs={{0,8},{8,16},{16,24},{1,9},{9,17},{17,25},{2,10},{10,18},{18,26},{... | collective-permute-start | bytes 2899976 | tf_op jit(solution)/shard_map/ppermute | solution.py:544
  26.9 1.9 %collective-permute-start.4 = (f32[118,16,128]{2,1,0:T(8,128)S(1)}, f32[118,16,128]{2,1,0:T(8,128)S(1)}, u32[]{:S(2)}, u32[]{:S(2)}) collective-permute-start(f32[118,16,128]{2,1,0:T(8,128)S(1)} %get-tuple-element.31), channel_id=1, source_target_pairs={{8,0},{16,8},{24,16},{9,1},{17,9},{25,17},{10,2},{18,10},{26,18},{... | collective-permute-start | bytes 2899976 | tf_op jit(solution)/shard_map/ppermute | solution.py:544
  28.8 1.9 %middle.1 = (f32[26,592,128]{2,1,0:T(8,128)S(1)}, f32[3,592,128]{2,1,0:T(8,128)S(1)}) custom-call(s32[8]{0:T(128)} %owner.11, f32[26,592,128]{2,1,0:T(8,128)S(1)} %get-tuple-element.32.cells.refs_0_, f32[21,592,128]{2,1,0:T(8,128)S(1)} %get-tuple-element.33.fields.refs_1_), custom_call_target="tpu_custom_call" | custom-call | flops 16777216 | bytes 8388608 | tf_op jit(solution)/shard_map/middle/pallas_call | solution.py:586
  30.8 4.7 %collective-permute-done.1.y_low = f32[118,16,128]{2,1,0:T(8,128)S(1)} collective-permute-done((f32[118,16,128]{2,1,0:T(8,128)S(1)}, f32[118,16,128]{2,1,0:T(8,128)S(1)}, u32[]{:S(2)}, u32[]{:S(2)}) %collective-permute-start.1) | collective-permute-done | bytes 966688 | tf_op jit(solution)/shard_map/ppermute | solution.py:544
  35.5 3.9 %collective-permute-done.2.y_high = f32[118,16,128]{2,1,0:T(8,128)S(1)} collective-permute-done((f32[118,16,128]{2,1,0:T(8,128)S(1)}, f32[118,16,128]{2,1,0:T(8,128)S(1)}, u32[]{:S(2)}, u32[]{:S(2)}) %collective-permute-start.2) | collective-permute-done | bytes 966688 | tf_op jit(solution)/shard_map/ppermute | solution.py:544
  39.4 0.4 corners.1
  39.8 5.8 %collective-permute-start.5 = (f32[944,128]{1,0:T(8,128)S(1)}, f32[944,128]{1,0:T(8,128)S(1)}, u32[]{:S(2)}, u32[]{:S(2)}) collective-permute-start(f32[944,128]{1,0:T(8,128)S(1)} %get-tuple-element.40), channel_id=1, source_target_pairs={{0,8},{8,16},{16,24},{1,9},{9,17},{17,25},{2,10},{10,18},{18,26},{... | collective-permute-start | bytes 1449992 | tf_op jit(solution)/shard_map/ppermute | solution.py:544
  45.5 1.9 %collective-permute-start.6 = (f32[944,128]{1,0:T(8,128)S(1)}, f32[944,128]{1,0:T(8,128)S(1)}, u32[]{:S(2)}, u32[]{:S(2)}) collective-permute-start(f32[944,128]{1,0:T(8,128)S(1)} %get-tuple-element.41), channel_id=1, source_target_pairs={{8,0},{16,8},{24,16},{9,1},{17,9},{25,17},{10,2},{18,10},{26,18},{... | collective-permute-start | bytes 1449992 | tf_op jit(solution)/shard_map/ppermute | solution.py:544
  47.5 0.0 collective-permute-done.3.x_low
  47.5 0.0 collective-permute-done.4.x_high
  47.5 6.7 %first.1 = (f32[26,592,128]{2,1,0:T(8,128)S(1)}, f32[21,592,128]{2,1,0:T(8,128)S(1)}, f32[26,592,128]{2,1,0:T(8,128)S(1)}, f32[3,592,128]{2,1,0:T(8,128)S(1)}) custom-call(s32[8]{0:T(128)} %owner.11, f32[118,16,128]{2,1,0:T(8,128)S(1)} %collective-permute-done.1.y_low, ...), custom_call_target="tpu_custom_call", output_to_operand_aliasing={{0}: (5, {}), {1}: (6, {}), {2}: (7, {}), {3}: (8, {})} | custom-call | flops 67108864 | bytes 8388608 | tf_op jit(solution)/shard_map/first/pallas_call | solution.py:601
  54.2 0.0 collective-permute-done.5
  54.2 1.4 %collective-permute-done.6 = f32[944,128]{1,0:T(8,128)S(1)} collective-permute-done((f32[944,128]{1,0:T(8,128)S(1)}, f32[944,128]{1,0:T(8,128)S(1)}, u32[]{:S(2)}, u32[]{:S(2)}) %collective-permute-start.6) | collective-permute-done | bytes 483360 | tf_op jit(solution)/shard_map/ppermute | solution.py:544
  55.6 6.5 %steps.1 = (f32[19,16,16,128]{3,2,1,0:T(8,128)}, f32[7,16,16,128]{3,2,1,0:T(8,128)}) custom-call(s32[8]{0:T(128)} %owner.11, f32[26,592,128]{2,1,0:T(8,128)S(1)} %get-tuple-element.36.cells, f32[21,592,128]{2,1,0:T(8,128)S(1)} %get-tuple-element.37.fields, f32[26,592,128]{2,1,0:T(8,128)S(1)} %get-tuple-element.38.other, ...), custom_call_target="tpu_custom_call" | custom-call | flops 268435456 | bytes 8388608 | tf_op jit(solution)/shard_map/steps/pallas_call | solution.py:611
Async XLA Ops:
  5.0 6.2 %collective-permute-start = (f32[42,8,128]{2,1,0:T(8,128)S(1)}, f32[42,8,128]{2,1,0:T(8,128)S(1)}, u32[]{:S(2)}, u32[]{:S(2)}) collective-permute-start(f32[42,8,128]{2,1,0:T(8,128)S(1)} %get-tuple-element.25.packed), channel_id=1, source_target_pairs={{0,1},{1,0},{2,3},{3,2},{4,5},{5,4},{6,7},{7,6},{8,9},{9,8},{10,11... | collective-permute-start | bytes 516104 | tf_op jit(solution)/shard_map/ppermute | solution.py:561
  13.2 22.2 %collective-permute-start.1 = (f32[118,16,128]{2,1,0:T(8,128)S(1)}, f32[118,16,128]{2,1,0:T(8,128)S(1)}, u32[]{:S(2)}, u32[]{:S(2)}) collective-permute-start(f32[118,16,128]{2,1,0:T(8,128)S(1)} %get-tuple-element.28), channel_id=1, source_target_pairs={{0,2},{2,4},{4,6},{1,3},{3,5},{5,7},{8,10},{10,12},{12,14},{9,11},... | collective-permute-start | bytes 2899976 | tf_op jit(solution)/shard_map/ppermute | solution.py:544
  16.4 23.0 %collective-permute-start.2 = (f32[118,16,128]{2,1,0:T(8,128)S(1)}, f32[118,16,128]{2,1,0:T(8,128)S(1)}, u32[]{:S(2)}, u32[]{:S(2)}) collective-permute-start(f32[118,16,128]{2,1,0:T(8,128)S(1)} %get-tuple-element.29), channel_id=1, source_target_pairs={{2,0},{4,2},{6,4},{3,1},{5,3},{7,5},{10,8},{12,10},{14,12},{11,9},... | collective-permute-start | bytes 2899976 | tf_op jit(solution)/shard_map/ppermute | solution.py:544
  22.1 25.4 %collective-permute-start.3 = (f32[118,16,128]{2,1,0:T(8,128)S(1)}, f32[118,16,128]{2,1,0:T(8,128)S(1)}, u32[]{:S(2)}, u32[]{:S(2)}) collective-permute-start(f32[118,16,128]{2,1,0:T(8,128)S(1)} %get-tuple-element.30), channel_id=1, source_target_pairs={{0,8},{8,16},{16,24},{1,9},{9,17},{17,25},{2,10},{10,18},{18,26},{... | collective-permute-start | bytes 2899976 | tf_op jit(solution)/shard_map/ppermute | solution.py:544
  26.9 20.6 %collective-permute-start.4 = (f32[118,16,128]{2,1,0:T(8,128)S(1)}, f32[118,16,128]{2,1,0:T(8,128)S(1)}, u32[]{:S(2)}, u32[]{:S(2)}) collective-permute-start(f32[118,16,128]{2,1,0:T(8,128)S(1)} %get-tuple-element.31), channel_id=1, source_target_pairs={{8,0},{16,8},{24,16},{9,1},{17,9},{25,17},{10,2},{18,10},{26,18},{... | collective-permute-start | bytes 2899976 | tf_op jit(solution)/shard_map/ppermute | solution.py:544
  39.8 14.4 %collective-permute-start.5 = (f32[944,128]{1,0:T(8,128)S(1)}, f32[944,128]{1,0:T(8,128)S(1)}, u32[]{:S(2)}, u32[]{:S(2)}) collective-permute-start(f32[944,128]{1,0:T(8,128)S(1)} %get-tuple-element.40), channel_id=1, source_target_pairs={{0,8},{8,16},{16,24},{1,9},{9,17},{17,25},{2,10},{10,18},{18,26},{... | collective-permute-start | bytes 1449992 | tf_op jit(solution)/shard_map/ppermute | solution.py:544
  45.5 10.1 %collective-permute-start.6 = (f32[944,128]{1,0:T(8,128)S(1)}, f32[944,128]{1,0:T(8,128)S(1)}, u32[]{:S(2)}, u32[]{:S(2)}) collective-permute-start(f32[944,128]{1,0:T(8,128)S(1)} %get-tuple-element.41), channel_id=1, source_target_pairs={{8,0},{16,8},{24,16},{9,1},{17,9},{25,17},{10,2},{18,10},{26,18},{... | collective-permute-start | bytes 1449992 | tf_op jit(solution)/shard_map/ppermute | solution.py:544
